TPU v7x, 32 devices: a whole 2x2x4 slice. The times are simulated.
32 devices in a mesh: seq: 8 (over z, y), dp: 4 (over x, core).
Axes of the slice: x: 2, y: 2, z: 4, core: 2. Of those that a mesh axis runs over, the one named last changes fastest.
Arguments:
- queries: bfloat16 [4, 2048, 4096], P('dp', None, 'seq'), may hold values from -6 to 6
- keys: bfloat16 [4, 2048, 4096], P('dp', None, 'seq'), may hold values from -6 to 6
- values: bfloat16 [4, 2048, 4096], P('dp', None, 'seq'), may hold values from -6 to 6
- random_blocks: int32 [4, 32, 64, 3], P('dp', 'seq'), may hold values from 0 to 63
- global_blocks: int32 [4, 2], P('dp'), may hold values from 0 to 63, as said below
- out_weight: bfloat16 [2048, 2048], P('dp'), may hold values from -0.125 to 0.125
Outputs:
- projected: bfloat16 [4, 4096, 2048], P('dp', 'seq')
Inputs may be any that keep to these rules, and one draw needn't show every extreme that they name: `global_blocks`: the two global blocks of a sequence differ; some sequence has block 0 and some has block 63.
All inputs are finite; a program needn't handle non-finite values.
Results may differ from a plain program's by a relative error of at most 0.01.
Values may be sent and summed in bfloat16 or wider, within the bound.
No kernel may reach another device: no remote copies, remote signals or barrier semaphores. Data moves between devices by JAX's collectives and lax.ppermute only.
A program may use at most 128 MiB of HBM per device.

v0:
```python
import math

import jax
import jax.numpy as jnp
from jax import lax
from jax.sharding import PartitionSpec as P

HD = 64
BLK = 64


def candidate_blocks(nblocks, glob, rand_h):
    rows = jnp.arange(nblocks, dtype=jnp.int32)
    window = jnp.stack([rows - 1, rows, rows + 1], axis=1)
    globs = jnp.broadcast_to(glob[None, :], (nblocks, glob.shape[0]))
    cand = jnp.concatenate([window, globs, rand_h], axis=1)
    inside = (cand >= 0) & (cand < nblocks)
    width = cand.shape[1]
    equal = cand[:, :, None] == cand[:, None, :]
    earlier = jnp.arange(width)[None, :] < jnp.arange(width)[:, None]
    repeated = jnp.any(equal & earlier[None, :, :], axis=2)
    return (jnp.clip(cand, 0, nblocks - 1), inside & ~repeated)


def head_attention(q_head, k_head, v_head, rand_h, glob):
    length = q_head.shape[1]
    nblocks = length // BLK
    scale = HD ** (-0.5)
    qb = q_head.reshape(HD, nblocks, BLK)
    kb = k_head.reshape(HD, nblocks, BLK)
    vb = v_head.reshape(HD, nblocks, BLK)
    index, valid = candidate_blocks(nblocks, glob, rand_h)
    group = math.gcd(nblocks, 32)
    turns = nblocks // group

    def one_group(turn):
        first = turn * group
        rows_index = lax.dynamic_slice_in_dim(index, first, group, 0)
        rows_valid = lax.dynamic_slice_in_dim(valid, first, group, 0)
        q_rows = lax.dynamic_slice_in_dim(qb, first, group, 1)
        k_rows = jnp.take(kb, rows_index, axis=1)
        v_rows = jnp.take(vb, rows_index, axis=1)
        scores = (
            jnp.einsum("dnq,dnck->nqck", q_rows, k_rows, preferred_element_type=jnp.float32) * scale
        )
        scores = jnp.where(rows_valid[:, None, :, None], scores, -jnp.inf)
        top = jnp.max(scores, axis=(2, 3), keepdims=True)
        expo = jnp.exp(scores - top)
        probs = (expo / jnp.sum(expo, axis=(2, 3), keepdims=True)).astype(jnp.bfloat16)
        return jnp.einsum(
            "nqck,dnck->dnq", probs, v_rows, preferred_element_type=jnp.float32
        ).astype(jnp.bfloat16)

    parts = lax.map(one_group, jnp.arange(turns, dtype=jnp.int32))
    blocks = jnp.transpose(parts, (1, 0, 2, 3)).reshape(HD, nblocks, BLK)
    qglob = jnp.take(qb, glob, axis=1)
    gscore = jnp.einsum("dgq,dk->gqk", qglob, k_head, preferred_element_type=jnp.float32) * scale
    gtop = jnp.max(gscore, axis=2, keepdims=True)
    gexp = jnp.exp(gscore - gtop)
    gprob = (gexp / jnp.sum(gexp, axis=2, keepdims=True)).astype(jnp.bfloat16)
    full = jnp.einsum("gqk,dk->dgq", gprob, v_head, preferred_element_type=jnp.float32).astype(
        jnp.bfloat16
    )
    blocks = blocks.at[:, glob, :].set(full)
    return blocks.reshape(HD, length)


def local(queries, keys, values, random_blocks, global_blocks, out_weight):
    q_heads, k_heads, v_heads = (
        lax.all_to_all(queries[0], "seq", split_axis=0, concat_axis=1, tiled=True),
        lax.all_to_all(keys[0], "seq", split_axis=0, concat_axis=1, tiled=True),
        lax.all_to_all(values[0], "seq", split_axis=0, concat_axis=1, tiled=True),
    )
    count = q_heads.shape[0] // HD
    length = q_heads.shape[1]
    glob = global_blocks[0]

    def one_head(packed):
        q_head, k_head, v_head, rand_h = packed
        return head_attention(q_head, k_head, v_head, rand_h, glob)

    outputs = lax.map(
        one_head,
        (
            q_heads.reshape(count, HD, length),
            k_heads.reshape(count, HD, length),
            v_heads.reshape(count, HD, length),
            random_blocks[0],
        ),
    )
    attended = lax.all_to_all(
        outputs.reshape(count * HD, length), "seq", split_axis=1, concat_axis=0, tiled=True
    )
    result = lax.dot_general(
        attended,
        lax.all_gather(out_weight, "dp", axis=0, tiled=True),
        (((0,), (0,)), ((), ())),
        preferred_element_type=jnp.float32,
    )
    return result.astype(jnp.bfloat16)[None]


def solution(mesh):
    in_specs = (
        P("dp", None, "seq"),
        P("dp", None, "seq"),
        P("dp", None, "seq"),
        P("dp", "seq", None, None),
        P("dp", None),
        P("dp", None),
    )
    out_specs = P("dp", "seq", None)
    return jax.shard_map(local, mesh=mesh, in_specs=in_specs, out_specs=out_specs, check_vma=False)
```

profile of v0, /device:TPU:8, one launch (start us, length us, event | category | flops | bytes accessed | tf_op | source)
XLA Modules:
  0.0 575.2 jit_solution(15196046790141294175)
XLA Ops:
  6.5 53.8 %all_to_all.67 = bf16[8,256,512]{2,1,0:T(8,128)(2,1)} all-to-all(bf16[8,256,512]{2,1,0:T(8,128)(2,1)} %bitcast.155), channel_id=1, replica_groups=mesh['seq'=8,'dp'=4] {'seq'}, dimensions={0} | all-to-all | bytes 4194304 | tf_op jit(solution)/shard_map/all_to_all | solution.py:70
  60.4 51.4 %all_to_all.68 = bf16[8,256,512]{2,1,0:T(8,128)(2,1)} all-to-all(bf16[8,256,512]{2,1,0:T(8,128)(2,1)S(1)} %bitcast.156), channel_id=1, replica_groups=mesh['seq'=8,'dp'=4] {'seq'}, dimensions={0} | all-to-all | bytes 4194304 | tf_op jit(solution)/shard_map/all_to_all | solution.py:71
  134.8 26.6 %all-to-all-done.2 = bf16[8,256,512]{2,1,0:T(8,128)(2,1)S(1)} async-done(((bf16[8,256,512]{2,1,0:T(8,128)(2,1)}), bf16[8,256,512]{2,1,0:T(8,128)(2,1)S(1)}, u32[]{:S(2)}, u32[]{:S(2)}) %all-to-all-start.2) | async-done | bytes 2097184 | tf_op jit(solution)/shard_map/all_to_all | solution.py:72
  168.2 334.3 %while.32 = (s32[]{:T(128)}, bf16[4,64,4096]{2,1,0:T(8,128)(2,1)}, s32[1,2]{1,0:T(1,128)S(1)}, s32[4,64,3]{1,2,0:T(4,128)}, bf16[4,64,4096]{2,1,0:T(8,128)(2,1)}...) while((s32[]{:T(128)}, bf16[4,64,4096]{2,1,0:T(8,128)(2,1)}, ...), condition=%wide.region_9.11_spmd, body=%wide.region_0.10_spmd.sunk | while | flops 420121536 | bytes 86193384 | solution.py:82
  180.8 63.6 %while.33 = (s32[]{:T(128)}, bf16[2,64,32,64]{3,1,2,0:T(8,128)(2,1)}, s32[2]{0:T(128)S(1)}, s32[64,8]{0,1:T(8,128)S(1)}, bf16[64,64,64]{2,0,1:T(8,128)(2,1)S(1)}...) while((s32[]{:T(128)}, ...), condition=%wide.region_5.6_spmd, body=%wide.region_2.5_spmd.sunk | while | flops 283245824 | bytes 61938648 | solution.py:54
  185.3 6.4 %copy.104 = bf16[32,8,64,64]{2,3,1,0:T(8,128)(2,1)} copy(bf16[32,8,64,64]{3,2,1,0:T(8,128)(2,1)} %bitcast.147) | data formatting | bytes 4194304 | tf_op jit(solution)/shard_map/while/body/eval_jaxpr/while/body/eval_jaxpr/jit(_take)/gather | solution.py:41
  205.0 7.5 %fusion.77 = bf16[2,64,32,64]{3,1,2,0:T(8,128)(2,1)} fusion(bf16[2,64,32,64]{3,1,2,0:T(8,128)(2,1)} %get-tuple-element.376, s32[]{:T(128)} %get-tuple-element.375, f32[32,64,512]{1,2,0} %copy-done, f32[32,64]{1,0:T(8,128)S(1)} %fusion.76, f32[32,64]{1,0:T(8,128)S(1)} %get-tuple-element.362, pred[32,8]{1,0:T(8,128)(4,1)S(1)} %copy.102, ...), kind=kOutput, calls=%fused_computation.19.clone.1 | convolution fusion | flops 140640256 | bytes 13124608 | tf_op jit(solution)/shard_map/while/body/eval_jaxpr/while/body/eval_jaxpr/nqck,dnck->dnq/dot_general | solution.py:50
  217.1 6.4 %copy.104 = bf16[32,8,64,64]{2,3,1,0:T(8,128)(2,1)} copy(bf16[32,8,64,64]{3,2,1,0:T(8,128)(2,1)} %bitcast.147) | data formatting | bytes 4194304 | tf_op jit(solution)/shard_map/while/body/eval_jaxpr/while/body/eval_jaxpr/jit(_take)/gather | solution.py:41
  236.8 7.5 %fusion.77 = bf16[2,64,32,64]{3,1,2,0:T(8,128)(2,1)} fusion(bf16[2,64,32,64]{3,1,2,0:T(8,128)(2,1)} %get-tuple-element.376, s32[]{:T(128)} %get-tuple-element.375, f32[32,64,512]{1,2,0} %copy-done, f32[32,64]{1,0:T(8,128)S(1)} %fusion.76, f32[32,64]{1,0:T(8,128)S(1)} %get-tuple-element.362, pred[32,8]{1,0:T(8,128)(4,1)S(1)} %copy.102, ...), kind=kOutput, calls=%fused_computation.19.clone.1 | convolution fusion | flops 140640256 | bytes 13124608 | tf_op jit(solution)/shard_map/while/body/eval_jaxpr/while/body/eval_jaxpr/nqck,dnck->dnq/dot_general | solution.py:50
  264.3 63.6 %while.33 = (s32[]{:T(128)}, bf16[2,64,32,64]{3,1,2,0:T(8,128)(2,1)}, s32[2]{0:T(128)S(1)}, s32[64,8]{0,1:T(8,128)S(1)}, bf16[64,64,64]{2,0,1:T(8,128)(2,1)S(1)}...) while((s32[]{:T(128)}, ...), condition=%wide.region_5.6_spmd, body=%wide.region_2.5_spmd.sunk | while | flops 283245824 | bytes 61938648 | solution.py:54
  268.8 6.4 %copy.104 = bf16[32,8,64,64]{2,3,1,0:T(8,128)(2,1)} copy(bf16[32,8,64,64]{3,2,1,0:T(8,128)(2,1)} %bitcast.147) | data formatting | bytes 4194304 | tf_op jit(solution)/shard_map/while/body/eval_jaxpr/while/body/eval_jaxpr/jit(_take)/gather | solution.py:41
  288.6 7.5 %fusion.77 = bf16[2,64,32,64]{3,1,2,0:T(8,128)(2,1)} fusion(bf16[2,64,32,64]{3,1,2,0:T(8,128)(2,1)} %get-tuple-element.376, s32[]{:T(128)} %get-tuple-element.375, f32[32,64,512]{1,2,0} %copy-done, f32[32,64]{1,0:T(8,128)S(1)} %fusion.76, f32[32,64]{1,0:T(8,128)S(1)} %get-tuple-element.362, pred[32,8]{1,0:T(8,128)(4,1)S(1)} %copy.102, ...), kind=kOutput, calls=%fused_computation.19.clone.1 | convolution fusion | flops 140640256 | bytes 13124608 | tf_op jit(solution)/shard_map/while/body/eval_jaxpr/while/body/eval_jaxpr/nqck,dnck->dnq/dot_general | solution.py:50
  300.6 6.4 %copy.104 = bf16[32,8,64,64]{2,3,1,0:T(8,128)(2,1)} copy(bf16[32,8,64,64]{3,2,1,0:T(8,128)(2,1)} %bitcast.147) | data formatting | bytes 4194304 | tf_op jit(solution)/shard_map/while/body/eval_jaxpr/while/body/eval_jaxpr/jit(_take)/gather | solution.py:41
  320.4 7.5 %fusion.77 = bf16[2,64,32,64]{3,1,2,0:T(8,128)(2,1)} fusion(bf16[2,64,32,64]{3,1,2,0:T(8,128)(2,1)} %get-tuple-element.376, s32[]{:T(128)} %get-tuple-element.375, f32[32,64,512]{1,2,0} %copy-done, f32[32,64]{1,0:T(8,128)S(1)} %fusion.76, f32[32,64]{1,0:T(8,128)S(1)} %get-tuple-element.362, pred[32,8]{1,0:T(8,128)(4,1)S(1)} %copy.102, ...), kind=kOutput, calls=%fused_computation.19.clone.1 | convolution fusion | flops 140640256 | bytes 13124608 | tf_op jit(solution)/shard_map/while/body/eval_jaxpr/while/body/eval_jaxpr/nqck,dnck->dnq/dot_general | solution.py:50
  347.9 63.6 %while.33 = (s32[]{:T(128)}, bf16[2,64,32,64]{3,1,2,0:T(8,128)(2,1)}, s32[2]{0:T(128)S(1)}, s32[64,8]{0,1:T(8,128)S(1)}, bf16[64,64,64]{2,0,1:T(8,128)(2,1)S(1)}...) while((s32[]{:T(128)}, ...), condition=%wide.region_5.6_spmd, body=%wide.region_2.5_spmd.sunk | while | flops 283245824 | bytes 61938648 | solution.py:54
  372.2 7.5 %fusion.77 = bf16[2,64,32,64]{3,1,2,0:T(8,128)(2,1)} fusion(bf16[2,64,32,64]{3,1,2,0:T(8,128)(2,1)} %get-tuple-element.376, s32[]{:T(128)} %get-tuple-element.375, f32[32,64,512]{1,2,0} %copy-done, f32[32,64]{1,0:T(8,128)S(1)} %fusion.76, f32[32,64]{1,0:T(8,128)S(1)} %get-tuple-element.362, pred[32,8]{1,0:T(8,128)(4,1)S(1)} %copy.102, ...), kind=kOutput, calls=%fused_computation.19.clone.1 | convolution fusion | flops 140640256 | bytes 13124608 | tf_op jit(solution)/shard_map/while/body/eval_jaxpr/while/body/eval_jaxpr/nqck,dnck->dnq/dot_general | solution.py:50
  384.2 6.4 %copy.104 = bf16[32,8,64,64]{2,3,1,0:T(8,128)(2,1)} copy(bf16[32,8,64,64]{3,2,1,0:T(8,128)(2,1)} %bitcast.147) | data formatting | bytes 4194304 | tf_op jit(solution)/shard_map/while/body/eval_jaxpr/while/body/eval_jaxpr/jit(_take)/gather | solution.py:41
  404.0 7.5 %fusion.77 = bf16[2,64,32,64]{3,1,2,0:T(8,128)(2,1)} fusion(bf16[2,64,32,64]{3,1,2,0:T(8,128)(2,1)} %get-tuple-element.376, s32[]{:T(128)} %get-tuple-element.375, f32[32,64,512]{1,2,0} %copy-done, f32[32,64]{1,0:T(8,128)S(1)} %fusion.76, f32[32,64]{1,0:T(8,128)S(1)} %get-tuple-element.362, pred[32,8]{1,0:T(8,128)(4,1)S(1)} %copy.102, ...), kind=kOutput, calls=%fused_computation.19.clone.1 | convolution fusion | flops 140640256 | bytes 13124608 | tf_op jit(solution)/shard_map/while/body/eval_jaxpr/while/body/eval_jaxpr/nqck,dnck->dnq/dot_general | solution.py:50
  431.5 63.6 %while.33 = (s32[]{:T(128)}, bf16[2,64,32,64]{3,1,2,0:T(8,128)(2,1)}, s32[2]{0:T(128)S(1)}, s32[64,8]{0,1:T(8,128)S(1)}, bf16[64,64,64]{2,0,1:T(8,128)(2,1)S(1)}...) while((s32[]{:T(128)}, ...), condition=%wide.region_5.6_spmd, body=%wide.region_2.5_spmd.sunk | while | flops 283245824 | bytes 61938648 | solution.py:54
  436.0 6.4 %copy.104 = bf16[32,8,64,64]{2,3,1,0:T(8,128)(2,1)} copy(bf16[32,8,64,64]{3,2,1,0:T(8,128)(2,1)} %bitcast.147) | data formatting | bytes 4194304 | tf_op jit(solution)/shard_map/while/body/eval_jaxpr/while/body/eval_jaxpr/jit(_take)/gather | solution.py:41
  455.8 7.5 %fusion.77 = bf16[2,64,32,64]{3,1,2,0:T(8,128)(2,1)} fusion(bf16[2,64,32,64]{3,1,2,0:T(8,128)(2,1)} %get-tuple-element.376, s32[]{:T(128)} %get-tuple-element.375, f32[32,64,512]{1,2,0} %copy-done, f32[32,64]{1,0:T(8,128)S(1)} %fusion.76, f32[32,64]{1,0:T(8,128)S(1)} %get-tuple-element.362, pred[32,8]{1,0:T(8,128)(4,1)S(1)} %copy.102, ...), kind=kOutput, calls=%fused_computation.19.clone.1 | convolution fusion | flops 140640256 | bytes 13124608 | tf_op jit(solution)/shard_map/while/body/eval_jaxpr/while/body/eval_jaxpr/nqck,dnck->dnq/dot_general | solution.py:50
  487.5 7.5 %fusion.77 = bf16[2,64,32,64]{3,1,2,0:T(8,128)(2,1)} fusion(bf16[2,64,32,64]{3,1,2,0:T(8,128)(2,1)} %get-tuple-element.376, s32[]{:T(128)} %get-tuple-element.375, f32[32,64,512]{1,2,0} %copy-done, f32[32,64]{1,0:T(8,128)S(1)} %fusion.76, f32[32,64]{1,0:T(8,128)S(1)} %get-tuple-element.362, pred[32,8]{1,0:T(8,128)(4,1)S(1)} %copy.102, ...), kind=kOutput, calls=%fused_computation.19.clone.1 | convolution fusion | flops 140640256 | bytes 13124608 | tf_op jit(solution)/shard_map/while/body/eval_jaxpr/while/body/eval_jaxpr/nqck,dnck->dnq/dot_general | solution.py:50
  505.7 53.6 %all_to_all.69 = bf16[256,8,512]{2,0,1:T(8,128)(2,1)S(1)} all-to-all(bf16[256,8,512]{2,0,1:T(8,128)(2,1)S(1)} %copy.82), channel_id=1, replica_groups=mesh['seq'=8,'dp'=4] {'seq'}, dimensions={1} | all-to-all | bytes 4194304 | tf_op jit(solution)/shard_map/all_to_all | solution.py:91
  559.3 9.1 %fusion.47 = bf16[1,512,2048]{2,1,0:T(8,128)(2,1)} fusion(bf16[2048,512]{1,0:T(8,128)(2,1)S(1)} %bitcast.159, bf16[2048,2048]{1,0:T(8,128)(2,1)} %all-gather.2.cloned.1.call-done), kind=kOutput, calls=%fused_computation.64 | convolution fusion | flops 4296015872 | bytes 12582912 | tf_op jit(solution)/shard_map/dot_general | solution.py:94
  (290 shorter events, 263.2 us)
Async XLA Ops:
  6.5 53.8 %copy-start.4 = (bf16[1,2048,512]{2,1,0:T(8,128)(2,1)S(1)}, bf16[1,2048,512]{2,1,0:T(8,128)(2,1)}, u32[]{:S(2)}) copy-start(bf16[1,2048,512]{2,1,0:T(8,128)(2,1)} %param.13) | copy-start | bytes 6291460
  111.7 5.4 copy-start.5
  111.8 49.7 %all-to-all-start.2 = ((bf16[8,256,512]{2,1,0:T(8,128)(2,1)}), bf16[8,256,512]{2,1,0:T(8,128)(2,1)S(1)}, u32[]{:S(2)}, u32[]{:S(2)}) async-start(bf16[8,256,512]{2,1,0:T(8,128)(2,1)} %bitcast.157), calls=%async_computation.2 | async-start | bytes 4194304 | tf_op jit(solution)/shard_map/all_to_all | solution.py:72
  116.4 442.9 %all-gather.2.cloned.1.call-start = ((), (), s32[]{:S(2)}) async-start(), calls=%async_computation.4 | async-start | bytes 10485760 | tf_op jit(solution)/shard_map/all_gather | solution.py:96
  161.4 6.8 %copy-start.6 = (s32[1,2]{1,0:T(1,128)S(1)}, s32[1,2]{1,0:T(1,128)}, u32[]{:S(2)}) copy-start(s32[1,2]{1,0:T(1,128)} %param.16) | copy-start | bytes 28
  170.4 0.8 copy-start.1
  175.9 0.8 copy-start.2
  198.8 3.2 copy-start
  230.6 3.2 copy-start
  247.0 1.8 copy-start.3
  254.0 0.8 copy-start.1
  259.5 0.8 copy-start.2
  282.4 3.2 copy-start
  314.2 3.2 copy-start
  330.6 1.8 copy-start.3
  337.5 0.8 copy-start.1
  343.0 0.8 copy-start.2
  366.0 3.2 copy-start
  397.7 3.2 copy-start
  414.1 1.8 copy-start.3
  426.6 0.8 copy-start.2
  449.5 3.2 copy-start
  481.3 3.2 copy-start
  497.7 1.8 copy-start.3
  (1 other events, 0.8 us)
Sparse Core Ops, SparseCore 0:
  118.8 59.1 all-gather.1
where the time goes:
time: 580 us; the launch traced here: 575 us
  local copies, waits for them, and re-layouts  207 us (36%)
  blocking collectives  159 us (27%)
  matrix products  110 us (19%)
  other arithmetic  48.7 us (8%)
  waiting for transfers between devices  27.4 us (5%)
  between operations  13.4 us (2%)
    gather x16, local copies, waits for them, and re-layouts, one_group(): k_rows = jnp.take(kb, rows_index, axis=1)  75.5 us
    dot_general x8, matrix products, one_group(): jnp.einsum('nqck,dnck->dnq', probs, v_rows, preferred_element_type=jnp.fl...  60.2 us
    all_to_all x1, blocking collectives, local(): lax.all_to_all(queries[0], 'seq', split_axis=0, concat_axis=1, tiled=True)  53.8 us
    all_to_all x1, blocking collectives, local(): lax.all_to_all(outputs.reshape(count * HD, length), 'seq', split_axis=1,...  53.6 us
    all_to_all x1, blocking collectives, local(): lax.all_to_all(keys[0], 'seq', split_axis=0, concat_axis=1, tiled=True)  51.4 us
    select_n x8, other arithmetic, one_group(): k_rows = jnp.take(kb, rows_index, axis=1)  30.6 us
    all_to_all x1, waiting for transfers between devices, local(): lax.all_to_all(values[0], 'seq', split_axis=0, concat_axis=1, tiled=True)  26.6 us
    while x8, matrix products  25 us
  transfers between devices with their start and end apart: 2, of which 1 were waited for; matrix products, arithmetic and copies ran while one was open for 59% of the time, Pallas kernels for 0%

commit v1 on v0

--- a/solution.py
+++ b/solution.py
@@ -1,12 +1,18 @@
+import functools
 import math
 
 import jax
 import jax.numpy as jnp
 from jax import lax
+from jax.experimental import pallas as pl
+from jax.experimental.pallas import tpu as pltpu
 from jax.sharding import PartitionSpec as P
 
 HD = 64
 BLK = 64
+PAIR = 2 * HD
+EXP_SCALE = HD ** (-0.5) * math.log2(math.e)
+BIG = 1e30
 
 
 def candidate_blocks(nblocks, glob, rand_h):
@@ -65,7 +71,7 @@
     return blocks.reshape(HD, length)
 
 
-def local(queries, keys, values, random_blocks, global_blocks, out_weight):
+def local_plain(queries, keys, values, random_blocks, global_blocks, out_weight):
     q_heads, k_heads, v_heads = (
         lax.all_to_all(queries[0], "seq", split_axis=0, concat_axis=1, tiled=True),
         lax.all_to_all(keys[0], "seq", split_axis=0, concat_axis=1, tiled=True),
@@ -100,7 +106,302 @@
     return result.astype(jnp.bfloat16)[None]
 
 
+def cut_kernel(n, feats, row, me_ref, q_ref, k_ref, v_ref, *rest):
+    outs = rest[: n - 1]
+    held, in_sems, out_sems = rest[n - 1 :]
+    me = me_ref[0]
+    order = range(n - 1, 0, -1)
+
+    def read(k, i):
+        start = pl.multiple_of(lax.rem(me + k, n) * feats + row, PAIR)
+        src = (q_ref, k_ref, v_ref)[i]
+        return pltpu.make_async_copy(
+            src.at[0, pl.ds(start, PAIR), :], held.at[k - 1, i], in_sems.at[k - 1, i]
+        )
+
+    def write(k):
+        return pltpu.make_async_copy(held.at[k - 1], outs[k - 1], out_sems.at[k - 1])
+
+    for k in order:
+        for i in range(3):
+            read(k, i).start()
+    for k in order:
+        for i in range(3):
+            read(k, i).wait()
+        write(k).start()
+    for k in order:
+        write(k).wait()
+
+
+def cut(n, row, me, queries, keys, values):
+    feats = queries.shape[1] // n
+    length = queries.shape[2]
+    hbm = pl.BlockSpec(memory_space=pl.ANY)
+    return pl.pallas_call(
+        functools.partial(cut_kernel, n, feats, row),
+        out_shape=[jax.ShapeDtypeStruct((3, PAIR, length), queries.dtype)] * (n - 1),
+        in_specs=[pl.BlockSpec(memory_space=pltpu.SMEM), hbm, hbm, hbm],
+        out_specs=[hbm] * (n - 1),
+        scratch_shapes=[
+            pltpu.VMEM((n - 1, 3, PAIR, length), queries.dtype),
+            pltpu.SemaphoreType.DMA((n - 1, 3)),
+            pltpu.SemaphoreType.DMA((n - 1,)),
+        ],
+        name="cut",
+    )(me, queries, keys, values)
+
+
+def swap_halves(x):
+    return jnp.concatenate([x[:, BLK:], x[:, :BLK]], axis=1)
+
+
+def attend_kernel(
+    n, nblocks, feats, row, me_ref, rand_ref, glob_ref, pen_ref, q_ref, k_ref, v_ref, *rest
+):
+    parts, outs = rest[: n - 1], rest[n - 1 : 2 * n - 1]
+    raw, kt, vv, ob, sg, in_sems, own_sems, out_sems = rest[2 * n - 1 :]
+    me = me_ref[0]
+    shard = raw.shape[3]
+    per = shard // BLK
+    tiles = shard // PAIR
+    f32, bf16 = jnp.float32, jnp.bfloat16
+
+    own = pl.multiple_of(me * feats + row, PAIR)
+    arrivals = []
+    for i, src in enumerate((q_ref, k_ref, v_ref)):
+        copy = pltpu.make_async_copy(
+            src.at[0, pl.ds(own, PAIR), :], raw.at[me, i], own_sems.at[i]
+        )
+        copy.start()
+        arrivals.append(copy)
+    for k in range(1, n):
+        came = lax.rem(me - k + n, n)
+        copy = pltpu.make_async_copy(parts[k - 1], raw.at[came], in_sems.at[k - 1])
+        copy.start()
+        arrivals.append(copy)
+    for copy in arrivals:
+        copy.wait()
+
+    def prepare(s, carry):
+        for t in range(tiles):
+            lanes = slice(t * PAIR, (t + 1) * PAIR)
+            first = pl.multiple_of(s * shard + t * PAIR, PAIR)
+            kt[pl.ds(first, PAIR), :] = raw[s, 1, :, lanes].T
+            v = raw[s, 2, :, lanes]
+            vv[0, s * tiles + t] = v
+            vv[1, s * tiles + t] = swap_halves(v)
+        return carry
+
+    lax.fori_loop(0, n, prepare, 0)
+
+    low = lax.broadcasted_iota(jnp.int32, (BLK, PAIR), 1) < BLK
+    zero = jnp.zeros((HD, PAIR), bf16)
+
+    def queries_of(x, odd):
+        y = swap_halves(x)
+        a, b = (y, x) if odd else (x, y)
+        return jnp.concatenate(
+            [jnp.where(low, a[:HD], zero), jnp.where(low, zero, b[HD:])], axis=0
+        )
+
+    def key_rows(b):
+        return kt[pl.ds(pl.multiple_of(b * BLK, BLK), BLK), :]
+
+    def value_half(head, b, place):
+        side = lax.rem(b + place, 2)
+        return vv[side, lax.div(b, 2), head * HD : (head + 1) * HD, :]
+
+    def finish(ot, total):
+        t = (ot / total).astype(bf16).T
+        return jnp.where(low, t[:BLK], t[BLK:])
+
+    def sparse(j, qbd):
+        shared = [jnp.maximum(j - 1, 0), j, jnp.minimum(j + 1, nblocks - 1), glob_ref[0], glob_ref[1]]
+        cand = [
+            shared + [rand_ref[(h * nblocks + j) * 3 + c] for c in range(3)] for h in range(2)
+        ]
+        k_rows = [key_rows(b) for b in shared]
+        for c in range(5, 8):
+            k_rows.append(jnp.where(low, key_rows(cand[0][c]), key_rows(cand[1][c])))
+        scores = jnp.dot(jnp.concatenate(k_rows, axis=0), qbd, preferred_element_type=f32)
+        top = jnp.max(scores, axis=0, keepdims=True) * EXP_SCALE
+        shift = pen_ref[j] + top
+        probs = [
+            jnp.exp2(scores[c * BLK : (c + 1) * BLK] * EXP_SCALE - shift[c : c + 1])
+            for c in range(8)
+        ]
+        total = functools.reduce(
+            jnp.add, [jnp.sum(p, axis=0, keepdims=True) for p in probs]
+        )
+        pt = jnp.concatenate([p.astype(bf16) for p in probs], axis=0)
+        vcat = []
+        for c in range(0, 8, 2):
+            vcat.append(
+                jnp.concatenate(
+                    [
+                        jnp.where(
+                            low, value_half(h, cand[h][c], 0), value_half(h, cand[h][c + 1], 1)
+                        )
+                        for h in range(2)
+                    ],
+                    axis=0,
+                )
+            )
+        ot = jnp.dot(jnp.concatenate(vcat, axis=1), pt, preferred_element_type=f32)
+        return finish(ot, total)
+
+    def tile_of(i):
+        s = lax.div(i, tiles)
+        first = pl.multiple_of(lax.rem(i, tiles) * PAIR, PAIR)
+        return s, first
+
+    def two_blocks(i, carry):
+        s, first = tile_of(i)
+        x = raw[s, 0, :, pl.ds(first, PAIR)]
+        a = sparse(2 * i, queries_of(x, False))
+        b = sparse(2 * i + 1, queries_of(x, True))
+        ob[s, pl.ds(first, PAIR), :] = jnp.concatenate([a, b], axis=0)
+        return carry
+
+    lax.fori_loop(0, nblocks // 2, two_blocks, 0)
+
+    for g in range(2):
+        block = glob_ref[g]
+        s, first = tile_of(lax.div(block, 2))
+        x = raw[s, 0, :, pl.ds(first, PAIR)]
+        odd = lax.rem(block, 2)
+        qbd = jnp.where(odd == 1, queries_of(x, True), queries_of(x, False))
+
+        def scan_scores(t, top):
+            rows = pl.ds(pl.multiple_of(t * shard, shard), shard)
+            scores = jnp.dot(kt[rows, :], qbd, preferred_element_type=f32)
+            sg[rows, :] = scores
+            return jnp.maximum(top, jnp.max(scores, axis=0, keepdims=True))
+
+        top = lax.fori_loop(0, n, scan_scores, jnp.full((1, PAIR), -jnp.inf, f32))
+        top = top * EXP_SCALE
+
+        def scan_values(t, carry):
+            total, ot = carry
+            rows = pl.ds(pl.multiple_of(t * shard, shard), shard)
+            p = jnp.exp2(sg[rows, :] * EXP_SCALE - top)
+            total = total + jnp.sum(p, axis=0, keepdims=True)
+            ot = ot + jnp.dot(raw[t, 2], p.astype(bf16), preferred_element_type=f32)
+            return total, ot
+
+        total, ot = lax.fori_loop(
+            0, n, scan_values, (jnp.zeros((1, PAIR), f32), jnp.zeros((PAIR, PAIR), f32))
+        )
+        place = pl.multiple_of(lax.rem(block, per) * BLK, BLK)
+        ob[s, pl.ds(place, BLK), :] = finish(ot, total)
+
+    leaving = []
+    for k in range(n):
+        to = lax.rem(me + k, n)
+        copy = pltpu.make_async_copy(ob.at[to], outs[k], out_sems.at[k])
+        copy.start()
+        leaving.append(copy)
+    for copy in leaving:
+        copy.wait()
+
+
+def attend(n, row, me, rand, glob, pen, queries, keys, values, parts):
+    feats = queries.shape[1] // n
+    shard = queries.shape[2]
+    length = n * shard
+    nblocks = length // BLK
+    hbm = pl.BlockSpec(memory_space=pl.ANY)
+    smem = pl.BlockSpec(memory_space=pltpu.SMEM)
+    vmem = pl.BlockSpec(memory_space=pltpu.VMEM)
+    return pl.pallas_call(
+        functools.partial(attend_kernel, n, nblocks, feats, row),
+        out_shape=[jax.ShapeDtypeStruct((shard, PAIR), jnp.bfloat16)] * n,
+        in_specs=[smem, smem, smem, vmem, hbm, hbm, hbm] + [hbm] * (n - 1),
+        out_specs=[hbm] * n,
+        scratch_shapes=[
+            pltpu.VMEM((n, 3, PAIR, shard), jnp.bfloat16),
+            pltpu.VMEM((length, PAIR), jnp.bfloat16),
+            pltpu.VMEM((2, nblocks // 2, PAIR, PAIR), jnp.bfloat16),
+            pltpu.VMEM((n, shard, PAIR), jnp.bfloat16),
+            pltpu.VMEM((length, PAIR), jnp.float32),
+            pltpu.SemaphoreType.DMA((n - 1,)),
+            pltpu.SemaphoreType.DMA((3,)),
+            pltpu.SemaphoreType.DMA((n,)),
+        ],
+        compiler_params=pltpu.CompilerParams(vmem_limit_bytes=40 * 1024 * 1024),
+        cost_estimate=pl.CostEstimate(
+            flops=20_000_000_000, bytes_accessed=4_000_000, transcendentals=0
+        ),
+        name="attend",
+    )(me, rand, glob, pen, queries, keys, values, *parts)
+
+
+def project_kernel(n, pairs, me_ref, *rest):
+    pieces, w_ref, o_ref, a = rest[: n * pairs], rest[-3], rest[-2], rest[-1]
+    me = me_ref[0]
+
+    @pl.when(pl.program_id(0) == 0)
+    def _():
+        for p in range(pairs):
+            for k in range(n):
+                came = lax.rem(me - k + n, n)
+                first = pl.multiple_of((came * pairs + p) * PAIR, PAIR)
+                a[:, pl.ds(first, PAIR)] = pieces[p * n + k][...]
+
+    o_ref[0] = jnp.dot(a[...], w_ref[...], preferred_element_type=jnp.float32).astype(o_ref.dtype)
+
+
+def project(n, me, pieces, weight):
+    pairs = len(pieces) // n
+    shard = pieces[0].shape[0]
+    depth, width = weight.shape
+    tile = 256
+    piece = pl.BlockSpec((shard, PAIR), lambda i: (0, 0))
+    return pl.pallas_call(
+        functools.partial(project_kernel, n, pairs),
+        grid=(width // tile,),
+        out_shape=jax.ShapeDtypeStruct((1, shard, width), jnp.bfloat16),
+        in_specs=[pl.BlockSpec(memory_space=pltpu.SMEM)]
+        + [piece] * (n * pairs)
+        + [pl.BlockSpec((depth, tile), lambda i: (0, i))],
+        out_specs=pl.BlockSpec((1, shard, tile), lambda i: (0, 0, i)),
+        scratch_shapes=[pltpu.VMEM((shard, depth), jnp.bfloat16)],
+        compiler_params=pltpu.CompilerParams(vmem_limit_bytes=40 * 1024 * 1024),
+        name="project",
+    )(me, *pieces, weight)
+
+
+def local_paired(n, queries, keys, values, random_blocks, global_blocks, out_weight):
+    me = lax.axis_index("seq").astype(jnp.int32)[None]
+    feats = queries.shape[1] // n
+    length = queries.shape[2] * n
+    nblocks = length // BLK
+    pairs = feats // PAIR
+    glob = global_blocks[0]
+    weight = lax.all_gather(out_weight, "dp", axis=0, tiled=True)
+
+    def turn(x, k):
+        return lax.ppermute(x, "seq", [(i, (i + k) % n) for i in range(n)])
+
+    valid = jax.vmap(lambda r: candidate_blocks(nblocks, glob, r)[1])(random_blocks[0])
+    pen = jnp.where(valid, 0.0, BIG).astype(jnp.float32)
+
+    arrived = []
+    for p in range(pairs):
+        sent = cut(n, p * PAIR, me, queries, keys, values)
+        arrived.append([turn(sent[k - 1], k) for k in range(1, n)])
+    pieces = []
+    for p in range(pairs):
+        rand = random_blocks[0, 2 * p : 2 * p + 2].reshape(-1)
+        lanes = jnp.repeat(jnp.transpose(pen[2 * p : 2 * p + 2], (1, 2, 0)), HD, axis=2)
+        outs = attend(n, p * PAIR, me, rand, glob, lanes, queries, keys, values, arrived[p])
+        pieces.append(outs[0])
+        pieces.extend(turn(outs[k], k) for k in range(1, n))
+    return project(n, me, pieces, weight)
+
+
 def solution(mesh):
+    n = mesh.shape["seq"]
     in_specs = (
         P("dp", None, "seq"),
         P("dp", None, "seq"),
@@ -110,4 +411,11 @@
         P("dp", None),
     )
     out_specs = P("dp", "seq", None)
+
+    def local(queries, keys, *rest):
+        feats, shard = queries.shape[1] // n, queries.shape[2]
+        paired = feats % PAIR == 0 and shard % PAIR == 0
+        body = functools.partial(local_paired, n) if paired else local_plain
+        return body(queries, keys, *rest)
+
     return jax.shard_map(local, mesh=mesh, in_specs=in_specs, out_specs=out_specs, check_vma=False)

time: 580 us -> 241 us (0.42)
  local copies, waits for them, and re-layouts: 207 us -> 15.9 us
  blocking collectives: 159 us -> 0 us
  matrix products: 110 us -> 0 us
  Pallas kernels: 0 us -> 80 us
  starting transfers between devices: 4.65 us -> 78.4 us
  other arithmetic: 48.7 us -> 0.29 us
  waiting for transfers between devices: 27.4 us -> 52.3 us
    all_to_all x3 -> x0, blocking collectives: 159 us -> none  [the longest x1 53.8 us: local(): lax.all_to_all(queries[0], 'seq', split_axis=0, concat_axis=1, tiled=True)]
    gather x28 -> x0, local copies, waits for them, and re-layouts: 102 us -> none  [the longest x16 75.5 us: one_group(): k_rows = jnp.take(kb, rows_index, axis=1)]
    pallas_call x0 -> x5, Pallas kernels: none -> 80 us  [the longest x2 65 us: attend(): pl.pallas_call(functools.partial(attend_kernel, n, nblocks, feats, row),...]
    ppermute x0 -> x28, starting transfers between devices: none -> 78.4 us  [turn(): return lax.ppermute(x, 'seq', [(i, (i + k) % n) for i in range(n)])]
    dot_general x13 -> x0, matrix products: 76.6 us -> none  [the longest x8 60.2 us: one_group(): jnp.einsum('nqck,dnck->dnq', probs, v_rows, preferred_element_type=jnp.fl...]
    ppermute x0 -> x28, waiting for transfers between devices: none -> 51.6 us  [turn(): return lax.ppermute(x, 'seq', [(i, (i + k) % n) for i in range(n)])]
    select_n x20 -> x1, other arithmetic: 30.7 us -> 0.08 us  [local_paired(): pen = jnp.where(valid, 0.0, BIG).astype(jnp.float32)]
    reshape x15 -> x2, local copies, waits for them, and re-layouts: 30.5 us -> 2.67 us  [local_paired(): jnp.repeat(jnp.transpose(pen[2 * p:2 * p + 2], (1, 2, 0)), HD, axis=2)]
  transfers between devices with their start and end apart: 2 -> 29, of which waited for: 1 -> 9; matrix products, arithmetic and copies ran while one was open for 59% -> 3% of each run, Pallas kernels for 0% -> 30%
where the time goes in v1:
time: 241 us; the launch traced here: 240 us
  Pallas kernels  80 us (33%)
  starting transfers between devices  78.4 us (33%)
  waiting for transfers between devices  52.3 us (22%)
  local copies, waits for them, and re-layouts  15.9 us (7%)
  between operations  13.6 us (6%)
    ppermute x28, starting transfers between devices, turn(): return lax.ppermute(x, 'seq', [(i, (i + k) % n) for i in range(n)])  78.4 us
    pallas_call x2, Pallas kernels, attend(): pl.pallas_call(functools.partial(attend_kernel, n, nblocks, feats, row),...  65 us
    ppermute x28, waiting for transfers between devices, turn(): return lax.ppermute(x, 'seq', [(i, (i + k) % n) for i in range(n)])  51.6 us
    unnamed x21, local copies, waits for them, and re-layouts  9.34 us
    pallas_call x1, Pallas kernels, project(): pl.pallas_call(functools.partial(project_kernel, n, pairs), grid=(width /...  8.47 us
    pallas_call x2, Pallas kernels, cut(): pl.pallas_call(functools.partial(cut_kernel, n, feats, row), out_shape=[j...  6.51 us
  transfers between devices with their start and end apart: 29, of which 9 were waited for; matrix products, arithmetic and copies ran while one was open for 3% of the time, Pallas kernels for 30%

profile of v1, /device:TPU:8, one launch (start us, length us, event | category | flops | bytes accessed | tf_op | source)
XLA Modules:
  0.0 240.4 jit_solution(12927124097366844276)
XLA Ops:
  7.3 2.9 %cut.3 = (bf16[3,128,512]{2,1,0:T(8,128)(2,1)}, bf16[3,128,512]{2,1,0:T(8,128)(2,1)}, bf16[3,128,512]{2,1,0:T(8,128)(2,1)}, bf16[3,128,512]{2,1,0:T(8,128)(2,1)}...) custom-call(s32[1]{0:T(128)} %bitcast.me_ref, ...), custom_call_target="tpu_custom_call" | custom-call | tf_op jit(solution)/shard_map/cut/pallas_call | solution.py:140
  14.4 2.7 %collective-permute-start.17 = (bf16[3,128,512]{2,1,0:T(8,128)(2,1)}, bf16[3,128,512]{2,1,0:T(8,128)(2,1)}, u32[]{:S(2)}, u32[]{:S(2)}) collective-permute-start(bf16[3,128,512]{2,1,0:T(8,128)(2,1)} %get-tuple-element.53), channel_id=1, source_target_pairs={{0,16},{4,20},{8,24},{12,28},{16,0},{20,4},{24,8},{28,12},{1,17},{... | collective-permute-start | bytes 1179656 | tf_op jit(solution)/shard_map/ppermute | solution.py:384
  18.5 3.7 %cut.2 = (bf16[3,128,512]{2,1,0:T(8,128)(2,1)}, bf16[3,128,512]{2,1,0:T(8,128)(2,1)}, bf16[3,128,512]{2,1,0:T(8,128)(2,1)}, bf16[3,128,512]{2,1,0:T(8,128)(2,1)}...) custom-call(s32[1]{0:T(128)} %bitcast.me_ref, ...), custom_call_target="tpu_custom_call" | custom-call | tf_op jit(solution)/shard_map/cut/pallas_call | solution.py:140
  23.3 2.2 collective-permute-start.19
  26.3 8.4 %collective-permute-start.20 = (bf16[3,128,512]{2,1,0:T(8,128)(2,1)}, bf16[3,128,512]{2,1,0:T(8,128)(2,1)}, u32[]{:S(2)}, u32[]{:S(2)}) collective-permute-start(bf16[3,128,512]{2,1,0:T(8,128)(2,1)} %get-tuple-element.56), channel_id=1, source_target_pairs={{0,28},{4,0},{8,4},{12,8},{16,12},{20,16},{24,20},{28,24},{1,29},{... | collective-permute-start | bytes 1179656 | tf_op jit(solution)/shard_map/ppermute | solution.py:384
  34.7 30.6 %collective-permute-done.16.rest_2_ = bf16[3,128,512]{2,1,0:T(8,128)(2,1)S(1)} collective-permute-done((bf16[3,128,512]{2,1,0:T(8,128)(2,1)}, bf16[3,128,512]{2,1,0:T(8,128)(2,1)S(1)}, u32[]{:S(2)}, u32[]{:S(2)}) %collective-permute-start.16) | collective-permute-done | bytes 393248 | tf_op jit(solution)/shard_map/ppermute | solution.py:384
  65.3 8.3 %collective-permute-start = (bf16[3,128,512]{2,1,0:T(8,128)(2,1)}, bf16[3,128,512]{2,1,0:T(8,128)(2,1)}, u32[]{:S(2)}, u32[]{:S(2)}) collective-permute-start(bf16[3,128,512]{2,1,0:T(8,128)(2,1)} %get-tuple-element.35), channel_id=1, source_target_pairs={{0,4},{4,8},{8,12},{12,16},{16,20},{20,24},{24,28},{28,0},{1,5},{5... | collective-permute-start | bytes 1179656 | tf_op jit(solution)/shard_map/ppermute | solution.py:384
  80.2 2.4 %collective-permute-done.18.rest_4_ = bf16[3,128,512]{2,1,0:T(8,128)(2,1)} collective-permute-done((bf16[3,128,512]{2,1,0:T(8,128)(2,1)}, bf16[3,128,512]{2,1,0:T(8,128)(2,1)}, u32[]{:S(2)}, u32[]{:S(2)}) %collective-permute-start.18) | collective-permute-done | bytes 393248 | tf_op jit(solution)/shard_map/ppermute | solution.py:384
  82.7 9.4 %collective-permute-start.2 = (bf16[3,128,512]{2,1,0:T(8,128)(2,1)}, bf16[3,128,512]{2,1,0:T(8,128)(2,1)S(1)}, u32[]{:S(2)}, u32[]{:S(2)}) collective-permute-start(bf16[3,128,512]{2,1,0:T(8,128)(2,1)} %get-tuple-element.37), channel_id=1, source_target_pairs={{0,12},{4,16},{8,20},{12,24},{16,28},{20,0},{24,4},{28,8},{1,13},{... | collective-permute-start | bytes 1179656 | tf_op jit(solution)/shard_map/ppermute | solution.py:384
  92.5 18.4 %collective-permute-start.4 = (bf16[3,128,512]{2,1,0:T(8,128)(2,1)}, bf16[3,128,512]{2,1,0:T(8,128)(2,1)S(1)}, u32[]{:S(2)}, u32[]{:S(2)}) collective-permute-start(bf16[3,128,512]{2,1,0:T(8,128)(2,1)} %get-tuple-element.39), channel_id=1, source_target_pairs={{0,20},{4,24},{8,28},{12,0},{16,4},{20,8},{24,12},{28,16},{1,21},{... | collective-permute-start | bytes 1179656 | tf_op jit(solution)/shard_map/ppermute | solution.py:384
  117.6 32.9 %attend.3 = (bf16[512,128]{1,0:T(8,128)(2,1)S(1)}, bf16[512,128]{1,0:T(8,128)(2,1)S(1)}, bf16[512,128]{1,0:T(8,128)(2,1)S(1)}, bf16[512,128]{1,0:T(8,128)(2,1)S(...) custom-call(s32[1]{0:T(128)} %bitcast.me_ref, ...), custom_call_target="tpu_custom_call" | custom-call | flops 20000000000 | bytes 4000000 | tf_op jit(solution)/shard_map/attend/pallas_call | solution.py:316
  151.1 2.0 collective-permute-start.22
  153.1 2.6 %collective-permute-start.23 = (bf16[512,128]{1,0:T(8,128)(2,1)S(1)}, bf16[512,128]{1,0:T(8,128)(2,1)S(1)}, u32[]{:S(2)}, u32[]{:S(2)}) collective-permute-start(bf16[512,128]{1,0:T(8,128)(2,1)S(1)} %get-tuple-element.60), channel_id=1, source_target_pairs={{0,12},{4,16},{8,20},{12,24},{16,28},{20,0},{24,4},{28,8},{1,13},{... | collective-permute-start | bytes 393224 | tf_op jit(solution)/shard_map/ppermute | solution.py:384
  156.4 3.7 %collective-permute-start.25 = (bf16[512,128]{1,0:T(8,128)(2,1)S(1)}, bf16[512,128]{1,0:T(8,128)(2,1)S(1)}, u32[]{:S(2)}, u32[]{:S(2)}) collective-permute-start(bf16[512,128]{1,0:T(8,128)(2,1)S(1)} %get-tuple-element.62), channel_id=1, source_target_pairs={{0,20},{4,24},{8,28},{12,0},{16,4},{20,8},{24,12},{28,16},{1,21},{... | collective-permute-start | bytes 393224 | tf_op jit(solution)/shard_map/ppermute | solution.py:384
  160.1 32.1 %attend.2 = (bf16[512,128]{1,0:T(8,128)(2,1)S(1)}, bf16[512,128]{1,0:T(8,128)(2,1)S(1)}, bf16[512,128]{1,0:T(8,128)(2,1)S(1)}, bf16[512,128]{1,0:T(8,128)(2,1)S(...) custom-call(s32[1]{0:T(128)} %bitcast.me_ref, ...), custom_call_target="tpu_custom_call" | custom-call | flops 20000000000 | bytes 4000000 | tf_op jit(solution)/shard_map/attend/pallas_call | solution.py:316
  194.4 2.3 collective-permute-start.11
  198.2 3.8 %collective-permute-done.26.rest_14_ = bf16[512,128]{1,0:T(8,128)(2,1)S(1)} collective-permute-done((bf16[512,128]{1,0:T(8,128)(2,1)S(1)}, bf16[512,128]{1,0:T(8,128)(2,1)S(1)}, u32[]{:S(2)}, u32[]{:S(2)}) %collective-permute-start.26) | collective-permute-done | bytes 131104 | tf_op jit(solution)/shard_map/ppermute | solution.py:384
  202.0 6.0 %collective-permute-start.7 = (bf16[512,128]{1,0:T(8,128)(2,1)S(1)}, bf16[512,128]{1,0:T(8,128)(2,1)S(1)}, u32[]{:S(2)}, u32[]{:S(2)}) collective-permute-start(bf16[512,128]{1,0:T(8,128)(2,1)S(1)} %get-tuple-element.43), channel_id=1, source_target_pairs={{0,4},{4,8},{8,12},{12,16},{16,20},{20,24},{24,28},{28,0},{1,5},{5... | collective-permute-start | bytes 393224 | tf_op jit(solution)/shard_map/ppermute | solution.py:384
  208.0 3.1 %collective-permute-done.10.rest_4_ = bf16[512,128]{1,0:T(8,128)(2,1)S(1)} collective-permute-done((bf16[512,128]{1,0:T(8,128)(2,1)S(1)}, bf16[512,128]{1,0:T(8,128)(2,1)S(1)}, u32[]{:S(2)}, u32[]{:S(2)}) %collective-permute-start.10) | collective-permute-done | bytes 131104 | tf_op jit(solution)/shard_map/ppermute | solution.py:384
  211.0 2.8 %collective-permute-done.11.rest_5_ = bf16[512,128]{1,0:T(8,128)(2,1)S(1)} collective-permute-done((bf16[512,128]{1,0:T(8,128)(2,1)S(1)}, bf16[512,128]{1,0:T(8,128)(2,1)S(1)}, u32[]{:S(2)}, u32[]{:S(2)}) %collective-permute-start.11) | collective-permute-done | bytes 131104 | tf_op jit(solution)/shard_map/ppermute | solution.py:384
  213.9 3.5 %collective-permute-done.8.rest_2_ = bf16[512,128]{1,0:T(8,128)(2,1)S(1)} collective-permute-done((bf16[512,128]{1,0:T(8,128)(2,1)S(1)}, bf16[512,128]{1,0:T(8,128)(2,1)S(1)}, u32[]{:S(2)}, u32[]{:S(2)}) %collective-permute-start.8) | collective-permute-done | bytes 131104 | tf_op jit(solution)/shard_map/ppermute | solution.py:384
  217.4 4.3 %collective-permute-done.9.rest_3_ = bf16[512,128]{1,0:T(8,128)(2,1)S(1)} collective-permute-done((bf16[512,128]{1,0:T(8,128)(2,1)S(1)}, bf16[512,128]{1,0:T(8,128)(2,1)S(1)}, u32[]{:S(2)}, u32[]{:S(2)}) %collective-permute-start.9) | collective-permute-done | bytes 131104 | tf_op jit(solution)/shard_map/ppermute | solution.py:384
  221.7 3.4 %copy-done.3 = bf16[2048,2048]{1,0:T(8,128)(2,1)S(1)} copy-done((bf16[2048,2048]{1,0:T(8,128)(2,1)S(1)}, bf16[2048,2048]{1,0:T(8,128)(2,1)}, u32[]{:S(2)}) %copy-start.3) | copy-done | bytes 8388632
  225.1 8.5 %project.1 = bf16[1,512,2048]{2,1,0:T(8,128)(2,1)} custom-call(s32[1]{0:T(128)} %bitcast.me_ref, bf16[512,128]{1,0:T(8,128)(2,1)S(1)} %get-tuple-element.42.rest_0_, bf16[512,128]{1,0:T(8,128)(2,1)S(1)} %collective-permute-done.7.rest_1_, bf16[512,128]{1,0:T(8,128)(2,1)S(1)} %collective-permute-done.8.rest_2_, ...), custom_call_target="tpu_custom_call" | custom-call | tf_op jit(solution)/shard_map/project/pallas_call | solution.py:360
  (82 shorter events, 27.0 us)
Async XLA Ops:
  6.5 215.2 %all-gather.2.cloned.1.call-start = ((), (), s32[]{:S(2)}) async-start(), calls=%async_computation | async-start | bytes 10485760 | tf_op jit(solution)/shard_map/all_gather | solution.py:381
  10.1 13.2 %collective-permute-start.14 = (bf16[3,128,512]{2,1,0:T(8,128)(2,1)}, bf16[3,128,512]{2,1,0:T(8,128)(2,1)S(1)}, u32[]{:S(2)}, u32[]{:S(2)}) collective-permute-start(bf16[3,128,512]{2,1,0:T(8,128)(2,1)} %get-tuple-element.50), channel_id=1, source_target_pairs={{0,4},{4,8},{8,12},{12,16},{16,20},{20,24},{24,28},{28,0},{1,5},{5... | collective-permute-start | bytes 1179656 | tf_op jit(solution)/shard_map/ppermute | solution.py:384
  11.7 13.8 %collective-permute-start.15 = (bf16[3,128,512]{2,1,0:T(8,128)(2,1)}, bf16[3,128,512]{2,1,0:T(8,128)(2,1)S(1)}, u32[]{:S(2)}, u32[]{:S(2)}) collective-permute-start(bf16[3,128,512]{2,1,0:T(8,128)(2,1)} %get-tuple-element.51), channel_id=1, source_target_pairs={{0,8},{4,12},{8,16},{12,20},{16,24},{20,28},{24,0},{28,4},{1,9},{5... | collective-permute-start | bytes 1179656 | tf_op jit(solution)/shard_map/ppermute | solution.py:384
  13.3 52.0 %collective-permute-start.16 = (bf16[3,128,512]{2,1,0:T(8,128)(2,1)}, bf16[3,128,512]{2,1,0:T(8,128)(2,1)S(1)}, u32[]{:S(2)}, u32[]{:S(2)}) collective-permute-start(bf16[3,128,512]{2,1,0:T(8,128)(2,1)} %get-tuple-element.52), channel_id=1, source_target_pairs={{0,12},{4,16},{8,20},{12,24},{16,28},{20,0},{24,4},{28,8},{1,13},{... | collective-permute-start | bytes 1179656 | tf_op jit(solution)/shard_map/ppermute | solution.py:384
  14.4 59.4 %collective-permute-start.17 = (bf16[3,128,512]{2,1,0:T(8,128)(2,1)}, bf16[3,128,512]{2,1,0:T(8,128)(2,1)}, u32[]{:S(2)}, u32[]{:S(2)}) collective-permute-start(bf16[3,128,512]{2,1,0:T(8,128)(2,1)} %get-tuple-element.53), channel_id=1, source_target_pairs={{0,16},{4,20},{8,24},{12,28},{16,0},{20,4},{24,8},{28,12},{1,17},{... | collective-permute-start | bytes 1179656 | tf_op jit(solution)/shard_map/ppermute | solution.py:384
  17.1 65.6 %collective-permute-start.18 = (bf16[3,128,512]{2,1,0:T(8,128)(2,1)}, bf16[3,128,512]{2,1,0:T(8,128)(2,1)}, u32[]{:S(2)}, u32[]{:S(2)}) collective-permute-start(bf16[3,128,512]{2,1,0:T(8,128)(2,1)} %get-tuple-element.54), channel_id=1, source_target_pairs={{0,20},{4,24},{8,28},{12,0},{16,4},{20,8},{24,12},{28,16},{1,21},{... | collective-permute-start | bytes 1179656 | tf_op jit(solution)/shard_map/ppermute | solution.py:384
  23.3 68.8 %collective-permute-start.19 = (bf16[3,128,512]{2,1,0:T(8,128)(2,1)}, bf16[3,128,512]{2,1,0:T(8,128)(2,1)}, u32[]{:S(2)}, u32[]{:S(2)}) collective-permute-start(bf16[3,128,512]{2,1,0:T(8,128)(2,1)} %get-tuple-element.55), channel_id=1, source_target_pairs={{0,24},{4,28},{8,0},{12,4},{16,8},{20,12},{24,16},{28,20},{1,25},{... | collective-permute-start | bytes 1179656 | tf_op jit(solution)/shard_map/ppermute | solution.py:384
  26.3 66.2 %collective-permute-start.20 = (bf16[3,128,512]{2,1,0:T(8,128)(2,1)}, bf16[3,128,512]{2,1,0:T(8,128)(2,1)}, u32[]{:S(2)}, u32[]{:S(2)}) collective-permute-start(bf16[3,128,512]{2,1,0:T(8,128)(2,1)} %get-tuple-element.56), channel_id=1, source_target_pairs={{0,28},{4,0},{8,4},{12,8},{16,12},{20,16},{24,20},{28,24},{1,29},{... | collective-permute-start | bytes 1179656 | tf_op jit(solution)/shard_map/ppermute | solution.py:384
  65.3 45.6 %collective-permute-start = (bf16[3,128,512]{2,1,0:T(8,128)(2,1)}, bf16[3,128,512]{2,1,0:T(8,128)(2,1)}, u32[]{:S(2)}, u32[]{:S(2)}) collective-permute-start(bf16[3,128,512]{2,1,0:T(8,128)(2,1)} %get-tuple-element.35), channel_id=1, source_target_pairs={{0,4},{4,8},{8,12},{12,16},{16,20},{20,24},{24,28},{28,0},{1,5},{5... | collective-permute-start | bytes 1179656 | tf_op jit(solution)/shard_map/ppermute | solution.py:384
  73.7 37.2 %collective-permute-start.1 = (bf16[3,128,512]{2,1,0:T(8,128)(2,1)}, bf16[3,128,512]{2,1,0:T(8,128)(2,1)}, u32[]{:S(2)}, u32[]{:S(2)}) collective-permute-start(bf16[3,128,512]{2,1,0:T(8,128)(2,1)} %get-tuple-element.36), channel_id=1, source_target_pairs={{0,8},{4,12},{8,16},{12,20},{16,24},{20,28},{24,0},{28,4},{1,9},{5... | collective-permute-start | bytes 1179656 | tf_op jit(solution)/shard_map/ppermute | solution.py:384
  82.7 67.8 %collective-permute-start.2 = (bf16[3,128,512]{2,1,0:T(8,128)(2,1)}, bf16[3,128,512]{2,1,0:T(8,128)(2,1)S(1)}, u32[]{:S(2)}, u32[]{:S(2)}) collective-permute-start(bf16[3,128,512]{2,1,0:T(8,128)(2,1)} %get-tuple-element.37), channel_id=1, source_target_pairs={{0,12},{4,16},{8,20},{12,24},{16,28},{20,0},{24,4},{28,8},{1,13},{... | collective-permute-start | bytes 1179656 | tf_op jit(solution)/shard_map/ppermute | solution.py:384
  92.1 59.0 %collective-permute-start.3 = (bf16[3,128,512]{2,1,0:T(8,128)(2,1)}, bf16[3,128,512]{2,1,0:T(8,128)(2,1)S(1)}, u32[]{:S(2)}, u32[]{:S(2)}) collective-permute-start(bf16[3,128,512]{2,1,0:T(8,128)(2,1)} %get-tuple-element.38), channel_id=1, source_target_pairs={{0,16},{4,20},{8,24},{12,28},{16,0},{20,4},{24,8},{28,12},{1,17},{... | collective-permute-start | bytes 1179656 | tf_op jit(solution)/shard_map/ppermute | solution.py:384
  92.5 60.6 %collective-permute-start.4 = (bf16[3,128,512]{2,1,0:T(8,128)(2,1)}, bf16[3,128,512]{2,1,0:T(8,128)(2,1)S(1)}, u32[]{:S(2)}, u32[]{:S(2)}) collective-permute-start(bf16[3,128,512]{2,1,0:T(8,128)(2,1)} %get-tuple-element.39), channel_id=1, source_target_pairs={{0,20},{4,24},{8,28},{12,0},{16,4},{20,8},{24,12},{28,16},{1,21},{... | collective-permute-start | bytes 1179656 | tf_op jit(solution)/shard_map/ppermute | solution.py:384
  110.9 44.8 %collective-permute-start.5 = (bf16[3,128,512]{2,1,0:T(8,128)(2,1)}, bf16[3,128,512]{2,1,0:T(8,128)(2,1)S(1)}, u32[]{:S(2)}, u32[]{:S(2)}) collective-permute-start(bf16[3,128,512]{2,1,0:T(8,128)(2,1)} %get-tuple-element.40), channel_id=1, source_target_pairs={{0,24},{4,28},{8,0},{12,4},{16,8},{20,12},{24,16},{28,20},{1,25},{... | collective-permute-start | bytes 1179656 | tf_op jit(solution)/shard_map/ppermute | solution.py:384
  110.9 45.5 %collective-permute-start.6 = (bf16[3,128,512]{2,1,0:T(8,128)(2,1)}, bf16[3,128,512]{2,1,0:T(8,128)(2,1)S(1)}, u32[]{:S(2)}, u32[]{:S(2)}) collective-permute-start(bf16[3,128,512]{2,1,0:T(8,128)(2,1)} %get-tuple-element.41), channel_id=1, source_target_pairs={{0,28},{4,0},{8,4},{12,8},{16,12},{20,16},{24,20},{28,24},{1,29},{... | collective-permute-start | bytes 1179656 | tf_op jit(solution)/shard_map/ppermute | solution.py:384
  150.5 41.7 %collective-permute-start.21 = (bf16[512,128]{1,0:T(8,128)(2,1)S(1)}, bf16[512,128]{1,0:T(8,128)(2,1)S(1)}, u32[]{:S(2)}, u32[]{:S(2)}) collective-permute-start(bf16[512,128]{1,0:T(8,128)(2,1)S(1)} %get-tuple-element.58), channel_id=1, source_target_pairs={{0,4},{4,8},{8,12},{12,16},{16,20},{20,24},{24,28},{28,0},{1,5},{5... | collective-permute-start | bytes 393224 | tf_op jit(solution)/shard_map/ppermute | solution.py:384
  151.1 41.1 %collective-permute-start.22 = (bf16[512,128]{1,0:T(8,128)(2,1)S(1)}, bf16[512,128]{1,0:T(8,128)(2,1)S(1)}, u32[]{:S(2)}, u32[]{:S(2)}) collective-permute-start(bf16[512,128]{1,0:T(8,128)(2,1)S(1)} %get-tuple-element.59), channel_id=1, source_target_pairs={{0,8},{4,12},{8,16},{12,20},{16,24},{20,28},{24,0},{28,4},{1,9},{5... | collective-permute-start | bytes 393224 | tf_op jit(solution)/shard_map/ppermute | solution.py:384
  153.1 40.6 %collective-permute-start.23 = (bf16[512,128]{1,0:T(8,128)(2,1)S(1)}, bf16[512,128]{1,0:T(8,128)(2,1)S(1)}, u32[]{:S(2)}, u32[]{:S(2)}) collective-permute-start(bf16[512,128]{1,0:T(8,128)(2,1)S(1)} %get-tuple-element.60), channel_id=1, source_target_pairs={{0,12},{4,16},{8,20},{12,24},{16,28},{20,0},{24,4},{28,8},{1,13},{... | collective-permute-start | bytes 393224 | tf_op jit(solution)/shard_map/ppermute | solution.py:384
  155.7 38.7 %collective-permute-start.24 = (bf16[512,128]{1,0:T(8,128)(2,1)S(1)}, bf16[512,128]{1,0:T(8,128)(2,1)S(1)}, u32[]{:S(2)}, u32[]{:S(2)}) collective-permute-start(bf16[512,128]{1,0:T(8,128)(2,1)S(1)} %get-tuple-element.61), channel_id=1, source_target_pairs={{0,16},{4,20},{8,24},{12,28},{16,0},{20,4},{24,8},{28,12},{1,17},{... | collective-permute-start | bytes 393224 | tf_op jit(solution)/shard_map/ppermute | solution.py:384
  156.4 40.4 %collective-permute-start.25 = (bf16[512,128]{1,0:T(8,128)(2,1)S(1)}, bf16[512,128]{1,0:T(8,128)(2,1)S(1)}, u32[]{:S(2)}, u32[]{:S(2)}) collective-permute-start(bf16[512,128]{1,0:T(8,128)(2,1)S(1)} %get-tuple-element.62), channel_id=1, source_target_pairs={{0,20},{4,24},{8,28},{12,0},{16,4},{20,8},{24,12},{28,16},{1,21},{... | collective-permute-start | bytes 393224 | tf_op jit(solution)/shard_map/ppermute | solution.py:384
  193.7 17.3 %collective-permute-start.10 = (bf16[512,128]{1,0:T(8,128)(2,1)S(1)}, bf16[512,128]{1,0:T(8,128)(2,1)S(1)}, u32[]{:S(2)}, u32[]{:S(2)}) collective-permute-start(bf16[512,128]{1,0:T(8,128)(2,1)S(1)} %get-tuple-element.46), channel_id=1, source_target_pairs={{0,16},{4,20},{8,24},{12,28},{16,0},{20,4},{24,8},{28,12},{1,17},{... | collective-permute-start | bytes 393224 | tf_op jit(solution)/shard_map/ppermute | solution.py:384
  194.4 19.4 %collective-permute-start.11 = (bf16[512,128]{1,0:T(8,128)(2,1)S(1)}, bf16[512,128]{1,0:T(8,128)(2,1)S(1)}, u32[]{:S(2)}, u32[]{:S(2)}) collective-permute-start(bf16[512,128]{1,0:T(8,128)(2,1)S(1)} %get-tuple-element.47), channel_id=1, source_target_pairs={{0,20},{4,24},{8,28},{12,0},{16,4},{20,8},{24,12},{28,16},{1,21},{... | collective-permute-start | bytes 393224 | tf_op jit(solution)/shard_map/ppermute | solution.py:384
  196.7 17.1 %collective-permute-start.12 = (bf16[512,128]{1,0:T(8,128)(2,1)S(1)}, bf16[512,128]{1,0:T(8,128)(2,1)S(1)}, u32[]{:S(2)}, u32[]{:S(2)}) collective-permute-start(bf16[512,128]{1,0:T(8,128)(2,1)S(1)} %get-tuple-element.48), channel_id=1, source_target_pairs={{0,24},{4,28},{8,0},{12,4},{16,8},{20,12},{24,16},{28,20},{1,25},{... | collective-permute-start | bytes 393224 | tf_op jit(solution)/shard_map/ppermute | solution.py:384
  202.0 11.9 %collective-permute-start.13 = (bf16[512,128]{1,0:T(8,128)(2,1)S(1)}, bf16[512,128]{1,0:T(8,128)(2,1)S(1)}, u32[]{:S(2)}, u32[]{:S(2)}) collective-permute-start(bf16[512,128]{1,0:T(8,128)(2,1)S(1)} %get-tuple-element.49), channel_id=1, source_target_pairs={{0,28},{4,0},{8,4},{12,8},{16,12},{20,16},{24,20},{28,24},{1,29},{... | collective-permute-start | bytes 393224 | tf_op jit(solution)/shard_map/ppermute | solution.py:384
  (15 other events, 181.9 us)
Sparse Core Ops, SparseCore 0:
  8.9 59.4 all-gather.1

commit v2 on v1

--- a/solution.py
+++ b/solution.py
@@ -13,6 +13,8 @@
 PAIR = 2 * HD
 EXP_SCALE = HD ** (-0.5) * math.log2(math.e)
 BIG = 1e30
+APART_IN = (False, True)
+APART_OUT = (False, True)
 
 
 def candidate_blocks(nblocks, glob, rand_h):
@@ -106,7 +108,46 @@
     return result.astype(jnp.bfloat16)[None]
 
 
-def cut_kernel(n, feats, row, me_ref, q_ref, k_ref, v_ref, *rest):
+def cut_kernel(n, feats, row, q_ref, k_ref, v_ref, out, held, in_sems, out_sems):
+    def read(to, i):
+        src = (q_ref, k_ref, v_ref)[i]
+        return pltpu.make_async_copy(
+            src.at[0, pl.ds(to * feats + row, PAIR), :], held.at[to, i], in_sems.at[to, i]
+        )
+
+    def write(to):
+        return pltpu.make_async_copy(held.at[to], out.at[to], out_sems.at[to])
+
+    for to in range(n):
+        for i in range(3):
+            read(to, i).start()
+    for to in range(n):
+        for i in range(3):
+            read(to, i).wait()
+        write(to).start()
+    for to in range(n):
+        write(to).wait()
+
+
+def cut(n, row, queries, keys, values):
+    feats = queries.shape[1] // n
+    length = queries.shape[2]
+    hbm = pl.BlockSpec(memory_space=pl.ANY)
+    return pl.pallas_call(
+        functools.partial(cut_kernel, n, feats, row),
+        out_shape=jax.ShapeDtypeStruct((n, 3, PAIR, length), queries.dtype),
+        in_specs=[hbm, hbm, hbm],
+        out_specs=hbm,
+        scratch_shapes=[
+            pltpu.VMEM((n, 3, PAIR, length), queries.dtype),
+            pltpu.SemaphoreType.DMA((n, 3)),
+            pltpu.SemaphoreType.DMA((n,)),
+        ],
+        name="cut",
+    )(queries, keys, values)
+
+
+def cut_apart_kernel(n, feats, row, me_ref, q_ref, k_ref, v_ref, *rest):
     outs = rest[: n - 1]
     held, in_sems, out_sems = rest[n - 1 :]
     me = me_ref[0]
@@ -133,12 +174,12 @@
         write(k).wait()
 
 
-def cut(n, row, me, queries, keys, values):
+def cut_apart(n, row, me, queries, keys, values):
     feats = queries.shape[1] // n
     length = queries.shape[2]
     hbm = pl.BlockSpec(memory_space=pl.ANY)
     return pl.pallas_call(
-        functools.partial(cut_kernel, n, feats, row),
+        functools.partial(cut_apart_kernel, n, feats, row),
         out_shape=[jax.ShapeDtypeStruct((3, PAIR, length), queries.dtype)] * (n - 1),
         in_specs=[pl.BlockSpec(memory_space=pltpu.SMEM), hbm, hbm, hbm],
         out_specs=[hbm] * (n - 1),
@@ -147,7 +188,7 @@
             pltpu.SemaphoreType.DMA((n - 1, 3)),
             pltpu.SemaphoreType.DMA((n - 1,)),
         ],
-        name="cut",
+        name="cut_apart",
     )(me, queries, keys, values)
 
 
@@ -155,34 +196,48 @@
     return jnp.concatenate([x[:, BLK:], x[:, :BLK]], axis=1)
 
 
-def attend_kernel(
-    n, nblocks, feats, row, me_ref, rand_ref, glob_ref, pen_ref, q_ref, k_ref, v_ref, *rest
-):
-    parts, outs = rest[: n - 1], rest[n - 1 : 2 * n - 1]
-    raw, kt, vv, ob, sg, in_sems, own_sems, out_sems = rest[2 * n - 1 :]
+def attend_kernel(n, nblocks, feats, row, apart_in, apart_out, me_ref, rand_ref, glob_ref, *rest):
+    pen_ref, rest = rest[0], rest[1:]
+    ins, rest = (rest[: n + 2], rest[n + 2 :]) if apart_in else (rest[:1], rest[1:])
+    outs, rest = (rest[:n], rest[n:]) if apart_out else (rest[:1], rest[1:])
+    raw, kt, vv, ob, sg, own_sems, in_sems, out_sems = rest
     me = me_ref[0]
     shard = raw.shape[3]
     per = shard // BLK
     tiles = shard // PAIR
     f32, bf16 = jnp.float32, jnp.bfloat16
 
-    own = pl.multiple_of(me * feats + row, PAIR)
     arrivals = []
-    for i, src in enumerate((q_ref, k_ref, v_ref)):
-        copy = pltpu.make_async_copy(
-            src.at[0, pl.ds(own, PAIR), :], raw.at[me, i], own_sems.at[i]
-        )
-        copy.start()
-        arrivals.append(copy)
-    for k in range(1, n):
-        came = lax.rem(me - k + n, n)
-        copy = pltpu.make_async_copy(parts[k - 1], raw.at[came], in_sems.at[k - 1])
-        copy.start()
-        arrivals.append(copy)
-    for copy in arrivals:
-        copy.wait()
-
-    def prepare(s, carry):
+    if apart_in:
+        own = pl.multiple_of(me * feats + row, PAIR)
+        arrivals.append(
+            (
+                me,
+                [
+                    pltpu.make_async_copy(
+                        ins[i].at[0, pl.ds(own, PAIR), :], raw.at[me, i], own_sems.at[i]
+                    )
+                    for i in range(3)
+                ],
+            )
+        )
+        for k in range(1, n):
+            came = lax.rem(me - k + n, n)
+            arrivals.append(
+                (came, [pltpu.make_async_copy(ins[2 + k], raw.at[came], in_sems.at[k])])
+            )
+    else:
+        for s in range(n):
+            arrivals.append(
+                (s, [pltpu.make_async_copy(ins[0].at[s], raw.at[s], in_sems.at[s])])
+            )
+    for _, copies in arrivals:
+        for copy in copies:
+            copy.start()
+
+    for s, copies in arrivals:
+        for copy in copies:
+            copy.wait()
         for t in range(tiles):
             lanes = slice(t * PAIR, (t + 1) * PAIR)
             first = pl.multiple_of(s * shard + t * PAIR, PAIR)
@@ -190,9 +245,6 @@
             v = raw[s, 2, :, lanes]
             vv[0, s * tiles + t] = v
             vv[1, s * tiles + t] = swap_halves(v)
-        return carry
-
-    lax.fori_loop(0, n, prepare, 0)
 
     low = lax.broadcasted_iota(jnp.int32, (BLK, PAIR), 1) < BLK
     zero = jnp.zeros((HD, PAIR), bf16)
@@ -225,7 +277,8 @@
             k_rows.append(jnp.where(low, key_rows(cand[0][c]), key_rows(cand[1][c])))
         scores = jnp.dot(jnp.concatenate(k_rows, axis=0), qbd, preferred_element_type=f32)
         top = jnp.max(scores, axis=0, keepdims=True) * EXP_SCALE
-        shift = pen_ref[j] + top
+        pen = pen_ref[j]
+        shift = jnp.where(low[:8], pen[:, 0:1], pen[:, 1:2]) + top
         probs = [
             jnp.exp2(scores[c * BLK : (c + 1) * BLK] * EXP_SCALE - shift[c : c + 1])
             for c in range(8)
@@ -263,112 +316,124 @@
         ob[s, pl.ds(first, PAIR), :] = jnp.concatenate([a, b], axis=0)
         return carry
 
-    lax.fori_loop(0, nblocks // 2, two_blocks, 0)
-
+    lax.fori_loop(0, nblocks // 2, two_blocks, 0, unroll=8)
+
+    places, columns = [], []
     for g in range(2):
-        block = glob_ref[g]
-        s, first = tile_of(lax.div(block, 2))
+        s, first = tile_of(lax.div(glob_ref[g], 2))
         x = raw[s, 0, :, pl.ds(first, PAIR)]
-        odd = lax.rem(block, 2)
-        qbd = jnp.where(odd == 1, queries_of(x, True), queries_of(x, False))
-
-        def scan_scores(t, top):
-            rows = pl.ds(pl.multiple_of(t * shard, shard), shard)
-            scores = jnp.dot(kt[rows, :], qbd, preferred_element_type=f32)
-            sg[rows, :] = scores
-            return jnp.maximum(top, jnp.max(scores, axis=0, keepdims=True))
-
-        top = lax.fori_loop(0, n, scan_scores, jnp.full((1, PAIR), -jnp.inf, f32))
-        top = top * EXP_SCALE
-
-        def scan_values(t, carry):
-            total, ot = carry
-            rows = pl.ds(pl.multiple_of(t * shard, shard), shard)
-            p = jnp.exp2(sg[rows, :] * EXP_SCALE - top)
-            total = total + jnp.sum(p, axis=0, keepdims=True)
-            ot = ot + jnp.dot(raw[t, 2], p.astype(bf16), preferred_element_type=f32)
-            return total, ot
-
-        total, ot = lax.fori_loop(
-            0, n, scan_values, (jnp.zeros((1, PAIR), f32), jnp.zeros((PAIR, PAIR), f32))
-        )
-        place = pl.multiple_of(lax.rem(block, per) * BLK, BLK)
-        ob[s, pl.ds(place, BLK), :] = finish(ot, total)
-
-    leaving = []
-    for k in range(n):
-        to = lax.rem(me + k, n)
-        copy = pltpu.make_async_copy(ob.at[to], outs[k], out_sems.at[k])
+        odd = lax.rem(glob_ref[g], 2)
+        columns.append(jnp.where(odd == 1, queries_of(x, True), queries_of(x, False)))
+        places.append((s, pl.multiple_of(lax.rem(glob_ref[g], per) * BLK, BLK)))
+    qbd = jnp.concatenate(columns, axis=1)
+    top = jnp.full((1, 2 * PAIR), -jnp.inf, f32)
+    for t in range(n):
+        rows = slice(t * shard, (t + 1) * shard)
+        scores = jnp.dot(kt[rows, :], qbd, preferred_element_type=f32)
+        sg[rows, :] = scores
+        top = jnp.maximum(top, jnp.max(scores, axis=0, keepdims=True))
+    top = top * EXP_SCALE
+    total = jnp.zeros((1, 2 * PAIR), f32)
+    ot = jnp.zeros((PAIR, 2 * PAIR), f32)
+    for t in range(n):
+        p = jnp.exp2(sg[t * shard : (t + 1) * shard, :] * EXP_SCALE - top)
+        total = total + jnp.sum(p, axis=0, keepdims=True)
+        ot = ot + jnp.dot(raw[t, 2], p.astype(bf16), preferred_element_type=f32)
+    for g, (s, place) in enumerate(places):
+        lanes = slice(g * PAIR, (g + 1) * PAIR)
+        ob[s, pl.ds(place, BLK), :] = finish(ot[:, lanes], total[:, lanes])
+
+    if apart_out:
+        leaving = [
+            pltpu.make_async_copy(ob.at[lax.rem(me + k, n)], outs[k], out_sems.at[k])
+            for k in range(n)
+        ]
+    else:
+        leaving = [pltpu.make_async_copy(ob, outs[0], out_sems.at[0])]
+    for copy in leaving:
         copy.start()
-        leaving.append(copy)
     for copy in leaving:
         copy.wait()
 
 
-def attend(n, row, me, rand, glob, pen, queries, keys, values, parts):
-    feats = queries.shape[1] // n
-    shard = queries.shape[2]
+def attend(n, row, me, rand, glob, pen, arrays, feats, apart_out):
+    apart_in = len(arrays) > 1
+    shard = arrays[0].shape[-1]
     length = n * shard
     nblocks = length // BLK
     hbm = pl.BlockSpec(memory_space=pl.ANY)
     smem = pl.BlockSpec(memory_space=pltpu.SMEM)
     vmem = pl.BlockSpec(memory_space=pltpu.VMEM)
+    if apart_out:
+        out_shape = [jax.ShapeDtypeStruct((shard, PAIR), jnp.bfloat16)] * n
+    else:
+        out_shape = [jax.ShapeDtypeStruct((n, shard, PAIR), jnp.bfloat16)]
     return pl.pallas_call(
-        functools.partial(attend_kernel, n, nblocks, feats, row),
-        out_shape=[jax.ShapeDtypeStruct((shard, PAIR), jnp.bfloat16)] * n,
-        in_specs=[smem, smem, smem, vmem, hbm, hbm, hbm] + [hbm] * (n - 1),
-        out_specs=[hbm] * n,
+        functools.partial(attend_kernel, n, nblocks, feats, row, apart_in, apart_out),
+        out_shape=out_shape,
+        in_specs=[smem, smem, smem, vmem] + [hbm] * len(arrays),
+        out_specs=[hbm] * len(out_shape),
         scratch_shapes=[
             pltpu.VMEM((n, 3, PAIR, shard), jnp.bfloat16),
             pltpu.VMEM((length, PAIR), jnp.bfloat16),
             pltpu.VMEM((2, nblocks // 2, PAIR, PAIR), jnp.bfloat16),
             pltpu.VMEM((n, shard, PAIR), jnp.bfloat16),
-            pltpu.VMEM((length, PAIR), jnp.float32),
-            pltpu.SemaphoreType.DMA((n - 1,)),
+            pltpu.VMEM((length, 2 * PAIR), jnp.float32),
             pltpu.SemaphoreType.DMA((3,)),
             pltpu.SemaphoreType.DMA((n,)),
+            pltpu.SemaphoreType.DMA((n,)),
         ],
-        compiler_params=pltpu.CompilerParams(vmem_limit_bytes=40 * 1024 * 1024),
+        compiler_params=pltpu.CompilerParams(vmem_limit_bytes=32 * 1024 * 1024),
         cost_estimate=pl.CostEstimate(
-            flops=20_000_000_000, bytes_accessed=4_000_000, transcendentals=0
+            flops=15_000_000_000, bytes_accessed=4_000_000, transcendentals=0
         ),
         name="attend",
-    )(me, rand, glob, pen, queries, keys, values, *parts)
-
-
-def project_kernel(n, pairs, me_ref, *rest):
-    pieces, w_ref, o_ref, a = rest[: n * pairs], rest[-3], rest[-2], rest[-1]
-    me = me_ref[0]
+    )(me, rand, glob, pen, *arrays)
+
+
+def project_kernel(n, count, before, me_ref, *rest):
+    pieces, w_ref, rest = rest[:count], rest[count], rest[count + 1 :]
+    o_ref, a = rest[-2], rest[-1]
 
     @pl.when(pl.program_id(0) == 0)
     def _():
-        for p in range(pairs):
+        if count == 1:
+            for s in range(n):
+                a[:, s * PAIR : (s + 1) * PAIR] = pieces[0][s]
+        else:
             for k in range(n):
-                came = lax.rem(me - k + n, n)
-                first = pl.multiple_of((came * pairs + p) * PAIR, PAIR)
-                a[:, pl.ds(first, PAIR)] = pieces[p * n + k][...]
-
-    o_ref[0] = jnp.dot(a[...], w_ref[...], preferred_element_type=jnp.float32).astype(o_ref.dtype)
-
-
-def project(n, me, pieces, weight):
-    pairs = len(pieces) // n
-    shard = pieces[0].shape[0]
+                came = lax.rem(me_ref[0] - k + n, n)
+                a[:, pl.ds(pl.multiple_of(came * PAIR, PAIR), PAIR)] = pieces[k][...]
+
+    w = w_ref[...].reshape(a.shape[1], w_ref.shape[2])
+    total = jnp.dot(a[...], w, preferred_element_type=jnp.float32)
+    if before:
+        total = total + rest[0][0]
+    o_ref[0] = total.astype(o_ref.dtype)
+
+
+def project(n, p, me, pieces, weight, before, dtype):
+    shard = pieces[0].shape[-2]
     depth, width = weight.shape
-    tile = 256
-    piece = pl.BlockSpec((shard, PAIR), lambda i: (0, 0))
+    tile = 512
+    rows = weight.reshape(n, depth // n // PAIR, PAIR, width)
+    column = pl.BlockSpec((1, shard, tile), lambda i: (0, 0, i))
     return pl.pallas_call(
-        functools.partial(project_kernel, n, pairs),
+        functools.partial(project_kernel, n, len(pieces), before is not None),
         grid=(width // tile,),
-        out_shape=jax.ShapeDtypeStruct((1, shard, width), jnp.bfloat16),
+        out_shape=jax.ShapeDtypeStruct((1, shard, width), dtype),
         in_specs=[pl.BlockSpec(memory_space=pltpu.SMEM)]
-        + [piece] * (n * pairs)
-        + [pl.BlockSpec((depth, tile), lambda i: (0, i))],
-        out_specs=pl.BlockSpec((1, shard, tile), lambda i: (0, 0, i)),
-        scratch_shapes=[pltpu.VMEM((shard, depth), jnp.bfloat16)],
-        compiler_params=pltpu.CompilerParams(vmem_limit_bytes=40 * 1024 * 1024),
+        + [pl.BlockSpec(x.shape, lambda i, r=x.ndim: (0,) * r) for x in pieces]
+        + [pl.BlockSpec((n, None, PAIR, tile), lambda i: (0, p, 0, i))]
+        + ([] if before is None else [column]),
+        out_specs=column,
+        scratch_shapes=[pltpu.VMEM((shard, n * PAIR), jnp.bfloat16)],
+        compiler_params=pltpu.CompilerParams(vmem_limit_bytes=24 * 1024 * 1024),
+        cost_estimate=pl.CostEstimate(
+            flops=2 * shard * n * PAIR * width, bytes_accessed=10_000_000, transcendentals=0
+        ),
         name="project",
-    )(me, *pieces, weight)
+    )(me, *pieces, rows, *([] if before is None else [before]))
 
 
 def local_paired(n, queries, keys, values, random_blocks, global_blocks, out_weight):
@@ -380,24 +445,36 @@
     glob = global_blocks[0]
     weight = lax.all_gather(out_weight, "dp", axis=0, tiled=True)
 
+    def exchange(x):
+        return lax.all_to_all(x, "seq", split_axis=0, concat_axis=0, tiled=True)
+
     def turn(x, k):
         return lax.ppermute(x, "seq", [(i, (i + k) % n) for i in range(n)])
 
     valid = jax.vmap(lambda r: candidate_blocks(nblocks, glob, r)[1])(random_blocks[0])
     pen = jnp.where(valid, 0.0, BIG).astype(jnp.float32)
+    pen = jnp.transpose(pen.reshape(pairs, 2, nblocks, -1), (0, 2, 3, 1))
+    rand = random_blocks[0].reshape(pairs, -1)
 
     arrived = []
     for p in range(pairs):
-        sent = cut(n, p * PAIR, me, queries, keys, values)
-        arrived.append([turn(sent[k - 1], k) for k in range(1, n)])
-    pieces = []
+        if APART_IN[p % 2]:
+            sent = cut_apart(n, p * PAIR, me, queries, keys, values)
+            got = [turn(sent[k - 1], k) for k in range(1, n)]
+            arrived.append([queries, keys, values] + got)
+        else:
+            arrived.append([exchange(cut(n, p * PAIR, queries, keys, values))])
+    total = None
     for p in range(pairs):
-        rand = random_blocks[0, 2 * p : 2 * p + 2].reshape(-1)
-        lanes = jnp.repeat(jnp.transpose(pen[2 * p : 2 * p + 2], (1, 2, 0)), HD, axis=2)
-        outs = attend(n, p * PAIR, me, rand, glob, lanes, queries, keys, values, arrived[p])
-        pieces.append(outs[0])
-        pieces.extend(turn(outs[k], k) for k in range(1, n))
-    return project(n, me, pieces, weight)
+        apart = APART_OUT[p % 2]
+        outs = attend(n, p * PAIR, me, rand[p], glob, pen[p], arrived[p], feats, apart)
+        if apart:
+            pieces = [outs[0]] + [turn(outs[k], k) for k in range(1, n)]
+        else:
+            pieces = [exchange(outs[0])]
+        dtype = jnp.bfloat16 if p == pairs - 1 else jnp.float32
+        total = project(n, p, me, pieces, weight, total, dtype)
+    return total
 
 
 def solution(mesh):

time: 241 us -> 220 us (0.913); the launches traced: 240 us -> 217 us
  waiting for transfers between devices: 52.3 us -> 107 us
  starting transfers between devices: 78.4 us -> 39.2 us
  Pallas kernels: 80 us -> 43.8 us
  local copies, waits for them, and re-layouts: 15.9 us -> 12.9 us
    ppermute x28 -> x14, starting transfers between devices: 78.4 us -> 17.6 us  [turn(): return lax.ppermute(x, 'seq', [(i, (i + k) % n) for i in range(n)])]
    ppermute x28 -> x14, waiting for transfers between devices: 51.6 us -> 106 us  [turn(): return lax.ppermute(x, 'seq', [(i, (i + k) % n) for i in range(n)])]
    pallas_call x5 -> x6, Pallas kernels: 80 us -> 43.8 us  [the longest x2 28.9 us: attend(): pl.pallas_call(functools.partial(attend_kernel, n, nblocks, feats, row, a...]
    all_to_all x0 -> x2, starting transfers between devices: none -> 21.6 us  [exchange(): return lax.all_to_all(x, 'seq', split_axis=0, concat_axis=0, tiled=True)]
    broadcast_in_dim x2 -> x0, local copies, waits for them, and re-layouts: 2.8 us -> none  [local_paired(): jnp.repeat(jnp.transpose(pen[2 * p:2 * p + 2], (1, 2, 0)), HD, axis=2)]
    reshape x2 -> x0, local copies, waits for them, and re-layouts: 2.67 us -> none  [local_paired(): jnp.repeat(jnp.transpose(pen[2 * p:2 * p + 2], (1, 2, 0)), HD, axis=2)]
    unnamed x21 -> x20, local copies, waits for them, and re-layouts: 9.34 us -> 8.49 us
  transfers between devices with their start and end apart: 29 -> 17, of which waited for: 9 -> 5; matrix products, arithmetic and copies ran while one was open for 3% -> 2% of each run, Pallas kernels for 30% -> 18%
where the time goes in v2:
time: 220 us; the launch traced here: 217 us
  waiting for transfers between devices  107 us (49%)
  Pallas kernels  43.8 us (20%)
  starting transfers between devices  39.2 us (18%)
  between operations  13.6 us (6%)
  local copies, waits for them, and re-layouts  12.9 us (6%)
    ppermute x14, waiting for transfers between devices, turn(): return lax.ppermute(x, 'seq', [(i, (i + k) % n) for i in range(n)])  106 us
    pallas_call x2, Pallas kernels, attend(): pl.pallas_call(functools.partial(attend_kernel, n, nblocks, feats, row, a...  28.9 us
    all_to_all x2, starting transfers between devices, exchange(): return lax.all_to_all(x, 'seq', split_axis=0, concat_axis=0, tiled=True)  21.6 us
    ppermute x14, starting transfers between devices, turn(): return lax.ppermute(x, 'seq', [(i, (i + k) % n) for i in range(n)])  17.6 us
    unnamed x20, local copies, waits for them, and re-layouts  8.49 us
    pallas_call x2, Pallas kernels, project(): pl.pallas_call(functools.partial(project_kernel, n, len(pieces), before i...  8.38 us
  transfers between devices with their start and end apart: 17, of which 5 were waited for; matrix products, arithmetic and copies ran while one was open for 2% of the time, Pallas kernels for 18%

profile of v2, /device:TPU:8, one launch (start us, length us, event | category | flops | bytes accessed | tf_op | source)
XLA Modules:
  0.0 216.5 jit_solution(16286267313983601182)
XLA Ops:
  7.3 3.0 %cut.1 = bf16[8,3,128,512]{3,2,1,0:T(8,128)(2,1)} custom-call(bf16[1,2048,512]{2,1,0:T(8,128)(2,1)} %q_ref.3, bf16[1,2048,512]{2,1,0:T(8,128)(2,1)} %k_ref.3, bf16[1,2048,512]{2,1,0:T(8,128)(2,1)} %v_ref.3), custom_call_target="tpu_custom_call" | custom-call | tf_op jit(solution)/shard_map/cut/pallas_call | solution.py:136
  10.3 6.3 %all-to-all-start = ((bf16[8,3,128,512]{3,2,1,0:T(8,128)(2,1)}), bf16[8,3,128,512]{3,2,1,0:T(8,128)(2,1)S(1)}, u32[]{:S(2)}, u32[]{:S(2)}) async-start(bf16[8,3,128,512]{3,2,1,0:T(8,128)(2,1)} %cut.1), calls=%async_computation | async-start | bytes 6291456 | tf_op jit(solution)/shard_map/all_to_all | solution.py:449
  16.6 3.6 %cut_apart.1 = (bf16[3,128,512]{2,1,0:T(8,128)(2,1)}, bf16[3,128,512]{2,1,0:T(8,128)(2,1)}, bf16[3,128,512]{2,1,0:T(8,128)(2,1)}, bf16[3,128,512]{2,1,0:T(8,128)...) custom-call(s32[1]{0:T(128)} %bitcast.me_ref, ...), custom_call_target="tpu_custom_call" | custom-call | tf_op jit(solution)/shard_map/cut_apart/pallas_call | solution.py:181
  20.1 1.5 collective-permute-start
  21.7 1.5 collective-permute-start.1
  24.1 2.9 %collective-permute-start.3 = (bf16[3,128,512]{2,1,0:T(8,128)(2,1)}, bf16[3,128,512]{2,1,0:T(8,128)(2,1)}, u32[]{:S(2)}, u32[]{:S(2)}) collective-permute-start(bf16[3,128,512]{2,1,0:T(8,128)(2,1)} %get-tuple-element.23), channel_id=1, source_target_pairs={{0,16},{4,20},{8,24},{12,28},{16,0},{20,4},{24,8},{28,12},{1,17},{... | collective-permute-start | bytes 1179656 | tf_op jit(solution)/shard_map/ppermute | solution.py:452
  26.9 1.5 collective-permute-start.4
  31.1 1.0 squeeze.22.rand_ref
  33.0 46.5 %collective-permute-done.rest_4_ = bf16[3,128,512]{2,1,0:T(8,128)(2,1)} collective-permute-done((bf16[3,128,512]{2,1,0:T(8,128)(2,1)}, bf16[3,128,512]{2,1,0:T(8,128)(2,1)}, u32[]{:S(2)}, u32[]{:S(2)}) %collective-permute-start) | collective-permute-done | bytes 393248 | tf_op jit(solution)/shard_map/ppermute | solution.py:452
  79.5 2.8 %collective-permute-start.5 = (bf16[3,128,512]{2,1,0:T(8,128)(2,1)}, bf16[3,128,512]{2,1,0:T(8,128)(2,1)}, u32[]{:S(2)}, u32[]{:S(2)}) collective-permute-start(bf16[3,128,512]{2,1,0:T(8,128)(2,1)} %get-tuple-element.25), channel_id=1, source_target_pairs={{0,24},{4,28},{8,0},{12,4},{16,8},{20,12},{24,16},{28,20},{1,25},{... | collective-permute-start | bytes 1179656 | tf_op jit(solution)/shard_map/ppermute | solution.py:452
  82.3 44.7 %collective-permute-done.1.rest_5_ = bf16[3,128,512]{2,1,0:T(8,128)(2,1)} collective-permute-done((bf16[3,128,512]{2,1,0:T(8,128)(2,1)}, bf16[3,128,512]{2,1,0:T(8,128)(2,1)}, u32[]{:S(2)}, u32[]{:S(2)}) %collective-permute-start.1) | collective-permute-done | bytes 393248 | tf_op jit(solution)/shard_map/ppermute | solution.py:452
  128.0 13.9 %attend.3 = bf16[8,512,128]{2,1,0:T(8,128)(2,1)S(1)} custom-call(s32[1]{0:T(128)} %bitcast.me_ref, s32[384]{0:T(512)S(1)} %squeeze.22.rand_ref, s32[2]{0:T(128)S(1)} %bitcast.19, f32[64,8,2]{2,1,0:T(8,128)S(1)} %copy-done.6, bf16[8,3,128,512]{3,2,1,0:T(8,128)(2,1)S(1)} %all-to-all-done.rest_1_), custom_call_target="tpu_custom_call" | custom-call | flops 15000000512 | bytes 4000000 | tf_op jit(solution)/shard_map/attend/pallas_call | solution.py:371
  142.8 15.3 %all-to-all-start.1 = ((bf16[8,512,128]{2,1,0:T(8,128)(2,1)}), bf16[8,512,128]{2,1,0:T(8,128)(2,1)S(1)}, u32[]{:S(2)}, u32[]{:S(2)}) async-start(bf16[8,512,128]{2,1,0:T(8,128)(2,1)} %copy-done.5), calls=%async_computation.1 | async-start | bytes 2097152 | tf_op jit(solution)/shard_map/all_to_all | solution.py:449
  158.6 1.6 copy-done.3
  160.1 1.6 copy-done.4
  161.7 15.0 %attend.2 = (bf16[512,128]{1,0:T(8,128)(2,1)S(1)}, bf16[512,128]{1,0:T(8,128)(2,1)}, bf16[512,128]{1,0:T(8,128)(2,1)}, bf16[512,128]{1,0:T(8,128)(2,1)}, bf16[51...) custom-call(s32[1]{0:T(128)} %bitcast.me_ref, ...), custom_call_target="tpu_custom_call" | custom-call | flops 15000000512 | bytes 4000000 | tf_op jit(solution)/shard_map/attend/pallas_call | solution.py:371
  176.7 2.4 %collective-permute-start.10 = (bf16[512,128]{1,0:T(8,128)(2,1)S(1)}, bf16[512,128]{1,0:T(8,128)(2,1)S(1)}, u32[]{:S(2)}, u32[]{:S(2)}) collective-permute-start(bf16[512,128]{1,0:T(8,128)(2,1)S(1)} %get-tuple-element.31), channel_id=1, source_target_pairs={{0,16},{4,20},{8,24},{12,28},{16,0},{20,4},{24,8},{28,12},{1,17},{... | collective-permute-start | bytes 393224 | tf_op jit(solution)/shard_map/ppermute | solution.py:452
  179.2 1.5 collective-permute-start.11
  182.2 1.1 collective-permute-start.7
  183.2 11.1 %collective-permute-done.10.rest_4_ = bf16[512,128]{1,0:T(8,128)(2,1)S(1)} collective-permute-done((bf16[512,128]{1,0:T(8,128)(2,1)S(1)}, bf16[512,128]{1,0:T(8,128)(2,1)S(1)}, u32[]{:S(2)}, u32[]{:S(2)}) %collective-permute-start.10) | collective-permute-done | bytes 131104 | tf_op jit(solution)/shard_map/ppermute | solution.py:452
  194.3 2.8 %collective-permute-done.11.rest_5_ = bf16[512,128]{1,0:T(8,128)(2,1)S(1)} collective-permute-done((bf16[512,128]{1,0:T(8,128)(2,1)S(1)}, bf16[512,128]{1,0:T(8,128)(2,1)S(1)}, u32[]{:S(2)}, u32[]{:S(2)}) %collective-permute-start.11) | collective-permute-done | bytes 131104 | tf_op jit(solution)/shard_map/ppermute | solution.py:452
  197.1 3.4 %copy-done = bf16[2048,2048]{1,0:T(8,128)(2,1)S(1)} copy-done((bf16[2048,2048]{1,0:T(8,128)(2,1)S(1)}, bf16[2048,2048]{1,0:T(8,128)(2,1)}, u32[]{:S(2)}) %copy-start) | copy-done | bytes 8388632
  200.5 3.7 %project.2.rest_9_ = f32[1,512,2048]{2,1,0:T(8,128)S(1)} custom-call(s32[1]{0:T(128)} %bitcast.me_ref, bf16[8,512,128]{2,1,0:T(8,128)(2,1)S(1)} %all-to-all-done.1.rest_0_, bf16[8,2,128,2048]{3,2,1,0:T(8,128)(2,1)S(1)} %bitcast.16), custom_call_target="tpu_custom_call" | custom-call | flops 2147483648 | bytes 10000000 | tf_op jit(solution)/shard_map/project/pallas_call | solution.py:421
  205.0 4.7 %project.3 = bf16[1,512,2048]{2,1,0:T(8,128)(2,1)} custom-call(s32[1]{0:T(128)} %bitcast.me_ref, bf16[512,128]{1,0:T(8,128)(2,1)S(1)} %get-tuple-element.27.rest_0_, bf16[512,128]{1,0:T(8,128)(2,1)S(1)} %collective-permute-done.7.rest_1_, bf16[512,128]{1,0:T(8,128)(2,1)S(1)} %collective-permute-done.8.rest_2_, ...), custom_call_target="tpu_custom_call" | custom-call | flops 2147483648 | bytes 10000000 | tf_op jit(solution)/shard_map/project/pallas_call | solution.py:421
  (60 shorter events, 9.7 us)
Async XLA Ops:
  6.5 190.6 %all-gather.2.cloned.1.call-start = ((), (), s32[]{:S(2)}) async-start(), calls=%async_computation.2 | async-start | bytes 10485760 | tf_op jit(solution)/shard_map/all_gather | solution.py:446
  10.3 116.8 %all-to-all-start = ((bf16[8,3,128,512]{3,2,1,0:T(8,128)(2,1)}), bf16[8,3,128,512]{3,2,1,0:T(8,128)(2,1)S(1)}, u32[]{:S(2)}, u32[]{:S(2)}) async-start(bf16[8,3,128,512]{3,2,1,0:T(8,128)(2,1)} %cut.1), calls=%async_computation | async-start | bytes 6291456 | tf_op jit(solution)/shard_map/all_to_all | solution.py:449
  16.6 11.9 %copy-start.8 = (s32[1,4,64,3]{2,1,3,0:T(4,128)S(1)}, s32[1,4,64,3]{2,1,3,0:T(4,128)}, u32[]{:S(2)}) copy-start(s32[1,4,64,3]{2,1,3,0:T(4,128)} %param.9) | copy-start | bytes 9220
  16.6 11.9 %copy-start.7 = (s32[1,2]{1,0:T(1,128)S(1)}, s32[1,2]{1,0:T(1,128)}, u32[]{:S(2)}) copy-start(s32[1,2]{1,0:T(1,128)} %param.10) | copy-start | bytes 28
  20.1 59.4 %collective-permute-start = (bf16[3,128,512]{2,1,0:T(8,128)(2,1)}, bf16[3,128,512]{2,1,0:T(8,128)(2,1)}, u32[]{:S(2)}, u32[]{:S(2)}) collective-permute-start(bf16[3,128,512]{2,1,0:T(8,128)(2,1)} %get-tuple-element.20), channel_id=1, source_target_pairs={{0,4},{4,8},{8,12},{12,16},{16,20},{20,24},{24,28},{28,0},{1,5},{5... | collective-permute-start | bytes 1179656 | tf_op jit(solution)/shard_map/ppermute | solution.py:452
  21.7 105.4 %collective-permute-start.1 = (bf16[3,128,512]{2,1,0:T(8,128)(2,1)}, bf16[3,128,512]{2,1,0:T(8,128)(2,1)}, u32[]{:S(2)}, u32[]{:S(2)}) collective-permute-start(bf16[3,128,512]{2,1,0:T(8,128)(2,1)} %get-tuple-element.21), channel_id=1, source_target_pairs={{0,8},{4,12},{8,16},{12,20},{16,24},{20,28},{24,0},{28,4},{1,9},{5... | collective-permute-start | bytes 1179656 | tf_op jit(solution)/shard_map/ppermute | solution.py:452
  23.2 135.3 %collective-permute-start.2 = (bf16[3,128,512]{2,1,0:T(8,128)(2,1)}, bf16[3,128,512]{2,1,0:T(8,128)(2,1)}, u32[]{:S(2)}, u32[]{:S(2)}) collective-permute-start(bf16[3,128,512]{2,1,0:T(8,128)(2,1)} %get-tuple-element.22), channel_id=1, source_target_pairs={{0,12},{4,16},{8,20},{12,24},{16,28},{20,0},{24,4},{28,8},{1,13},{... | collective-permute-start | bytes 1179656 | tf_op jit(solution)/shard_map/ppermute | solution.py:452
  24.1 134.4 %collective-permute-start.3 = (bf16[3,128,512]{2,1,0:T(8,128)(2,1)}, bf16[3,128,512]{2,1,0:T(8,128)(2,1)}, u32[]{:S(2)}, u32[]{:S(2)}) collective-permute-start(bf16[3,128,512]{2,1,0:T(8,128)(2,1)} %get-tuple-element.23), channel_id=1, source_target_pairs={{0,16},{4,20},{8,24},{12,28},{16,0},{20,4},{24,8},{28,12},{1,17},{... | collective-permute-start | bytes 1179656 | tf_op jit(solution)/shard_map/ppermute | solution.py:452
  26.9 131.6 %collective-permute-start.4 = (bf16[3,128,512]{2,1,0:T(8,128)(2,1)}, bf16[3,128,512]{2,1,0:T(8,128)(2,1)}, u32[]{:S(2)}, u32[]{:S(2)}) collective-permute-start(bf16[3,128,512]{2,1,0:T(8,128)(2,1)} %get-tuple-element.24), channel_id=1, source_target_pairs={{0,20},{4,24},{8,28},{12,0},{16,4},{20,8},{24,12},{28,16},{1,21},{... | collective-permute-start | bytes 1179656 | tf_op jit(solution)/shard_map/ppermute | solution.py:452
  79.5 79.0 %collective-permute-start.5 = (bf16[3,128,512]{2,1,0:T(8,128)(2,1)}, bf16[3,128,512]{2,1,0:T(8,128)(2,1)}, u32[]{:S(2)}, u32[]{:S(2)}) collective-permute-start(bf16[3,128,512]{2,1,0:T(8,128)(2,1)} %get-tuple-element.25), channel_id=1, source_target_pairs={{0,24},{4,28},{8,0},{12,4},{16,8},{20,12},{24,16},{28,20},{1,25},{... | collective-permute-start | bytes 1179656 | tf_op jit(solution)/shard_map/ppermute | solution.py:452
  127.0 31.5 %collective-permute-start.6 = (bf16[3,128,512]{2,1,0:T(8,128)(2,1)}, bf16[3,128,512]{2,1,0:T(8,128)(2,1)}, u32[]{:S(2)}, u32[]{:S(2)}) collective-permute-start(bf16[3,128,512]{2,1,0:T(8,128)(2,1)} %get-tuple-element.26), channel_id=1, source_target_pairs={{0,28},{4,0},{8,4},{12,8},{16,12},{20,16},{24,20},{28,24},{1,29},{... | collective-permute-start | bytes 1179656 | tf_op jit(solution)/shard_map/ppermute | solution.py:452
  128.0 30.2 %copy-start.9 = (s32[1,2,64,3]{2,1,3,0:T(2,128)S(1)}, s32[1,2,64,3]{2,1,3,0:T(2,128)}, u32[]{:S(2)}) copy-start(s32[1,2,64,3]{2,1,3,0:T(2,128)} %get-tuple-element.40) | copy-start | bytes 4612
  142.8 15.7 %copy-start.2 = (bf16[1,2048,512]{2,1,0:T(8,128)(2,1)S(1)}, bf16[1,2048,512]{2,1,0:T(8,128)(2,1)}, u32[]{:S(2)}) copy-start(bf16[1,2048,512]{2,1,0:T(8,128)(2,1)} %q_ref.3) | copy-start | bytes 6291460
  142.8 54.3 %all-to-all-start.1 = ((bf16[8,512,128]{2,1,0:T(8,128)(2,1)}), bf16[8,512,128]{2,1,0:T(8,128)(2,1)S(1)}, u32[]{:S(2)}, u32[]{:S(2)}) async-start(bf16[8,512,128]{2,1,0:T(8,128)(2,1)} %copy-done.5), calls=%async_computation.1 | async-start | bytes 2097152 | tf_op jit(solution)/shard_map/all_to_all | solution.py:449
  158.5 1.6 copy-start.3
  176.7 17.6 %collective-permute-start.10 = (bf16[512,128]{1,0:T(8,128)(2,1)S(1)}, bf16[512,128]{1,0:T(8,128)(2,1)S(1)}, u32[]{:S(2)}, u32[]{:S(2)}) collective-permute-start(bf16[512,128]{1,0:T(8,128)(2,1)S(1)} %get-tuple-element.31), channel_id=1, source_target_pairs={{0,16},{4,20},{8,24},{12,28},{16,0},{20,4},{24,8},{28,12},{1,17},{... | collective-permute-start | bytes 393224 | tf_op jit(solution)/shard_map/ppermute | solution.py:452
  179.2 17.9 %collective-permute-start.11 = (bf16[512,128]{1,0:T(8,128)(2,1)S(1)}, bf16[512,128]{1,0:T(8,128)(2,1)S(1)}, u32[]{:S(2)}, u32[]{:S(2)}) collective-permute-start(bf16[512,128]{1,0:T(8,128)(2,1)S(1)} %get-tuple-element.32), channel_id=1, source_target_pairs={{0,20},{4,24},{8,28},{12,0},{16,4},{20,8},{24,12},{28,16},{1,21},{... | collective-permute-start | bytes 393224 | tf_op jit(solution)/shard_map/ppermute | solution.py:452
  180.6 23.6 %collective-permute-start.12 = (bf16[512,128]{1,0:T(8,128)(2,1)}, bf16[512,128]{1,0:T(8,128)(2,1)S(1)}, u32[]{:S(2)}, u32[]{:S(2)}) collective-permute-start(bf16[512,128]{1,0:T(8,128)(2,1)} %get-tuple-element.33), channel_id=1, source_target_pairs={{0,24},{4,28},{8,0},{12,4},{16,8},{20,12},{24,16},{28,20},{1,25},{... | collective-permute-start | bytes 393224 | tf_op jit(solution)/shard_map/ppermute | solution.py:452
  181.2 23.0 %collective-permute-start.13 = (bf16[512,128]{1,0:T(8,128)(2,1)}, bf16[512,128]{1,0:T(8,128)(2,1)S(1)}, u32[]{:S(2)}, u32[]{:S(2)}) collective-permute-start(bf16[512,128]{1,0:T(8,128)(2,1)} %get-tuple-element.34), channel_id=1, source_target_pairs={{0,28},{4,0},{8,4},{12,8},{16,12},{20,16},{24,20},{28,24},{1,29},{... | collective-permute-start | bytes 393224 | tf_op jit(solution)/shard_map/ppermute | solution.py:452
  182.2 22.1 %collective-permute-start.7 = (bf16[512,128]{1,0:T(8,128)(2,1)}, bf16[512,128]{1,0:T(8,128)(2,1)S(1)}, u32[]{:S(2)}, u32[]{:S(2)}) collective-permute-start(bf16[512,128]{1,0:T(8,128)(2,1)} %get-tuple-element.28), channel_id=1, source_target_pairs={{0,4},{4,8},{8,12},{12,16},{16,20},{20,24},{24,28},{28,0},{1,5},{5... | collective-permute-start | bytes 393224 | tf_op jit(solution)/shard_map/ppermute | solution.py:452
  194.3 10.0 %collective-permute-start.8 = (bf16[512,128]{1,0:T(8,128)(2,1)}, bf16[512,128]{1,0:T(8,128)(2,1)S(1)}, u32[]{:S(2)}, u32[]{:S(2)}) collective-permute-start(bf16[512,128]{1,0:T(8,128)(2,1)} %get-tuple-element.29), channel_id=1, source_target_pairs={{0,8},{4,12},{8,16},{12,20},{16,24},{20,28},{24,0},{28,4},{1,9},{5... | collective-permute-start | bytes 393224 | tf_op jit(solution)/shard_map/ppermute | solution.py:452
  197.1 7.9 %collective-permute-start.9 = (bf16[512,128]{1,0:T(8,128)(2,1)}, bf16[512,128]{1,0:T(8,128)(2,1)S(1)}, u32[]{:S(2)}, u32[]{:S(2)}) collective-permute-start(bf16[512,128]{1,0:T(8,128)(2,1)} %get-tuple-element.30), channel_id=1, source_target_pairs={{0,12},{4,16},{8,20},{12,24},{16,28},{20,0},{24,4},{28,8},{1,13},{... | collective-permute-start | bytes 393224 | tf_op jit(solution)/shard_map/ppermute | solution.py:452
  197.1 3.4 %copy-start = (bf16[2048,2048]{1,0:T(8,128)(2,1)S(1)}, bf16[2048,2048]{1,0:T(8,128)(2,1)}, u32[]{:S(2)}) copy-start(bf16[2048,2048]{1,0:T(8,128)(2,1)} %all-gather.2.cloned.1.call-done) | copy-start | bytes 25165828
  200.5 4.5 %copy-start.1 = (bf16[2048,2048]{1,0:T(8,128)(2,1)S(1)}, bf16[2048,2048]{1,0:T(8,128)(2,1)}, u32[]{:S(2)}) copy-start(bf16[2048,2048]{1,0:T(8,128)(2,1)} %all-gather.2.cloned.1.call-done) | copy-start | bytes 25165828
  (3 other events, 3.5 us)
Sparse Core Ops, SparseCore 0:
  8.9 59.4 all-gather.1

commit v3 on v2

--- a/solution.py
+++ b/solution.py
@@ -154,7 +154,7 @@
     order = range(n - 1, 0, -1)
 
     def read(k, i):
-        start = pl.multiple_of(lax.rem(me + k, n) * feats + row, PAIR)
+        start = pl.multiple_of((me ^ k) * feats + row, PAIR)
         src = (q_ref, k_ref, v_ref)[i]
         return pltpu.make_async_copy(
             src.at[0, pl.ds(start, PAIR), :], held.at[k - 1, i], in_sems.at[k - 1, i]
@@ -222,7 +222,7 @@
             )
         )
         for k in range(1, n):
-            came = lax.rem(me - k + n, n)
+            came = me ^ k
             arrivals.append(
                 (came, [pltpu.make_async_copy(ins[2 + k], raw.at[came], in_sems.at[k])])
             )
@@ -345,7 +345,7 @@
 
     if apart_out:
         leaving = [
-            pltpu.make_async_copy(ob.at[lax.rem(me + k, n)], outs[k], out_sems.at[k])
+            pltpu.make_async_copy(ob.at[me ^ k], outs[k], out_sems.at[k])
             for k in range(n)
         ]
     else:
@@ -391,40 +391,47 @@
     )(me, rand, glob, pen, *arrays)
 
 
-def project_kernel(n, count, before, me_ref, *rest):
-    pieces, w_ref, rest = rest[:count], rest[count], rest[count + 1 :]
+def project_kernel(n, ndp, count, before, me_ref, *rest):
+    pieces, rest = rest[:count], rest[count:]
+    weights, rest = rest[:ndp], rest[ndp:]
     o_ref, a = rest[-2], rest[-1]
+    held = n // ndp
 
     @pl.when(pl.program_id(0) == 0)
     def _():
         if count == 1:
-            for s in range(n):
-                a[:, s * PAIR : (s + 1) * PAIR] = pieces[0][s]
+            for r in range(ndp):
+                for u in range(held):
+                    first = (r * held + u) * PAIR
+                    a[:, first : first + PAIR] = pieces[0][(me_ref[1] ^ r) * held + u]
         else:
             for k in range(n):
-                came = lax.rem(me_ref[0] - k + n, n)
-                a[:, pl.ds(pl.multiple_of(came * PAIR, PAIR), PAIR)] = pieces[k][...]
-
-    w = w_ref[...].reshape(a.shape[1], w_ref.shape[2])
+                came = me_ref[0] ^ k
+                place = (lax.div(came, held) ^ me_ref[1]) * held + lax.rem(came, held)
+                a[:, pl.ds(pl.multiple_of(place * PAIR, PAIR), PAIR)] = pieces[k][...]
+
+    w = jnp.concatenate([w_ref[...].reshape(held * PAIR, -1) for w_ref in weights], axis=0)
     total = jnp.dot(a[...], w, preferred_element_type=jnp.float32)
     if before:
         total = total + rest[0][0]
     o_ref[0] = total.astype(o_ref.dtype)
 
 
-def project(n, p, me, pieces, weight, before, dtype):
+def project(n, p, me, pieces, weights, before, dtype):
     shard = pieces[0].shape[-2]
-    depth, width = weight.shape
+    ndp = len(weights)
+    depth, width = weights[0].shape
+    held = n // ndp
     tile = 512
-    rows = weight.reshape(n, depth // n // PAIR, PAIR, width)
+    rows = [w.reshape(held, depth // held // PAIR, PAIR, width) for w in weights]
     column = pl.BlockSpec((1, shard, tile), lambda i: (0, 0, i))
     return pl.pallas_call(
-        functools.partial(project_kernel, n, len(pieces), before is not None),
+        functools.partial(project_kernel, n, ndp, len(pieces), before is not None),
         grid=(width // tile,),
         out_shape=jax.ShapeDtypeStruct((1, shard, width), dtype),
         in_specs=[pl.BlockSpec(memory_space=pltpu.SMEM)]
         + [pl.BlockSpec(x.shape, lambda i, r=x.ndim: (0,) * r) for x in pieces]
-        + [pl.BlockSpec((n, None, PAIR, tile), lambda i: (0, p, 0, i))]
+        + [pl.BlockSpec((held, None, PAIR, tile), lambda i: (0, p, 0, i))] * ndp
         + ([] if before is None else [column]),
         out_specs=column,
         scratch_shapes=[pltpu.VMEM((shard, n * PAIR), jnp.bfloat16)],
@@ -433,23 +440,35 @@
             flops=2 * shard * n * PAIR * width, bytes_accessed=10_000_000, transcendentals=0
         ),
         name="project",
-    )(me, *pieces, rows, *([] if before is None else [before]))
-
-
-def local_paired(n, queries, keys, values, random_blocks, global_blocks, out_weight):
-    me = lax.axis_index("seq").astype(jnp.int32)[None]
+    )(me, *pieces, *rows, *([] if before is None else [before]))
+
+
+def gather_weight(ndp, weight):
+    parts = {0: weight}
+    bit = ndp // 2
+    while bit:
+        for r in list(parts):
+            parts[r + bit] = lax.ppermute(parts[r], "dp", [(i, i ^ bit) for i in range(ndp)])
+        bit //= 2
+    return [parts[r] for r in range(ndp)]
+
+
+def local_paired(n, ndp, queries, keys, values, random_blocks, global_blocks, out_weight):
+    me = jnp.stack([lax.axis_index("seq"), lax.axis_index("dp")]).astype(jnp.int32)
     feats = queries.shape[1] // n
     length = queries.shape[2] * n
     nblocks = length // BLK
     pairs = feats // PAIR
     glob = global_blocks[0]
-    weight = lax.all_gather(out_weight, "dp", axis=0, tiled=True)
 
     def exchange(x):
         return lax.all_to_all(x, "seq", split_axis=0, concat_axis=0, tiled=True)
 
-    def turn(x, k):
-        return lax.ppermute(x, "seq", [(i, (i + k) % n) for i in range(n)])
+    def swap(arrays, order):
+        got = {k: lax.ppermute(arrays[k - 1], "seq", [(i, i ^ k) for i in range(n)]) for k in order}
+        return [got[k] for k in range(1, n)]
+
+    near, far = list(range(1, n // 2)), list(range(n // 2, n))
 
     valid = jax.vmap(lambda r: candidate_blocks(nblocks, glob, r)[1])(random_blocks[0])
     pen = jnp.where(valid, 0.0, BIG).astype(jnp.float32)
@@ -460,25 +479,25 @@
     for p in range(pairs):
         if APART_IN[p % 2]:
             sent = cut_apart(n, p * PAIR, me, queries, keys, values)
-            got = [turn(sent[k - 1], k) for k in range(1, n)]
-            arrived.append([queries, keys, values] + got)
+            arrived.append([queries, keys, values] + swap(sent, near + far))
         else:
             arrived.append([exchange(cut(n, p * PAIR, queries, keys, values))])
+    weights = gather_weight(ndp, lax.optimization_barrier((out_weight, arrived[1][3]))[0])
     total = None
     for p in range(pairs):
         apart = APART_OUT[p % 2]
         outs = attend(n, p * PAIR, me, rand[p], glob, pen[p], arrived[p], feats, apart)
         if apart:
-            pieces = [outs[0]] + [turn(outs[k], k) for k in range(1, n)]
+            pieces = [outs[0]] + swap(outs[1:], far + near)
         else:
             pieces = [exchange(outs[0])]
         dtype = jnp.bfloat16 if p == pairs - 1 else jnp.float32
-        total = project(n, p, me, pieces, weight, total, dtype)
+        total = project(n, p, me, pieces, weights, total, dtype)
     return total
 
 
 def solution(mesh):
-    n = mesh.shape["seq"]
+    n, ndp = mesh.shape["seq"], mesh.shape["dp"]
     in_specs = (
         P("dp", None, "seq"),
         P("dp", None, "seq"),
@@ -491,8 +510,9 @@
 
     def local(queries, keys, *rest):
         feats, shard = queries.shape[1] // n, queries.shape[2]
-        paired = feats % PAIR == 0 and shard % PAIR == 0
-        body = functools.partial(local_paired, n) if paired else local_plain
+        paired = feats % PAIR == 0 and shard % PAIR == 0 and n % ndp == 0
+        paired = paired and n & (n - 1) == 0 and ndp & (ndp - 1) == 0
+        body = functools.partial(local_paired, n, ndp) if paired else local_plain
         return body(queries, keys, *rest)
 
     return jax.shard_map(local, mesh=mesh, in_specs=in_specs, out_specs=out_specs, check_vma=False)

time: 220 us -> 205 us (0.932)
  between operations: 13.6 us -> 0.19 us
  waiting for transfers between devices: 107 us -> 101 us
  Pallas kernels: 43.8 us -> 47 us
  local copies, waits for them, and re-layouts: 12.9 us -> 9.86 us
  starting transfers between devices: 39.2 us -> 41.5 us
    ppermute x14 -> x17, starting transfers between devices: 17.6 us -> 27.7 us  [the longest x14 25.7 us: swap(): lax.ppermute(arrays[k - 1], 'seq', [(i, i ^ k) for i in range(n)])]
    all_to_all x2, starting transfers between devices: 21.6 us -> 13.8 us  [exchange(): return lax.all_to_all(x, 'seq', split_axis=0, concat_axis=0, tiled=True)]
    ppermute x14 -> x17, waiting for transfers between devices: 106 us -> 101 us  [the longest x14 101 us: swap(): lax.ppermute(arrays[k - 1], 'seq', [(i, i ^ k) for i in range(n)])]
    pallas_call x2, Pallas kernels: 8.38 us -> 11.5 us  [project(): pl.pallas_call(functools.partial(project_kernel, n, ndp, len(pieces), bef...]
  transfers between devices with their start and end apart: 17 -> 19, of which waited for: 5 -> 8; matrix products, arithmetic and copies ran while one was open for 2% -> 2% of each run, Pallas kernels for 18% -> 19%
where the time goes in v3:
time: 205 us; the launch traced here: 202 us
  waiting for transfers between devices  101 us (49%)
  Pallas kernels  47 us (23%)
  starting transfers between devices  41.5 us (20%)
  local copies, waits for them, and re-layouts  9.86 us (5%)
    ppermute x14, waiting for transfers between devices, swap(): lax.ppermute(arrays[k - 1], 'seq', [(i, i ^ k) for i in range(n)])  101 us
    pallas_call x2, Pallas kernels, attend(): pl.pallas_call(functools.partial(attend_kernel, n, nblocks, feats, row, a...  28.9 us
    ppermute x14, starting transfers between devices, swap(): lax.ppermute(arrays[k - 1], 'seq', [(i, i ^ k) for i in range(n)])  25.7 us
    all_to_all x2, starting transfers between devices, exchange(): return lax.all_to_all(x, 'seq', split_axis=0, concat_axis=0, tiled=True)  13.8 us
    pallas_call x2, Pallas kernels, project(): pl.pallas_call(functools.partial(project_kernel, n, ndp, len(pieces), bef...  11.5 us
    unnamed x20, local copies, waits for them, and re-layouts  6.86 us
  transfers between devices with their start and end apart: 19, of which 8 were waited for; matrix products, arithmetic and copies ran while one was open for 2% of the time, Pallas kernels for 19%

profile of v3, /device:TPU:8, one launch (start us, length us, event | category | flops | bytes accessed | tf_op | source)
XLA Modules:
  0.0 202.0 jit_solution(614254146026425634)
XLA Ops:
  0.0 3.0 %cut.1 = bf16[8,3,128,512]{3,2,1,0:T(8,128)(2,1)} custom-call(bf16[1,2048,512]{2,1,0:T(8,128)(2,1)} %q_ref.3, bf16[1,2048,512]{2,1,0:T(8,128)(2,1)} %k_ref.3, bf16[1,2048,512]{2,1,0:T(8,128)(2,1)} %v_ref.3), custom_call_target="tpu_custom_call" | custom-call | tf_op jit(solution)/shard_map/cut/pallas_call | solution.py:136
  3.0 6.3 %all-to-all-start = ((bf16[8,3,128,512]{3,2,1,0:T(8,128)(2,1)}), bf16[8,3,128,512]{3,2,1,0:T(8,128)(2,1)S(1)}, u32[]{:S(2)}, u32[]{:S(2)}) async-start(bf16[8,3,128,512]{3,2,1,0:T(8,128)(2,1)} %cut.1), calls=%async_computation | async-start | bytes 6291456 | tf_op jit(solution)/shard_map/all_to_all | solution.py:465
  10.0 3.6 %cut_apart.1 = (bf16[3,128,512]{2,1,0:T(8,128)(2,1)}, bf16[3,128,512]{2,1,0:T(8,128)(2,1)}, bf16[3,128,512]{2,1,0:T(8,128)(2,1)}, bf16[3,128,512]{2,1,0:T(8,128)...) custom-call(s32[2]{0:T(128)} %pad_add_fusion.3.me_ref, ...), custom_call_target="tpu_custom_call" | custom-call | tf_op jit(solution)/shard_map/cut_apart/pallas_call | solution.py:181
  15.2 27.8 %collective-permute-done.rest_4_ = bf16[3,128,512]{2,1,0:T(8,128)(2,1)S(1)} collective-permute-done((bf16[3,128,512]{2,1,0:T(8,128)(2,1)}, bf16[3,128,512]{2,1,0:T(8,128)(2,1)S(1)}, u32[]{:S(2)}, u32[]{:S(2)}) %collective-permute-start) | collective-permute-done | bytes 393248 | tf_op jit(solution)/shard_map/ppermute | solution.py:468
  46.8 2.3 %collective-permute-start.2 = (bf16[3,128,512]{2,1,0:T(8,128)(2,1)}, bf16[3,128,512]{2,1,0:T(8,128)(2,1)}, u32[]{:S(2)}, u32[]{:S(2)}) collective-permute-start(bf16[3,128,512]{2,1,0:T(8,128)(2,1)} %get-tuple-element.23), channel_id=1, source_target_pairs={{0,12},{4,8},{8,4},{12,0},{16,28},{20,24},{24,20},{28,16},{1,13},{... | collective-permute-start | bytes 1179656 | tf_op jit(solution)/shard_map/ppermute | solution.py:468
  49.1 2.1 %collective-permute-start.3 = (bf16[3,128,512]{2,1,0:T(8,128)(2,1)}, bf16[3,128,512]{2,1,0:T(8,128)(2,1)}, u32[]{:S(2)}, u32[]{:S(2)}) collective-permute-start(bf16[3,128,512]{2,1,0:T(8,128)(2,1)} %get-tuple-element.24), channel_id=1, source_target_pairs={{0,16},{4,20},{8,24},{12,28},{16,0},{20,4},{24,8},{28,12},{1,17},{... | collective-permute-start | bytes 1179656 | tf_op jit(solution)/shard_map/ppermute | solution.py:468
  51.2 2.2 %collective-permute-start.4 = (bf16[3,128,512]{2,1,0:T(8,128)(2,1)}, bf16[3,128,512]{2,1,0:T(8,128)(2,1)}, u32[]{:S(2)}, u32[]{:S(2)}) collective-permute-start(bf16[3,128,512]{2,1,0:T(8,128)(2,1)} %get-tuple-element.25), channel_id=1, source_target_pairs={{0,20},{4,16},{8,28},{12,24},{16,4},{20,0},{24,12},{28,8},{1,21},{... | collective-permute-start | bytes 1179656 | tf_op jit(solution)/shard_map/ppermute | solution.py:468
  57.4 13.8 %collective-permute-done.1.rest_5_ = bf16[3,128,512]{2,1,0:T(8,128)(2,1)} collective-permute-done((bf16[3,128,512]{2,1,0:T(8,128)(2,1)}, bf16[3,128,512]{2,1,0:T(8,128)(2,1)}, u32[]{:S(2)}, u32[]{:S(2)}) %collective-permute-start.1) | collective-permute-done | bytes 393248 | tf_op jit(solution)/shard_map/ppermute | solution.py:468
  71.3 1.9 collective-permute-start.5
  73.2 7.8 %collective-permute-done.2.rest_6_ = bf16[3,128,512]{2,1,0:T(8,128)(2,1)} collective-permute-done((bf16[3,128,512]{2,1,0:T(8,128)(2,1)}, bf16[3,128,512]{2,1,0:T(8,128)(2,1)}, u32[]{:S(2)}, u32[]{:S(2)}) %collective-permute-start.2) | collective-permute-done | bytes 393248 | tf_op jit(solution)/shard_map/ppermute | solution.py:468
  82.5 37.3 %collective-permute-done.3.rest_7_ = bf16[3,128,512]{2,1,0:T(8,128)(2,1)} collective-permute-done((bf16[3,128,512]{2,1,0:T(8,128)(2,1)}, bf16[3,128,512]{2,1,0:T(8,128)(2,1)}, u32[]{:S(2)}, u32[]{:S(2)}) %collective-permute-start.3) | collective-permute-done | bytes 393248 | tf_op jit(solution)/shard_map/ppermute | solution.py:468
  121.3 13.9 %attend.3 = bf16[8,512,128]{2,1,0:T(8,128)(2,1)S(1)} custom-call(s32[2]{0:T(128)S(1)} %copy-done.5, s32[384]{0:T(512)S(1)} %squeeze.22.rand_ref, s32[2]{0:T(128)S(1)} %bitcast.21, f32[64,8,2]{2,1,0:T(8,128)S(1)} %copy-done.4, bf16[8,3,128,512]{3,2,1,0:T(8,128)(2,1)S(1)} %all-to-all-done.rest_1_), custom_call_target="tpu_custom_call" | custom-call | flops 15000000512 | bytes 4000000 | tf_op jit(solution)/shard_map/attend/pallas_call | solution.py:371
  136.2 7.5 %all-to-all-start.1 = ((bf16[8,512,128]{2,1,0:T(8,128)(2,1)}), bf16[8,512,128]{2,1,0:T(8,128)(2,1)S(1)}, u32[]{:S(2)}, u32[]{:S(2)}) async-start(bf16[8,512,128]{2,1,0:T(8,128)(2,1)} %copy-done.3), calls=%async_computation.1 | async-start | bytes 2097152 | tf_op jit(solution)/shard_map/all_to_all | solution.py:465
  144.0 3.9 %collective-permute-done.6.rest_10_ = bf16[3,128,512]{2,1,0:T(8,128)(2,1)} collective-permute-done((bf16[3,128,512]{2,1,0:T(8,128)(2,1)}, bf16[3,128,512]{2,1,0:T(8,128)(2,1)}, u32[]{:S(2)}, u32[]{:S(2)}) %collective-permute-start.6) | collective-permute-done | bytes 393248 | tf_op jit(solution)/shard_map/ppermute | solution.py:468
  147.9 1.6 copy-done.1
  152.0 15.0 %attend.2 = (bf16[512,128]{1,0:T(8,128)(2,1)S(1)}, bf16[512,128]{1,0:T(8,128)(2,1)}, bf16[512,128]{1,0:T(8,128)(2,1)}, bf16[512,128]{1,0:T(8,128)(2,1)}, bf16[51...) custom-call(s32[2]{0:T(128)S(1)} %copy-done.5, ...), custom_call_target="tpu_custom_call" | custom-call | flops 15000000512 | bytes 4000000 | tf_op jit(solution)/shard_map/attend/pallas_call | solution.py:371
  167.1 2.2 %collective-permute-start.11 = (bf16[512,128]{1,0:T(8,128)(2,1)S(1)}, bf16[512,128]{1,0:T(8,128)(2,1)S(1)}, u32[]{:S(2)}, u32[]{:S(2)}) collective-permute-start(bf16[512,128]{1,0:T(8,128)(2,1)S(1)} %get-tuple-element.33), channel_id=1, source_target_pairs={{0,20},{4,16},{8,28},{12,24},{16,4},{20,0},{24,12},{28,8},{1,21},{... | collective-permute-start | bytes 393224 | tf_op jit(solution)/shard_map/ppermute | solution.py:468
  169.3 4.7 %collective-permute-start.12 = (bf16[512,128]{1,0:T(8,128)(2,1)}, bf16[512,128]{1,0:T(8,128)(2,1)}, u32[]{:S(2)}, u32[]{:S(2)}) collective-permute-start(bf16[512,128]{1,0:T(8,128)(2,1)} %get-tuple-element.34), channel_id=1, source_target_pairs={{0,24},{4,28},{8,16},{12,20},{16,8},{20,12},{24,0},{28,4},{1,25},{... | collective-permute-start | bytes 393224 | tf_op jit(solution)/shard_map/ppermute | solution.py:468
  174.0 6.6 %collective-permute-done.10.rest_4_ = bf16[512,128]{1,0:T(8,128)(2,1)S(1)} collective-permute-done((bf16[512,128]{1,0:T(8,128)(2,1)S(1)}, bf16[512,128]{1,0:T(8,128)(2,1)S(1)}, u32[]{:S(2)}, u32[]{:S(2)}) %collective-permute-start.10) | collective-permute-done | bytes 131104 | tf_op jit(solution)/shard_map/ppermute | solution.py:468
  181.8 1.8 collective-permute-done.11.rest_5_
  183.6 3.6 %collective-permute-start.8 = (bf16[512,128]{1,0:T(8,128)(2,1)}, bf16[512,128]{1,0:T(8,128)(2,1)}, u32[]{:S(2)}, u32[]{:S(2)}) collective-permute-start(bf16[512,128]{1,0:T(8,128)(2,1)} %get-tuple-element.30), channel_id=1, source_target_pairs={{0,8},{4,12},{8,0},{12,4},{16,24},{20,28},{24,16},{28,20},{1,9},{5... | collective-permute-start | bytes 393224 | tf_op jit(solution)/shard_map/ppermute | solution.py:468
  188.0 5.2 %project.2.rest_12_ = f32[1,512,2048]{2,1,0:T(8,128)S(1)} custom-call(s32[2]{0:T(128)S(1)} %copy-done.5, bf16[8,512,128]{2,1,0:T(8,128)(2,1)S(1)} %all-to-all-done.1.rest_0_, bf16[2,2,128,2048]{3,2,1,0:T(8,128)(2,1)} %bitcast.8.rest_1_.rest_8_, bf16[2,2,128,2048]{3,2,1,0:T(8,128)(2,1)} %bitcast.9.rest_2_.rest_9_, ...), custom_call_target="tpu_custom_call" | custom-call | flops 2147483648 | bytes 10000000 | tf_op jit(solution)/shard_map/project/pallas_call | solution.py:428
  193.2 2.5 %collective-permute-done.9.rest_3_ = bf16[512,128]{1,0:T(8,128)(2,1)} collective-permute-done((bf16[512,128]{1,0:T(8,128)(2,1)}, bf16[512,128]{1,0:T(8,128)(2,1)}, u32[]{:S(2)}, u32[]{:S(2)}) %collective-permute-start.9) | collective-permute-done | bytes 131104 | tf_op jit(solution)/shard_map/ppermute | solution.py:468
  195.7 6.3 %project.3 = bf16[1,512,2048]{2,1,0:T(8,128)(2,1)} custom-call(s32[2]{0:T(128)S(1)} %copy-done.5, bf16[512,128]{1,0:T(8,128)(2,1)S(1)} %get-tuple-element.28.rest_0_, bf16[512,128]{1,0:T(8,128)(2,1)} %collective-permute-done.7.rest_1_, bf16[512,128]{1,0:T(8,128)(2,1)} %collective-permute-done.8.rest_2_, bf16[512,128]{1,0:T(8,128)(2,1)} %collective-permute-done.9.rest_3_, ...), custom_call_target="tpu_custom_call" | custom-call | flops 2147483648 | bytes 10000000 | tf_op jit(solution)/shard_map/project/pallas_call | solution.py:428
  (64 shorter events, 19.0 us)
Async XLA Ops:
  3.0 117.3 %all-to-all-start = ((bf16[8,3,128,512]{3,2,1,0:T(8,128)(2,1)}), bf16[8,3,128,512]{3,2,1,0:T(8,128)(2,1)S(1)}, u32[]{:S(2)}, u32[]{:S(2)}) async-start(bf16[8,3,128,512]{3,2,1,0:T(8,128)(2,1)} %cut.1), calls=%async_computation | async-start | bytes 6291456 | tf_op jit(solution)/shard_map/all_to_all | solution.py:465
  10.0 43.4 %copy-start.9 = (s32[1,4,64,3]{2,1,3,0:T(4,128)S(1)}, s32[1,4,64,3]{2,1,3,0:T(4,128)}, u32[]{:S(2)}) copy-start(s32[1,4,64,3]{2,1,3,0:T(4,128)} %param.9) | copy-start | bytes 9220
  10.0 43.4 %copy-start.8 = (s32[1,2]{1,0:T(1,128)S(1)}, s32[1,2]{1,0:T(1,128)}, u32[]{:S(2)}) copy-start(s32[1,2]{1,0:T(1,128)} %param.10) | copy-start | bytes 28
  13.6 106.7 %copy-start.5 = (s32[2]{0:T(128)S(1)}, s32[2]{0:T(128)}, u32[]{:S(2)}) copy-start(s32[2]{0:T(128)} %pad_add_fusion.3.me_ref) | copy-start | bytes 28
  13.6 29.4 %collective-permute-start = (bf16[3,128,512]{2,1,0:T(8,128)(2,1)}, bf16[3,128,512]{2,1,0:T(8,128)(2,1)S(1)}, u32[]{:S(2)}, u32[]{:S(2)}) collective-permute-start(bf16[3,128,512]{2,1,0:T(8,128)(2,1)} %get-tuple-element.21), channel_id=1, source_target_pairs={{0,4},{4,0},{8,12},{12,8},{16,20},{20,16},{24,28},{28,24},{1,5},{5... | collective-permute-start | bytes 1179656 | tf_op jit(solution)/shard_map/ppermute | solution.py:468
  43.7 76.1 %collective-permute-start.15 = (bf16[512,2048]{1,0:T(8,128)(2,1)}, bf16[512,2048]{1,0:T(8,128)(2,1)}, u32[]{:S(2)}, u32[]{:S(2)}) collective-permute-start(bf16[512,2048]{1,0:T(8,128)(2,1)} %param.11), channel_id=1, source_target_pairs={{0,2},{1,3},{2,0},{3,1},{4,6},{5,7},{6,4},{7,5},{8,10},{9,11},{10,... | collective-permute-start | bytes 6291464 | tf_op jit(solution)/shard_map/ppermute | solution.py:451
  45.2 26.0 %collective-permute-start.1 = (bf16[3,128,512]{2,1,0:T(8,128)(2,1)}, bf16[3,128,512]{2,1,0:T(8,128)(2,1)}, u32[]{:S(2)}, u32[]{:S(2)}) collective-permute-start(bf16[3,128,512]{2,1,0:T(8,128)(2,1)} %get-tuple-element.22), channel_id=1, source_target_pairs={{0,8},{4,12},{8,0},{12,4},{16,24},{20,28},{24,16},{28,20},{1,9},{5... | collective-permute-start | bytes 1179656 | tf_op jit(solution)/shard_map/ppermute | solution.py:468
  46.8 34.2 %collective-permute-start.2 = (bf16[3,128,512]{2,1,0:T(8,128)(2,1)}, bf16[3,128,512]{2,1,0:T(8,128)(2,1)}, u32[]{:S(2)}, u32[]{:S(2)}) collective-permute-start(bf16[3,128,512]{2,1,0:T(8,128)(2,1)} %get-tuple-element.23), channel_id=1, source_target_pairs={{0,12},{4,8},{8,4},{12,0},{16,28},{20,24},{24,20},{28,16},{1,13},{... | collective-permute-start | bytes 1179656 | tf_op jit(solution)/shard_map/ppermute | solution.py:468
  49.1 70.8 %collective-permute-start.3 = (bf16[3,128,512]{2,1,0:T(8,128)(2,1)}, bf16[3,128,512]{2,1,0:T(8,128)(2,1)}, u32[]{:S(2)}, u32[]{:S(2)}) collective-permute-start(bf16[3,128,512]{2,1,0:T(8,128)(2,1)} %get-tuple-element.24), channel_id=1, source_target_pairs={{0,16},{4,20},{8,24},{12,28},{16,0},{20,4},{24,8},{28,12},{1,17},{... | collective-permute-start | bytes 1179656 | tf_op jit(solution)/shard_map/ppermute | solution.py:468
  51.2 92.8 %collective-permute-start.4 = (bf16[3,128,512]{2,1,0:T(8,128)(2,1)}, bf16[3,128,512]{2,1,0:T(8,128)(2,1)}, u32[]{:S(2)}, u32[]{:S(2)}) collective-permute-start(bf16[3,128,512]{2,1,0:T(8,128)(2,1)} %get-tuple-element.25), channel_id=1, source_target_pairs={{0,20},{4,16},{8,28},{12,24},{16,4},{20,0},{24,12},{28,8},{1,21},{... | collective-permute-start | bytes 1179656 | tf_op jit(solution)/shard_map/ppermute | solution.py:468
  71.3 72.7 %collective-permute-start.5 = (bf16[3,128,512]{2,1,0:T(8,128)(2,1)}, bf16[3,128,512]{2,1,0:T(8,128)(2,1)}, u32[]{:S(2)}, u32[]{:S(2)}) collective-permute-start(bf16[3,128,512]{2,1,0:T(8,128)(2,1)} %get-tuple-element.26), channel_id=1, source_target_pairs={{0,24},{4,28},{8,16},{12,20},{16,8},{20,12},{24,0},{28,4},{1,25},{... | collective-permute-start | bytes 1179656 | tf_op jit(solution)/shard_map/ppermute | solution.py:468
  81.0 66.9 %collective-permute-start.6 = (bf16[3,128,512]{2,1,0:T(8,128)(2,1)}, bf16[3,128,512]{2,1,0:T(8,128)(2,1)}, u32[]{:S(2)}, u32[]{:S(2)}) collective-permute-start(bf16[3,128,512]{2,1,0:T(8,128)(2,1)} %get-tuple-element.27), channel_id=1, source_target_pairs={{0,28},{4,24},{8,20},{12,16},{16,12},{20,8},{24,4},{28,0},{1,29},{... | collective-permute-start | bytes 1179656 | tf_op jit(solution)/shard_map/ppermute | solution.py:468
  119.8 63.8 %collective-permute-start.14 = (bf16[512,2048]{1,0:T(8,128)(2,1)}, bf16[512,2048]{1,0:T(8,128)(2,1)}, u32[]{:S(2)}, u32[]{:S(2)}) collective-permute-start(bf16[512,2048]{1,0:T(8,128)(2,1)} %param.11), channel_id=1, source_target_pairs={{0,1},{1,0},{2,3},{3,2},{4,5},{5,4},{6,7},{7,6},{8,9},{9,8},{10,11... | collective-permute-start | bytes 6291464 | tf_op jit(solution)/shard_map/ppermute | solution.py:451
  119.8 67.4 %collective-permute-start.16 = (bf16[512,2048]{1,0:T(8,128)(2,1)}, bf16[512,2048]{1,0:T(8,128)(2,1)}, u32[]{:S(2)}, u32[]{:S(2)}) collective-permute-start(bf16[512,2048]{1,0:T(8,128)(2,1)} %collective-permute-done.15), channel_id=1, source_target_pairs={{0,1},{1,0},{2,3},{3,2},{4,5},{5,4},{6,7},{7,6},{8,9},{9,8},{10,11... | collective-permute-start | bytes 6291464 | tf_op jit(solution)/shard_map/ppermute | solution.py:451
  136.1 11.7 %copy-start = (bf16[1,2048,512]{2,1,0:T(8,128)(2,1)S(1)}, bf16[1,2048,512]{2,1,0:T(8,128)(2,1)}, u32[]{:S(2)}) copy-start(bf16[1,2048,512]{2,1,0:T(8,128)(2,1)} %q_ref.3) | copy-start | bytes 6291460
  136.2 51.9 %all-to-all-start.1 = ((bf16[8,512,128]{2,1,0:T(8,128)(2,1)}), bf16[8,512,128]{2,1,0:T(8,128)(2,1)S(1)}, u32[]{:S(2)}, u32[]{:S(2)}) async-start(bf16[8,512,128]{2,1,0:T(8,128)(2,1)} %copy-done.3), calls=%async_computation.1 | async-start | bytes 2097152 | tf_op jit(solution)/shard_map/all_to_all | solution.py:465
  147.9 1.6 copy-start.1
  167.1 13.6 %collective-permute-start.10 = (bf16[512,128]{1,0:T(8,128)(2,1)S(1)}, bf16[512,128]{1,0:T(8,128)(2,1)S(1)}, u32[]{:S(2)}, u32[]{:S(2)}) collective-permute-start(bf16[512,128]{1,0:T(8,128)(2,1)S(1)} %get-tuple-element.32), channel_id=1, source_target_pairs={{0,16},{4,20},{8,24},{12,28},{16,0},{20,4},{24,8},{28,12},{1,17},{... | collective-permute-start | bytes 393224 | tf_op jit(solution)/shard_map/ppermute | solution.py:468
  167.1 16.4 %collective-permute-start.11 = (bf16[512,128]{1,0:T(8,128)(2,1)S(1)}, bf16[512,128]{1,0:T(8,128)(2,1)S(1)}, u32[]{:S(2)}, u32[]{:S(2)}) collective-permute-start(bf16[512,128]{1,0:T(8,128)(2,1)S(1)} %get-tuple-element.33), channel_id=1, source_target_pairs={{0,20},{4,16},{8,28},{12,24},{16,4},{20,0},{24,12},{28,8},{1,21},{... | collective-permute-start | bytes 393224 | tf_op jit(solution)/shard_map/ppermute | solution.py:468
  169.3 23.9 %collective-permute-start.12 = (bf16[512,128]{1,0:T(8,128)(2,1)}, bf16[512,128]{1,0:T(8,128)(2,1)}, u32[]{:S(2)}, u32[]{:S(2)}) collective-permute-start(bf16[512,128]{1,0:T(8,128)(2,1)} %get-tuple-element.34), channel_id=1, source_target_pairs={{0,24},{4,28},{8,16},{12,20},{16,8},{20,12},{24,0},{28,4},{1,25},{... | collective-permute-start | bytes 393224 | tf_op jit(solution)/shard_map/ppermute | solution.py:468
  180.6 12.6 %collective-permute-start.13 = (bf16[512,128]{1,0:T(8,128)(2,1)}, bf16[512,128]{1,0:T(8,128)(2,1)}, u32[]{:S(2)}, u32[]{:S(2)}) collective-permute-start(bf16[512,128]{1,0:T(8,128)(2,1)} %get-tuple-element.35), channel_id=1, source_target_pairs={{0,28},{4,24},{8,20},{12,16},{16,12},{20,8},{24,4},{28,0},{1,29},{... | collective-permute-start | bytes 393224 | tf_op jit(solution)/shard_map/ppermute | solution.py:468
  183.5 9.7 %collective-permute-start.7 = (bf16[512,128]{1,0:T(8,128)(2,1)}, bf16[512,128]{1,0:T(8,128)(2,1)}, u32[]{:S(2)}, u32[]{:S(2)}) collective-permute-start(bf16[512,128]{1,0:T(8,128)(2,1)} %get-tuple-element.29), channel_id=1, source_target_pairs={{0,4},{4,0},{8,12},{12,8},{16,20},{20,16},{24,28},{28,24},{1,5},{5... | collective-permute-start | bytes 393224 | tf_op jit(solution)/shard_map/ppermute | solution.py:468
  183.6 9.6 %collective-permute-start.8 = (bf16[512,128]{1,0:T(8,128)(2,1)}, bf16[512,128]{1,0:T(8,128)(2,1)}, u32[]{:S(2)}, u32[]{:S(2)}) collective-permute-start(bf16[512,128]{1,0:T(8,128)(2,1)} %get-tuple-element.30), channel_id=1, source_target_pairs={{0,8},{4,12},{8,0},{12,4},{16,24},{20,28},{24,16},{28,20},{1,9},{5... | collective-permute-start | bytes 393224 | tf_op jit(solution)/shard_map/ppermute | solution.py:468
  187.2 8.5 %collective-permute-start.9 = (bf16[512,128]{1,0:T(8,128)(2,1)}, bf16[512,128]{1,0:T(8,128)(2,1)}, u32[]{:S(2)}, u32[]{:S(2)}) collective-permute-start(bf16[512,128]{1,0:T(8,128)(2,1)} %get-tuple-element.31), channel_id=1, source_target_pairs={{0,12},{4,8},{8,4},{12,0},{16,28},{20,24},{24,20},{28,16},{1,13},{... | collective-permute-start | bytes 393224 | tf_op jit(solution)/shard_map/ppermute | solution.py:468
  (5 other events, 5.3 us)

commit v4 on v3

--- a/solution.py
+++ b/solution.py
@@ -13,8 +13,6 @@
 PAIR = 2 * HD
 EXP_SCALE = HD ** (-0.5) * math.log2(math.e)
 BIG = 1e30
-APART_IN = (False, True)
-APART_OUT = (False, True)
 
 
 def candidate_blocks(nblocks, glob, rand_h):
@@ -132,7 +130,7 @@
 def cut(n, row, queries, keys, values):
     feats = queries.shape[1] // n
     length = queries.shape[2]
-    hbm = pl.BlockSpec(memory_space=pl.ANY)
+    hbm = pl.BlockSpec(memory_space=pltpu.HBM)
     return pl.pallas_call(
         functools.partial(cut_kernel, n, feats, row),
         out_shape=jax.ShapeDtypeStruct((n, 3, PAIR, length), queries.dtype),
@@ -148,45 +146,44 @@
 
 
 def cut_apart_kernel(n, feats, row, me_ref, q_ref, k_ref, v_ref, *rest):
-    outs = rest[: n - 1]
-    held, in_sems, out_sems = rest[n - 1 :]
+    outs = rest[:n]
+    held, in_sems, out_sems = rest[n:]
     me = me_ref[0]
-    order = range(n - 1, 0, -1)
 
     def read(k, i):
         start = pl.multiple_of((me ^ k) * feats + row, PAIR)
         src = (q_ref, k_ref, v_ref)[i]
         return pltpu.make_async_copy(
-            src.at[0, pl.ds(start, PAIR), :], held.at[k - 1, i], in_sems.at[k - 1, i]
+            src.at[0, pl.ds(start, PAIR), :], held.at[k, i], in_sems.at[k, i]
         )
 
     def write(k):
-        return pltpu.make_async_copy(held.at[k - 1], outs[k - 1], out_sems.at[k - 1])
-
-    for k in order:
+        return pltpu.make_async_copy(held.at[k], outs[k], out_sems.at[k])
+
+    for k in range(n):
         for i in range(3):
             read(k, i).start()
-    for k in order:
+    for k in range(n):
         for i in range(3):
             read(k, i).wait()
         write(k).start()
-    for k in order:
+    for k in range(n):
         write(k).wait()
 
 
 def cut_apart(n, row, me, queries, keys, values):
     feats = queries.shape[1] // n
     length = queries.shape[2]
-    hbm = pl.BlockSpec(memory_space=pl.ANY)
+    hbm = pl.BlockSpec(memory_space=pltpu.HBM)
     return pl.pallas_call(
         functools.partial(cut_apart_kernel, n, feats, row),
-        out_shape=[jax.ShapeDtypeStruct((3, PAIR, length), queries.dtype)] * (n - 1),
+        out_shape=[jax.ShapeDtypeStruct((3, PAIR, length), queries.dtype)] * n,
         in_specs=[pl.BlockSpec(memory_space=pltpu.SMEM), hbm, hbm, hbm],
-        out_specs=[hbm] * (n - 1),
+        out_specs=[hbm] * n,
         scratch_shapes=[
-            pltpu.VMEM((n - 1, 3, PAIR, length), queries.dtype),
-            pltpu.SemaphoreType.DMA((n - 1, 3)),
-            pltpu.SemaphoreType.DMA((n - 1,)),
+            pltpu.VMEM((n, 3, PAIR, length), queries.dtype),
+            pltpu.SemaphoreType.DMA((n, 3)),
+            pltpu.SemaphoreType.DMA((n,)),
         ],
         name="cut_apart",
     )(me, queries, keys, values)
@@ -196,48 +193,27 @@
     return jnp.concatenate([x[:, BLK:], x[:, :BLK]], axis=1)
 
 
-def attend_kernel(n, nblocks, feats, row, apart_in, apart_out, me_ref, rand_ref, glob_ref, *rest):
+def attend_kernel(n, nblocks, apart_in, apart_out, me_ref, rand_ref, glob_ref, *rest):
     pen_ref, rest = rest[0], rest[1:]
-    ins, rest = (rest[: n + 2], rest[n + 2 :]) if apart_in else (rest[:1], rest[1:])
+    ins, rest = (rest[:n], rest[n:]) if apart_in else (rest[:1], rest[1:])
     outs, rest = (rest[:n], rest[n:]) if apart_out else (rest[:1], rest[1:])
-    raw, kt, vv, ob, sg, own_sems, in_sems, out_sems = rest
+    raw, kt, vv, ob, sg, in_sems, out_sems = rest
     me = me_ref[0]
     shard = raw.shape[3]
     per = shard // BLK
     tiles = shard // PAIR
     f32, bf16 = jnp.float32, jnp.bfloat16
 
+    shards = [me ^ k for k in range(n)] if apart_in else list(range(n))
     arrivals = []
-    if apart_in:
-        own = pl.multiple_of(me * feats + row, PAIR)
-        arrivals.append(
-            (
-                me,
-                [
-                    pltpu.make_async_copy(
-                        ins[i].at[0, pl.ds(own, PAIR), :], raw.at[me, i], own_sems.at[i]
-                    )
-                    for i in range(3)
-                ],
-            )
-        )
-        for k in range(1, n):
-            came = me ^ k
-            arrivals.append(
-                (came, [pltpu.make_async_copy(ins[2 + k], raw.at[came], in_sems.at[k])])
-            )
-    else:
-        for s in range(n):
-            arrivals.append(
-                (s, [pltpu.make_async_copy(ins[0].at[s], raw.at[s], in_sems.at[s])])
-            )
-    for _, copies in arrivals:
-        for copy in copies:
-            copy.start()
-
-    for s, copies in arrivals:
-        for copy in copies:
-            copy.wait()
+    for i, s in enumerate(shards):
+        src = ins[i] if apart_in else ins[0].at[i]
+        arrivals.append(pltpu.make_async_copy(src, raw.at[s], in_sems.at[i]))
+    for copy in arrivals:
+        copy.start()
+
+    for s, copy in zip(shards, arrivals):
+        copy.wait()
         for t in range(tiles):
             lanes = slice(t * PAIR, (t + 1) * PAIR)
             first = pl.multiple_of(s * shard + t * PAIR, PAIR)
@@ -356,12 +332,12 @@
         copy.wait()
 
 
-def attend(n, row, me, rand, glob, pen, arrays, feats, apart_out):
+def attend(n, me, rand, glob, pen, arrays, apart_out):
     apart_in = len(arrays) > 1
     shard = arrays[0].shape[-1]
     length = n * shard
     nblocks = length // BLK
-    hbm = pl.BlockSpec(memory_space=pl.ANY)
+    hbm = pl.BlockSpec(memory_space=pltpu.HBM)
     smem = pl.BlockSpec(memory_space=pltpu.SMEM)
     vmem = pl.BlockSpec(memory_space=pltpu.VMEM)
     if apart_out:
@@ -369,7 +345,7 @@
     else:
         out_shape = [jax.ShapeDtypeStruct((n, shard, PAIR), jnp.bfloat16)]
     return pl.pallas_call(
-        functools.partial(attend_kernel, n, nblocks, feats, row, apart_in, apart_out),
+        functools.partial(attend_kernel, n, nblocks, apart_in, apart_out),
         out_shape=out_shape,
         in_specs=[smem, smem, smem, vmem] + [hbm] * len(arrays),
         out_specs=[hbm] * len(out_shape),
@@ -379,11 +355,10 @@
             pltpu.VMEM((2, nblocks // 2, PAIR, PAIR), jnp.bfloat16),
             pltpu.VMEM((n, shard, PAIR), jnp.bfloat16),
             pltpu.VMEM((length, 2 * PAIR), jnp.float32),
-            pltpu.SemaphoreType.DMA((3,)),
             pltpu.SemaphoreType.DMA((n,)),
             pltpu.SemaphoreType.DMA((n,)),
         ],
-        compiler_params=pltpu.CompilerParams(vmem_limit_bytes=32 * 1024 * 1024),
+        compiler_params=pltpu.CompilerParams(vmem_limit_bytes=60 * 1024 * 1024),
         cost_estimate=pl.CostEstimate(
             flops=15_000_000_000, bytes_accessed=4_000_000, transcendentals=0
         ),
@@ -391,56 +366,93 @@
     )(me, rand, glob, pen, *arrays)
 
 
-def project_kernel(n, ndp, count, before, me_ref, *rest):
-    pieces, rest = rest[:count], rest[count:]
+def project_kernel(n, ndp, slots, before, me_ref, *rest):
+    arrays = sorted({i for i, _, _ in slots})
+    pieces, rest = rest[: len(arrays)], rest[len(arrays) :]
     weights, rest = rest[:ndp], rest[ndp:]
-    o_ref, a = rest[-2], rest[-1]
+    if before:
+        before_ref, rest = rest[0], rest[1:]
+        acc, rest = rest[1], rest[:1] + rest[2:]
+    o_ref, a, w, a_sems, w_sems, acc_sems = rest
+    me, dp = me_ref[0], me_ref[1]
     held = n // ndp
-
-    @pl.when(pl.program_id(0) == 0)
-    def _():
-        if count == 1:
-            for r in range(ndp):
-                for u in range(held):
-                    first = (r * held + u) * PAIR
-                    a[:, first : first + PAIR] = pieces[0][(me_ref[1] ^ r) * held + u]
-        else:
-            for k in range(n):
-                came = me_ref[0] ^ k
-                place = (lax.div(came, held) ^ me_ref[1]) * held + lax.rem(came, held)
-                a[:, pl.ds(pl.multiple_of(place * PAIR, PAIR), PAIR)] = pieces[k][...]
-
-    w = jnp.concatenate([w_ref[...].reshape(held * PAIR, -1) for w_ref in weights], axis=0)
-    total = jnp.dot(a[...], w, preferred_element_type=jnp.float32)
+    feats = weights[0].shape[0] // held
+    width = weights[0].shape[1]
+    tile = width // 4
+
+    def piece_copy(slot):
+        i, _, k = slots[slot]
+        src = pieces[arrays.index(i)]
+        src = src.at[me ^ k] if len(src.shape) == 3 else src
+        dst = a.at[:, pl.ds(slot * PAIR, PAIR)]
+        return pltpu.make_async_copy(src, dst, a_sems.at[slot])
+
+    def weight_copy(slot, part):
+        _, p, k = slots[slot]
+        row = pl.multiple_of(lax.rem(me ^ k, held) * feats + p * PAIR, PAIR)
+        dst = w.at[pl.ds(slot * PAIR, PAIR), :]
+        return pltpu.make_async_copy(weights[part].at[pl.ds(row, PAIR), :], dst, w_sems.at[slot])
+
+    def acc_copy(t):
+        columns = pl.ds(t * tile, tile)
+        return pltpu.make_async_copy(
+            before_ref.at[0, :, columns], acc.at[:, columns], acc_sems.at[t]
+        )
+
+    every = range(len(slots))
+    for slot in every:
+        piece_copy(slot).start()
+    own = lax.div(me, held) ^ dp
+    for r in range(ndp):
+
+        @pl.when(own == r)
+        def _():
+            for slot in every:
+                weight_copy(slot, r ^ (slots[slot][2] // held)).start()
+
     if before:
-        total = total + rest[0][0]
-    o_ref[0] = total.astype(o_ref.dtype)
-
-
-def project(n, p, me, pieces, weights, before, dtype):
+        for t in range(4):
+            acc_copy(t).start()
+    for slot in every:
+        piece_copy(slot).wait()
+    for slot in every:
+        weight_copy(slot, 0).wait()
+    for t in range(4):
+        columns = slice(t * tile, (t + 1) * tile)
+        total = jnp.dot(a[...], w[:, columns], preferred_element_type=jnp.float32)
+        if before:
+            acc_copy(t).wait()
+            total = total + acc[:, columns]
+        o_ref[0, :, columns] = total.astype(o_ref.dtype)
+
+
+def project(n, me, pieces, slots, weights, before, dtype):
     shard = pieces[0].shape[-2]
     ndp = len(weights)
-    depth, width = weights[0].shape
-    held = n // ndp
-    tile = 512
-    rows = [w.reshape(held, depth // held // PAIR, PAIR, width) for w in weights]
-    column = pl.BlockSpec((1, shard, tile), lambda i: (0, 0, i))
+    width = weights[0].shape[1]
+    depth = len(slots) * PAIR
+    hbm = pl.BlockSpec(memory_space=pl.ANY)
+    more = [] if before is None else [before]
     return pl.pallas_call(
-        functools.partial(project_kernel, n, ndp, len(pieces), before is not None),
-        grid=(width // tile,),
+        functools.partial(project_kernel, n, ndp, slots, before is not None),
         out_shape=jax.ShapeDtypeStruct((1, shard, width), dtype),
         in_specs=[pl.BlockSpec(memory_space=pltpu.SMEM)]
-        + [pl.BlockSpec(x.shape, lambda i, r=x.ndim: (0,) * r) for x in pieces]
-        + [pl.BlockSpec((held, None, PAIR, tile), lambda i: (0, p, 0, i))] * ndp
-        + ([] if before is None else [column]),
-        out_specs=column,
-        scratch_shapes=[pltpu.VMEM((shard, n * PAIR), jnp.bfloat16)],
+        + [hbm] * (len(pieces) + ndp + len(more)),
+        out_specs=pl.BlockSpec(memory_space=pltpu.VMEM),
+        scratch_shapes=[pltpu.VMEM((shard, width), jnp.float32)] * len(more)
+        + [
+            pltpu.VMEM((shard, depth), jnp.bfloat16),
+            pltpu.VMEM((depth, width), jnp.bfloat16),
+            pltpu.SemaphoreType.DMA((len(slots),)),
+            pltpu.SemaphoreType.DMA((len(slots),)),
+            pltpu.SemaphoreType.DMA((4,)),
+        ],
         compiler_params=pltpu.CompilerParams(vmem_limit_bytes=24 * 1024 * 1024),
         cost_estimate=pl.CostEstimate(
-            flops=2 * shard * n * PAIR * width, bytes_accessed=10_000_000, transcendentals=0
+            flops=2 * shard * depth * width, bytes_accessed=10_000_000, transcendentals=0
         ),
         name="project",
-    )(me, *pieces, *rows, *([] if before is None else [before]))
+    )(me, *pieces, *weights, *more)
 
 
 def gather_weight(ndp, weight):
@@ -465,8 +477,8 @@
         return lax.all_to_all(x, "seq", split_axis=0, concat_axis=0, tiled=True)
 
     def swap(arrays, order):
-        got = {k: lax.ppermute(arrays[k - 1], "seq", [(i, i ^ k) for i in range(n)]) for k in order}
-        return [got[k] for k in range(1, n)]
+        got = {k: lax.ppermute(arrays[k], "seq", [(i, i ^ k) for i in range(n)]) for k in order}
+        return [arrays[0]] + [got[k] for k in range(1, n)]
 
     near, far = list(range(1, n // 2)), list(range(n // 2, n))
 
@@ -475,25 +487,24 @@
     pen = jnp.transpose(pen.reshape(pairs, 2, nblocks, -1), (0, 2, 3, 1))
     rand = random_blocks[0].reshape(pairs, -1)
 
-    arrived = []
-    for p in range(pairs):
-        if APART_IN[p % 2]:
-            sent = cut_apart(n, p * PAIR, me, queries, keys, values)
-            arrived.append([queries, keys, values] + swap(sent, near + far))
-        else:
-            arrived.append([exchange(cut(n, p * PAIR, queries, keys, values))])
-    weights = gather_weight(ndp, lax.optimization_barrier((out_weight, arrived[1][3]))[0])
-    total = None
-    for p in range(pairs):
-        apart = APART_OUT[p % 2]
-        outs = attend(n, p * PAIR, me, rand[p], glob, pen[p], arrived[p], feats, apart)
-        if apart:
-            pieces = [outs[0]] + swap(outs[1:], far + near)
-        else:
-            pieces = [exchange(outs[0])]
-        dtype = jnp.bfloat16 if p == pairs - 1 else jnp.float32
-        total = project(n, p, me, pieces, weights, total, dtype)
-    return total
+    last = pairs - 1
+    arrived = [exchange(cut(n, p * PAIR, queries, keys, values)) for p in range(last)]
+    messages = swap(cut_apart(n, last * PAIR, me, queries, keys, values), near + far)
+    weights = gather_weight(ndp, lax.optimization_barrier((out_weight, messages[1]))[0])
+
+    pieces, slots = [], []
+    for p in range(last):
+        outs = attend(n, me, rand[p], glob, pen[p], [arrived[p]], False)
+        pieces.append(exchange(outs[0]))
+        slots += [(p, p, k) for k in range(n)]
+    outs = attend(n, me, rand[last], glob, pen[last], messages, True)
+    outs, weights = lax.optimization_barrier((list(outs), weights))
+    results = swap(outs, far + near)
+    pieces += [results[k] for k in [0] + near]
+    slots += [(last + i, last, k) for i, k in enumerate([0] + near)]
+    total = project(n, me, pieces, slots, weights, None, jnp.float32)
+    slots = [(i, last, k) for i, k in enumerate(far)]
+    return project(n, me, [results[k] for k in far], slots, weights, total, jnp.bfloat16)
 
 
 def solution(mesh):

time: 205 us -> 201 us (0.980); the launches traced: 202 us -> 200 us
  starting transfers between devices: 41.5 us -> 38.5 us
    ppermute x14, starting transfers between devices: 25.7 us -> 22.9 us  [swap(): lax.ppermute(arrays[k], 'seq', [(i, i ^ k) for i in range(n)])]
    unnamed x20 -> x28, local copies, waits for them, and re-layouts: 6.86 us -> 5.61 us
  transfers between devices with their start and end apart: 19 -> 19, of which waited for: 8 -> 10; matrix products, arithmetic and copies ran while one was open for 2% -> 2% of each run, Pallas kernels for 19% -> 20%
where the time goes in v4:
time: 201 us; the launch traced here: 200 us
  waiting for transfers between devices  103 us (51%)
  Pallas kernels  48.3 us (24%)
  starting transfers between devices  38.5 us (19%)
  local copies, waits for them, and re-layouts  9.27 us (5%)
    ppermute x14, waiting for transfers between devices, swap(): lax.ppermute(arrays[k], 'seq', [(i, i ^ k) for i in range(n)])  103 us
    pallas_call x2, Pallas kernels, attend(): pl.pallas_call(functools.partial(attend_kernel, n, nblocks, apart_in, apa...  29.3 us
    ppermute x14, starting transfers between devices, swap(): lax.ppermute(arrays[k], 'seq', [(i, i ^ k) for i in range(n)])  22.9 us
    all_to_all x2, starting transfers between devices, exchange(): return lax.all_to_all(x, 'seq', split_axis=0, concat_axis=0, tiled=True)  13.7 us
    pallas_call x2, Pallas kernels, project(): pl.pallas_call(functools.partial(project_kernel, n, ndp, slots, before is...  12.1 us
    unnamed x28, local copies, waits for them, and re-layouts  5.61 us
  transfers between devices with their start and end apart: 19, of which 10 were waited for; matrix products, arithmetic and copies ran while one was open for 2% of the time, Pallas kernels for 20%

profile of v4, /device:TPU:8, one launch (start us, length us, event | category | flops | bytes accessed | tf_op | source)
XLA Modules:
  0.0 200.4 jit_solution(5274594843574079128)
XLA Ops:
  0.0 3.1 %cut.1 = bf16[8,3,128,512]{3,2,1,0:T(8,128)(2,1)} custom-call(bf16[1,2048,512]{2,1,0:T(8,128)(2,1)} %q_ref.3, bf16[1,2048,512]{2,1,0:T(8,128)(2,1)} %k_ref.3, bf16[1,2048,512]{2,1,0:T(8,128)(2,1)} %v_ref.3), custom_call_target="tpu_custom_call" | custom-call | tf_op jit(solution)/shard_map/cut/pallas_call | solution.py:134
  3.1 6.3 %all-to-all-start = ((bf16[8,3,128,512]{3,2,1,0:T(8,128)(2,1)}), bf16[8,3,128,512]{3,2,1,0:T(8,128)(2,1)}, u32[]{:S(2)}, u32[]{:S(2)}) async-start(bf16[8,3,128,512]{3,2,1,0:T(8,128)(2,1)} %cut.1), calls=%async_computation | async-start | bytes 6291456 | tf_op jit(solution)/shard_map/all_to_all | solution.py:477
  10.0 3.8 %cut_apart.1 = (bf16[3,128,512]{2,1,0:T(8,128)(2,1)}, bf16[3,128,512]{2,1,0:T(8,128)(2,1)}, bf16[3,128,512]{2,1,0:T(8,128)(2,1)}, bf16[3,128,512]{2,1,0:T(8,128)...) custom-call(s32[2]{0:T(128)} %pad_add_fusion.3.me_ref, ...), custom_call_target="tpu_custom_call" | custom-call | tf_op jit(solution)/shard_map/cut_apart/pallas_call | solution.py:178
  13.8 1.5 collective-permute-start
  15.3 27.7 %collective-permute-done.rest_2_ = bf16[3,128,512]{2,1,0:T(8,128)(2,1)S(1)} collective-permute-done((bf16[3,128,512]{2,1,0:T(8,128)(2,1)}, bf16[3,128,512]{2,1,0:T(8,128)(2,1)S(1)}, u32[]{:S(2)}, u32[]{:S(2)}) %collective-permute-start) | collective-permute-done | bytes 393248 | tf_op jit(solution)/shard_map/ppermute | solution.py:480
  46.1 2.3 %collective-permute-start.2 = (bf16[3,128,512]{2,1,0:T(8,128)(2,1)}, bf16[3,128,512]{2,1,0:T(8,128)(2,1)S(1)}, u32[]{:S(2)}, u32[]{:S(2)}) collective-permute-start(bf16[3,128,512]{2,1,0:T(8,128)(2,1)} %get-tuple-element.37), channel_id=1, source_target_pairs={{0,12},{4,8},{8,4},{12,0},{16,28},{20,24},{24,20},{28,16},{1,13},{... | collective-permute-start | bytes 1179656 | tf_op jit(solution)/shard_map/ppermute | solution.py:480
  48.4 2.1 %collective-permute-start.3 = (bf16[3,128,512]{2,1,0:T(8,128)(2,1)}, bf16[3,128,512]{2,1,0:T(8,128)(2,1)}, u32[]{:S(2)}, u32[]{:S(2)}) collective-permute-start(bf16[3,128,512]{2,1,0:T(8,128)(2,1)} %get-tuple-element.38), channel_id=1, source_target_pairs={{0,16},{4,20},{8,24},{12,28},{16,0},{20,4},{24,8},{28,12},{1,17},{... | collective-permute-start | bytes 1179656 | tf_op jit(solution)/shard_map/ppermute | solution.py:480
  50.5 2.2 %collective-permute-start.4 = (bf16[3,128,512]{2,1,0:T(8,128)(2,1)}, bf16[3,128,512]{2,1,0:T(8,128)(2,1)}, u32[]{:S(2)}, u32[]{:S(2)}) collective-permute-start(bf16[3,128,512]{2,1,0:T(8,128)(2,1)} %get-tuple-element.39), channel_id=1, source_target_pairs={{0,20},{4,16},{8,28},{12,24},{16,4},{20,0},{24,12},{28,8},{1,21},{... | collective-permute-start | bytes 1179656 | tf_op jit(solution)/shard_map/ppermute | solution.py:480
  55.9 15.3 %collective-permute-done.1.rest_3_ = bf16[3,128,512]{2,1,0:T(8,128)(2,1)S(1)} collective-permute-done((bf16[3,128,512]{2,1,0:T(8,128)(2,1)}, bf16[3,128,512]{2,1,0:T(8,128)(2,1)S(1)}, u32[]{:S(2)}, u32[]{:S(2)}) %collective-permute-start.1) | collective-permute-done | bytes 393248 | tf_op jit(solution)/shard_map/ppermute | solution.py:480
  71.2 1.9 collective-permute-start.5
  73.2 7.8 %collective-permute-done.2.rest_4_ = bf16[3,128,512]{2,1,0:T(8,128)(2,1)S(1)} collective-permute-done((bf16[3,128,512]{2,1,0:T(8,128)(2,1)}, bf16[3,128,512]{2,1,0:T(8,128)(2,1)S(1)}, u32[]{:S(2)}, u32[]{:S(2)}) %collective-permute-start.2) | collective-permute-done | bytes 393248 | tf_op jit(solution)/shard_map/ppermute | solution.py:480
  80.9 1.6 collective-permute-start.6
  82.5 37.4 %collective-permute-done.3.rest_5_ = bf16[3,128,512]{2,1,0:T(8,128)(2,1)} collective-permute-done((bf16[3,128,512]{2,1,0:T(8,128)(2,1)}, bf16[3,128,512]{2,1,0:T(8,128)(2,1)}, u32[]{:S(2)}, u32[]{:S(2)}) %collective-permute-start.3) | collective-permute-done | bytes 393248 | tf_op jit(solution)/shard_map/ppermute | solution.py:480
  120.4 14.6 %attend.3 = bf16[8,512,128]{2,1,0:T(8,128)(2,1)} custom-call(s32[2]{0:T(128)} %pad_add_fusion.3.me_ref, s32[384]{0:T(512)} %squeeze.22.rand_ref, s32[2]{0:T(128)} %bitcast.19, f32[64,8,2]{2,1,0:T(8,128)} %get-tuple-element.63.rest_0_, bf16[8,3,128,512]{3,2,1,0:T(8,128)(2,1)} %all-to-all-done.rest_1_), custom_call_target="tpu_custom_call" | custom-call | flops 15000000512 | bytes 4000000 | tf_op jit(solution)/shard_map/attend/pallas_call | solution.py:347
  135.1 7.4 %all-to-all-start.1 = ((bf16[8,512,128]{2,1,0:T(8,128)(2,1)}), bf16[8,512,128]{2,1,0:T(8,128)(2,1)S(1)}, u32[]{:S(2)}, u32[]{:S(2)}) async-start(bf16[8,512,128]{2,1,0:T(8,128)(2,1)} %attend.3), calls=%async_computation.1 | async-start | bytes 2097152 | tf_op jit(solution)/shard_map/all_to_all | solution.py:477
  143.3 7.6 %collective-permute-done.6.rest_8_ = bf16[3,128,512]{2,1,0:T(8,128)(2,1)} collective-permute-done((bf16[3,128,512]{2,1,0:T(8,128)(2,1)}, bf16[3,128,512]{2,1,0:T(8,128)(2,1)}, u32[]{:S(2)}, u32[]{:S(2)}) %collective-permute-start.6) | collective-permute-done | bytes 393248 | tf_op jit(solution)/shard_map/ppermute | solution.py:480
  150.9 14.7 %attend.2 = (bf16[512,128]{1,0:T(8,128)(2,1)}, bf16[512,128]{1,0:T(8,128)(2,1)}, bf16[512,128]{1,0:T(8,128)(2,1)}, bf16[512,128]{1,0:T(8,128)(2,1)}, bf16[512,12...) custom-call(s32[2]{0:T(128)} %pad_add_fusion.3.me_ref, ...), custom_call_target="tpu_custom_call" | custom-call | flops 15000000512 | bytes 4000000 | tf_op jit(solution)/shard_map/attend/pallas_call | solution.py:347
  166.2 3.0 %collective-permute-start.16 = (bf16[512,128]{1,0:T(8,128)(2,1)}, bf16[512,128]{1,0:T(8,128)(2,1)S(1)}, u32[]{:S(2)}, u32[]{:S(2)}) collective-permute-start(bf16[512,128]{1,0:T(8,128)(2,1)} %get-tuple-element.62), channel_id=1, source_target_pairs={{0,12},{4,8},{8,4},{12,0},{16,28},{20,24},{24,20},{28,16},{1,13},{... | collective-permute-start | bytes 393224 | tf_op jit(solution)/shard_map/ppermute | solution.py:480
  169.2 1.9 collective-permute-start.10
  172.9 1.8 collective-permute-start.12
  181.9 6.7 %project.2.rest_8_ = f32[1,512,2048]{2,1,0:T(8,128)S(1)} custom-call(s32[2]{0:T(128)S(1)} %copy-done.8, bf16[8,512,128]{2,1,0:T(8,128)(2,1)S(1)} %all-to-all-done.1.rest_0_, bf16[512,128]{1,0:T(8,128)(2,1)S(1)} %copy-done.1, bf16[512,128]{1,0:T(8,128)(2,1)S(1)} %copy-done.3, bf16[512,128]{1,0:T(8,128)(2,1)S(1)} %copy-done.5, bf16[512,128]{1,0:T(8,128)(2,1)S(1)} %copy-done.7, ...), custom_call_target="tpu_custom_call" | custom-call | flops 3221225472 | bytes 10000000 | tf_op jit(solution)/shard_map/project/pallas_call | solution.py:436
  189.2 3.4 %collective-permute-done.12.rest_2_ = bf16[512,128]{1,0:T(8,128)(2,1)S(1)} collective-permute-done((bf16[512,128]{1,0:T(8,128)(2,1)}, bf16[512,128]{1,0:T(8,128)(2,1)S(1)}, u32[]{:S(2)}, u32[]{:S(2)}) %collective-permute-start.12) | collective-permute-done | bytes 131104 | tf_op jit(solution)/shard_map/ppermute | solution.py:480
  192.6 2.2 %collective-permute-done.13.rest_3_ = bf16[512,128]{1,0:T(8,128)(2,1)} collective-permute-done((bf16[512,128]{1,0:T(8,128)(2,1)}, bf16[512,128]{1,0:T(8,128)(2,1)}, u32[]{:S(2)}, u32[]{:S(2)}) %collective-permute-start.13) | collective-permute-done | bytes 131104 | tf_op jit(solution)/shard_map/ppermute | solution.py:480
  194.8 5.5 %project.3 = bf16[1,512,2048]{2,1,0:T(8,128)(2,1)} custom-call(s32[2]{0:T(128)S(1)} %copy-done.8, bf16[512,128]{1,0:T(8,128)(2,1)S(1)} %collective-permute-done.10.rest_0_, bf16[512,128]{1,0:T(8,128)(2,1)S(1)} %collective-permute-done.11.rest_1_, bf16[512,128]{1,0:T(8,128)(2,1)S(1)} %collective-permute-done.12.rest_2_, ...), custom_call_target="tpu_custom_call" | custom-call | flops 1073741824 | bytes 10000000 | tf_op jit(solution)/shard_map/project/pallas_call | solution.py:436
  (72 shorter events, 18.4 us)
Async XLA Ops:
  3.1 117.3 %all-to-all-start = ((bf16[8,3,128,512]{3,2,1,0:T(8,128)(2,1)}), bf16[8,3,128,512]{3,2,1,0:T(8,128)(2,1)}, u32[]{:S(2)}, u32[]{:S(2)}) async-start(bf16[8,3,128,512]{3,2,1,0:T(8,128)(2,1)} %cut.1), calls=%async_computation | async-start | bytes 6291456 | tf_op jit(solution)/shard_map/all_to_all | solution.py:477
  9.9 33.1 %copy-start = (bf16[512,2048]{1,0:T(8,128)(2,1)S(1)}, bf16[512,2048]{1,0:T(8,128)(2,1)}, u32[]{:S(2)}) copy-start(bf16[512,2048]{1,0:T(8,128)(2,1)} %rest_4_) | copy-start | bytes 6291460
  10.0 42.7 %copy-start.9 = (s32[1,4,64,3]{2,1,3,0:T(4,128)S(1)}, s32[1,4,64,3]{2,1,3,0:T(4,128)}, u32[]{:S(2)}) copy-start(s32[1,4,64,3]{2,1,3,0:T(4,128)} %param.9) | copy-start | bytes 9220
  10.0 42.7 %copy-start.13 = (s32[1,2]{1,0:T(1,128)S(1)}, s32[1,2]{1,0:T(1,128)}, u32[]{:S(2)}) copy-start(s32[1,2]{1,0:T(1,128)} %param.10) | copy-start | bytes 28
  13.8 29.3 %collective-permute-start = (bf16[3,128,512]{2,1,0:T(8,128)(2,1)}, bf16[3,128,512]{2,1,0:T(8,128)(2,1)S(1)}, u32[]{:S(2)}, u32[]{:S(2)}) collective-permute-start(bf16[3,128,512]{2,1,0:T(8,128)(2,1)} %get-tuple-element.35), channel_id=1, source_target_pairs={{0,4},{4,0},{8,12},{12,8},{16,20},{20,16},{24,28},{28,24},{1,5},{5... | collective-permute-start | bytes 1179656 | tf_op jit(solution)/shard_map/ppermute | solution.py:480
  43.0 76.8 %collective-permute-start.8 = (bf16[512,2048]{1,0:T(8,128)(2,1)S(1)}, bf16[512,2048]{1,0:T(8,128)(2,1)}, u32[]{:S(2)}, u32[]{:S(2)}) collective-permute-start(bf16[512,2048]{1,0:T(8,128)(2,1)S(1)} %copy-done), channel_id=1, source_target_pairs={{0,2},{1,3},{2,0},{3,1},{4,6},{5,7},{6,4},{7,5},{8,10},{9,11},{10,... | collective-permute-start | bytes 6291464 | tf_op jit(solution)/shard_map/ppermute | solution.py:463
  44.5 26.7 %collective-permute-start.1 = (bf16[3,128,512]{2,1,0:T(8,128)(2,1)}, bf16[3,128,512]{2,1,0:T(8,128)(2,1)S(1)}, u32[]{:S(2)}, u32[]{:S(2)}) collective-permute-start(bf16[3,128,512]{2,1,0:T(8,128)(2,1)} %get-tuple-element.36), channel_id=1, source_target_pairs={{0,8},{4,12},{8,0},{12,4},{16,24},{20,28},{24,16},{28,20},{1,9},{5... | collective-permute-start | bytes 1179656 | tf_op jit(solution)/shard_map/ppermute | solution.py:480
  46.1 34.8 %collective-permute-start.2 = (bf16[3,128,512]{2,1,0:T(8,128)(2,1)}, bf16[3,128,512]{2,1,0:T(8,128)(2,1)S(1)}, u32[]{:S(2)}, u32[]{:S(2)}) collective-permute-start(bf16[3,128,512]{2,1,0:T(8,128)(2,1)} %get-tuple-element.37), channel_id=1, source_target_pairs={{0,12},{4,8},{8,4},{12,0},{16,28},{20,24},{24,20},{28,16},{1,13},{... | collective-permute-start | bytes 1179656 | tf_op jit(solution)/shard_map/ppermute | solution.py:480
  48.4 71.5 %collective-permute-start.3 = (bf16[3,128,512]{2,1,0:T(8,128)(2,1)}, bf16[3,128,512]{2,1,0:T(8,128)(2,1)}, u32[]{:S(2)}, u32[]{:S(2)}) collective-permute-start(bf16[3,128,512]{2,1,0:T(8,128)(2,1)} %get-tuple-element.38), channel_id=1, source_target_pairs={{0,16},{4,20},{8,24},{12,28},{16,0},{20,4},{24,8},{28,12},{1,17},{... | collective-permute-start | bytes 1179656 | tf_op jit(solution)/shard_map/ppermute | solution.py:480
  50.5 92.9 %collective-permute-start.4 = (bf16[3,128,512]{2,1,0:T(8,128)(2,1)}, bf16[3,128,512]{2,1,0:T(8,128)(2,1)}, u32[]{:S(2)}, u32[]{:S(2)}) collective-permute-start(bf16[3,128,512]{2,1,0:T(8,128)(2,1)} %get-tuple-element.39), channel_id=1, source_target_pairs={{0,20},{4,16},{8,28},{12,24},{16,4},{20,0},{24,12},{28,8},{1,21},{... | collective-permute-start | bytes 1179656 | tf_op jit(solution)/shard_map/ppermute | solution.py:480
  71.2 63.8 %copy-start.11 = (bf16[3,128,512]{2,1,0:T(8,128)(2,1)}, bf16[3,128,512]{2,1,0:T(8,128)(2,1)S(1)}, u32[]{:S(2)}) copy-start(bf16[3,128,512]{2,1,0:T(8,128)(2,1)S(1)} %collective-permute-done.1.rest_3_) | copy-start | bytes 1179652
  71.2 72.1 %collective-permute-start.5 = (bf16[3,128,512]{2,1,0:T(8,128)(2,1)}, bf16[3,128,512]{2,1,0:T(8,128)(2,1)}, u32[]{:S(2)}, u32[]{:S(2)}) collective-permute-start(bf16[3,128,512]{2,1,0:T(8,128)(2,1)} %get-tuple-element.40), channel_id=1, source_target_pairs={{0,24},{4,28},{8,16},{12,20},{16,8},{20,12},{24,0},{28,4},{1,25},{... | collective-permute-start | bytes 1179656 | tf_op jit(solution)/shard_map/ppermute | solution.py:480
  80.9 54.1 %copy-start.12 = (bf16[3,128,512]{2,1,0:T(8,128)(2,1)}, bf16[3,128,512]{2,1,0:T(8,128)(2,1)S(1)}, u32[]{:S(2)}) copy-start(bf16[3,128,512]{2,1,0:T(8,128)(2,1)S(1)} %collective-permute-done.2.rest_4_) | copy-start | bytes 1179652
  80.9 70.0 %collective-permute-start.6 = (bf16[3,128,512]{2,1,0:T(8,128)(2,1)}, bf16[3,128,512]{2,1,0:T(8,128)(2,1)}, u32[]{:S(2)}, u32[]{:S(2)}) collective-permute-start(bf16[3,128,512]{2,1,0:T(8,128)(2,1)} %get-tuple-element.41), channel_id=1, source_target_pairs={{0,28},{4,24},{8,20},{12,16},{16,12},{20,8},{24,4},{28,0},{1,29},{... | collective-permute-start | bytes 1179656 | tf_op jit(solution)/shard_map/ppermute | solution.py:480
  119.9 45.7 %collective-permute-start.7 = (bf16[512,2048]{1,0:T(8,128)(2,1)S(1)}, bf16[512,2048]{1,0:T(8,128)(2,1)}, u32[]{:S(2)}, u32[]{:S(2)}) collective-permute-start(bf16[512,2048]{1,0:T(8,128)(2,1)S(1)} %copy-done), channel_id=1, source_target_pairs={{0,1},{1,0},{2,3},{3,2},{4,5},{5,4},{6,7},{7,6},{8,9},{9,8},{10,11... | collective-permute-start | bytes 6291464 | tf_op jit(solution)/shard_map/ppermute | solution.py:463
  119.9 45.7 %collective-permute-start.9 = (bf16[512,2048]{1,0:T(8,128)(2,1)}, bf16[512,2048]{1,0:T(8,128)(2,1)}, u32[]{:S(2)}, u32[]{:S(2)}) collective-permute-start(bf16[512,2048]{1,0:T(8,128)(2,1)} %collective-permute-done.8.rest_7_.rest_6_), channel_id=1, source_target_pairs={{0,1},{1,0},{2,3},{3,2},{4,5},{5,4},{6,7},{7,6},{8,9},{9,8},{10,11... | collective-permute-start | bytes 6291464 | tf_op jit(solution)/shard_map/ppermute | solution.py:463
  135.1 43.2 %all-to-all-start.1 = ((bf16[8,512,128]{2,1,0:T(8,128)(2,1)}), bf16[8,512,128]{2,1,0:T(8,128)(2,1)S(1)}, u32[]{:S(2)}, u32[]{:S(2)}) async-start(bf16[8,512,128]{2,1,0:T(8,128)(2,1)} %attend.3), calls=%async_computation.1 | async-start | bytes 2097152 | tf_op jit(solution)/shard_map/all_to_all | solution.py:477
  165.6 6.6 %collective-permute-start.14 = (bf16[512,128]{1,0:T(8,128)(2,1)}, bf16[512,128]{1,0:T(8,128)(2,1)S(1)}, u32[]{:S(2)}, u32[]{:S(2)}) collective-permute-start(bf16[512,128]{1,0:T(8,128)(2,1)} %get-tuple-element.60), channel_id=1, source_target_pairs={{0,4},{4,0},{8,12},{12,8},{16,20},{20,16},{24,28},{28,24},{1,5},{5... | collective-permute-start | bytes 393224 | tf_op jit(solution)/shard_map/ppermute | solution.py:480
  166.2 8.6 %collective-permute-start.15 = (bf16[512,128]{1,0:T(8,128)(2,1)}, bf16[512,128]{1,0:T(8,128)(2,1)S(1)}, u32[]{:S(2)}, u32[]{:S(2)}) collective-permute-start(bf16[512,128]{1,0:T(8,128)(2,1)} %get-tuple-element.61), channel_id=1, source_target_pairs={{0,8},{4,12},{8,0},{12,4},{16,24},{20,28},{24,16},{28,20},{1,9},{5... | collective-permute-start | bytes 393224 | tf_op jit(solution)/shard_map/ppermute | solution.py:480
  166.2 11.4 %collective-permute-start.16 = (bf16[512,128]{1,0:T(8,128)(2,1)}, bf16[512,128]{1,0:T(8,128)(2,1)S(1)}, u32[]{:S(2)}, u32[]{:S(2)}) collective-permute-start(bf16[512,128]{1,0:T(8,128)(2,1)} %get-tuple-element.62), channel_id=1, source_target_pairs={{0,12},{4,8},{8,4},{12,0},{16,28},{20,24},{24,20},{28,16},{1,13},{... | collective-permute-start | bytes 393224 | tf_op jit(solution)/shard_map/ppermute | solution.py:480
  169.2 19.4 %collective-permute-start.10 = (bf16[512,128]{1,0:T(8,128)(2,1)}, bf16[512,128]{1,0:T(8,128)(2,1)S(1)}, u32[]{:S(2)}, u32[]{:S(2)}) collective-permute-start(bf16[512,128]{1,0:T(8,128)(2,1)} %get-tuple-element.51), channel_id=1, source_target_pairs={{0,16},{4,20},{8,24},{12,28},{16,0},{20,4},{24,8},{28,12},{1,17},{... | collective-permute-start | bytes 393224 | tf_op jit(solution)/shard_map/ppermute | solution.py:480
  171.1 18.1 %collective-permute-start.11 = (bf16[512,128]{1,0:T(8,128)(2,1)}, bf16[512,128]{1,0:T(8,128)(2,1)S(1)}, u32[]{:S(2)}, u32[]{:S(2)}) collective-permute-start(bf16[512,128]{1,0:T(8,128)(2,1)} %get-tuple-element.52), channel_id=1, source_target_pairs={{0,20},{4,16},{8,28},{12,24},{16,4},{20,0},{24,12},{28,8},{1,21},{... | collective-permute-start | bytes 393224 | tf_op jit(solution)/shard_map/ppermute | solution.py:480
  172.9 19.6 %collective-permute-start.12 = (bf16[512,128]{1,0:T(8,128)(2,1)}, bf16[512,128]{1,0:T(8,128)(2,1)S(1)}, u32[]{:S(2)}, u32[]{:S(2)}) collective-permute-start(bf16[512,128]{1,0:T(8,128)(2,1)} %get-tuple-element.53), channel_id=1, source_target_pairs={{0,24},{4,28},{8,16},{12,20},{16,8},{20,12},{24,0},{28,4},{1,25},{... | collective-permute-start | bytes 393224 | tf_op jit(solution)/shard_map/ppermute | solution.py:480
  175.4 19.4 %collective-permute-start.13 = (bf16[512,128]{1,0:T(8,128)(2,1)}, bf16[512,128]{1,0:T(8,128)(2,1)}, u32[]{:S(2)}, u32[]{:S(2)}) collective-permute-start(bf16[512,128]{1,0:T(8,128)(2,1)} %get-tuple-element.54), channel_id=1, source_target_pairs={{0,28},{4,24},{8,20},{12,16},{16,12},{20,8},{24,4},{28,0},{1,29},{... | collective-permute-start | bytes 393224 | tf_op jit(solution)/shard_map/ppermute | solution.py:480
  (9 other events, 42.5 us)

commit v5 on v4

--- a/solution.py
+++ b/solution.py
@@ -366,18 +366,16 @@
     )(me, rand, glob, pen, *arrays)
 
 
-def project_kernel(n, ndp, slots, before, me_ref, *rest):
+def project_kernel(n, ndp, slots, ahead, before, me_ref, *rest):
     arrays = sorted({i for i, _, _ in slots})
     pieces, rest = rest[: len(arrays)], rest[len(arrays) :]
-    weights, rest = rest[:ndp], rest[ndp:]
     if before:
-        before_ref, rest = rest[0], rest[1:]
-        acc, rest = rest[1], rest[:1] + rest[2:]
-    o_ref, a, w, a_sems, w_sems, acc_sems = rest
+        before_ref, w, o_ref, a, a_sems = rest
+    else:
+        weights, rest = rest[:ndp], rest[ndp:]
+        o_ref, ahead_ref, a, w, a_sems, w_sems, ahead_sems = rest
     me, dp = me_ref[0], me_ref[1]
-    held = n // ndp
-    feats = weights[0].shape[0] // held
-    width = weights[0].shape[1]
+    width = w.shape[1]
     tile = width // 4
 
     def piece_copy(slot):
@@ -387,72 +385,97 @@
         dst = a.at[:, pl.ds(slot * PAIR, PAIR)]
         return pltpu.make_async_copy(src, dst, a_sems.at[slot])
 
-    def weight_copy(slot, part):
-        _, p, k = slots[slot]
-        row = pl.multiple_of(lax.rem(me ^ k, held) * feats + p * PAIR, PAIR)
-        dst = w.at[pl.ds(slot * PAIR, PAIR), :]
-        return pltpu.make_async_copy(weights[part].at[pl.ds(row, PAIR), :], dst, w_sems.at[slot])
-
-    def acc_copy(t):
-        columns = pl.ds(t * tile, tile)
-        return pltpu.make_async_copy(
-            before_ref.at[0, :, columns], acc.at[:, columns], acc_sems.at[t]
-        )
-
-    every = range(len(slots))
-    for slot in every:
+    for slot in range(len(slots)):
         piece_copy(slot).start()
-    own = lax.div(me, held) ^ dp
-    for r in range(ndp):
-
-        @pl.when(own == r)
-        def _():
-            for slot in every:
-                weight_copy(slot, r ^ (slots[slot][2] // held)).start()
-
-    if before:
-        for t in range(4):
-            acc_copy(t).start()
-    for slot in every:
+    if not before:
+        held = n // ndp
+        feats = weights[0].shape[0] // held
+
+        def weight_copy(which, slot, part):
+            _, p, k = which[slot]
+            row = pl.multiple_of(lax.rem(me ^ k, held) * feats + p * PAIR, PAIR)
+            dst, sems = (w, w_sems) if which is slots else (ahead_ref, ahead_sems)
+            return pltpu.make_async_copy(
+                weights[part].at[pl.ds(row, PAIR), :],
+                dst.at[pl.ds(slot * PAIR, PAIR), :],
+                sems.at[slot],
+            )
+
+        own = lax.div(me, held) ^ dp
+        for r in range(ndp):
+
+            @pl.when(own == r)
+            def _():
+                for which in (slots, ahead):
+                    for slot in range(len(which)):
+                        weight_copy(which, slot, r ^ (which[slot][2] // held)).start()
+
+        for slot in range(len(slots)):
+            weight_copy(slots, slot, 0).wait()
+    for slot in range(len(slots)):
         piece_copy(slot).wait()
-    for slot in every:
-        weight_copy(slot, 0).wait()
     for t in range(4):
         columns = slice(t * tile, (t + 1) * tile)
         total = jnp.dot(a[...], w[:, columns], preferred_element_type=jnp.float32)
         if before:
-            acc_copy(t).wait()
-            total = total + acc[:, columns]
+            total = total + before_ref[0, :, columns]
         o_ref[0, :, columns] = total.astype(o_ref.dtype)
-
-
-def project(n, me, pieces, slots, weights, before, dtype):
+    if not before:
+        for slot in range(len(ahead)):
+            weight_copy(ahead, slot, 0).wait()
+
+
+def project_early(n, me, pieces, slots, ahead, weights):
     shard = pieces[0].shape[-2]
     ndp = len(weights)
     width = weights[0].shape[1]
     depth = len(slots) * PAIR
     hbm = pl.BlockSpec(memory_space=pl.ANY)
-    more = [] if before is None else [before]
     return pl.pallas_call(
-        functools.partial(project_kernel, n, ndp, slots, before is not None),
-        out_shape=jax.ShapeDtypeStruct((1, shard, width), dtype),
-        in_specs=[pl.BlockSpec(memory_space=pltpu.SMEM)]
-        + [hbm] * (len(pieces) + ndp + len(more)),
-        out_specs=pl.BlockSpec(memory_space=pltpu.VMEM),
-        scratch_shapes=[pltpu.VMEM((shard, width), jnp.float32)] * len(more)
-        + [
+        functools.partial(project_kernel, n, ndp, slots, ahead, False),
+        out_shape=[
+            pltpu.VMEM((1, shard, width), jnp.float32),
+            pltpu.VMEM((len(ahead) * PAIR, width), jnp.bfloat16),
+        ],
+        in_specs=[pl.BlockSpec(memory_space=pltpu.SMEM)] + [hbm] * (len(pieces) + ndp),
+        out_specs=[pl.BlockSpec(memory_space=pltpu.VMEM)] * 2,
+        scratch_shapes=[
             pltpu.VMEM((shard, depth), jnp.bfloat16),
             pltpu.VMEM((depth, width), jnp.bfloat16),
             pltpu.SemaphoreType.DMA((len(slots),)),
             pltpu.SemaphoreType.DMA((len(slots),)),
-            pltpu.SemaphoreType.DMA((4,)),
+            pltpu.SemaphoreType.DMA((len(ahead),)),
         ],
         compiler_params=pltpu.CompilerParams(vmem_limit_bytes=24 * 1024 * 1024),
         cost_estimate=pl.CostEstimate(
             flops=2 * shard * depth * width, bytes_accessed=10_000_000, transcendentals=0
         ),
-        name="project",
-    )(me, *pieces, *weights, *more)
+        name="project_early",
+    )(me, *pieces, *weights)
+
+
+def project_late(n, me, pieces, slots, before, rows):
+    shard = pieces[0].shape[-2]
+    width = rows.shape[1]
+    depth = len(slots) * PAIR
+    hbm = pl.BlockSpec(memory_space=pl.ANY)
+    vmem = pl.BlockSpec(memory_space=pltpu.VMEM)
+    before, rows = (pltpu.with_memory_space_constraint(x, pltpu.VMEM) for x in (before, rows))
+    return pl.pallas_call(
+        functools.partial(project_kernel, n, 0, slots, [], True),
+        out_shape=jax.ShapeDtypeStruct((1, shard, width), jnp.bfloat16),
+        in_specs=[pl.BlockSpec(memory_space=pltpu.SMEM)] + [hbm] * len(pieces) + [vmem, vmem],
+        out_specs=vmem,
+        scratch_shapes=[
+            pltpu.VMEM((shard, depth), jnp.bfloat16),
+            pltpu.SemaphoreType.DMA((len(slots),)),
+        ],
+        compiler_params=pltpu.CompilerParams(vmem_limit_bytes=24 * 1024 * 1024),
+        cost_estimate=pl.CostEstimate(
+            flops=2 * shard * depth * width, bytes_accessed=10_000_000, transcendentals=0
+        ),
+        name="project_late",
+    )(me, *pieces, before, rows)
 
 
 def gather_weight(ndp, weight):
@@ -502,9 +525,9 @@
     results = swap(outs, far + near)
     pieces += [results[k] for k in [0] + near]
     slots += [(last + i, last, k) for i, k in enumerate([0] + near)]
-    total = project(n, me, pieces, slots, weights, None, jnp.float32)
-    slots = [(i, last, k) for i, k in enumerate(far)]
-    return project(n, me, [results[k] for k in far], slots, weights, total, jnp.bfloat16)
+    late = [(i, last, k) for i, k in enumerate(far)]
+    total, rows = project_early(n, me, pieces, slots, late, weights)
+    return project_late(n, me, [results[k] for k in far], late, total, rows)
 
 
 def solution(mesh):

time: 201 us -> 198 us (0.985)
  local copies, waits for them, and re-layouts: 9.27 us -> 4.59 us
  waiting for transfers between devices: 103 us -> 106 us
    unnamed x28 -> x20, local copies, waits for them, and re-layouts: 5.61 us -> 0.94 us
    ppermute x14, waiting for transfers between devices: 103 us -> 106 us  [swap(): lax.ppermute(arrays[k], 'seq', [(i, i ^ k) for i in range(n)])]
  transfers between devices with their start and end apart: 19 -> 19, of which waited for: 10 -> 11; matrix products, arithmetic and copies ran while one was open for 2% -> 2% of each run, Pallas kernels for 20% -> 21%
where the time goes in v5:
time: 198 us
  waiting for transfers between devices  106 us (54%)
  Pallas kernels  47.1 us (24%)
  starting transfers between devices  39 us (20%)
  local copies, waits for them, and re-layouts  4.59 us (2%)
    ppermute x14, waiting for transfers between devices, swap(): lax.ppermute(arrays[k], 'seq', [(i, i ^ k) for i in range(n)])  106 us
    pallas_call x2, Pallas kernels, attend(): pl.pallas_call(functools.partial(attend_kernel, n, nblocks, apart_in, apa...  29.3 us
    ppermute x14, starting transfers between devices, swap(): lax.ppermute(arrays[k], 'seq', [(i, i ^ k) for i in range(n)])  23.4 us
    all_to_all x2, starting transfers between devices, exchange(): return lax.all_to_all(x, 'seq', split_axis=0, concat_axis=0, tiled=True)  13.6 us
    pallas_call x1, Pallas kernels, project_early(): pl.pallas_call(functools.partial(project_kernel, n, ndp, slots, ahead, Fa...  7.76 us
  transfers between devices with their start and end apart: 19, of which 11 were waited for; matrix products, arithmetic and copies ran while one was open for 2% of the time, Pallas kernels for 21%

profile of v5, /device:TPU:8, one launch (start us, length us, event | category | flops | bytes accessed | tf_op | source)
XLA Modules:
  0.0 198.1 jit_solution(6043080871295728452)
XLA Ops:
  0.0 3.0 %cut.1 = bf16[8,3,128,512]{3,2,1,0:T(8,128)(2,1)} custom-call(bf16[1,2048,512]{2,1,0:T(8,128)(2,1)} %q_ref.3, bf16[1,2048,512]{2,1,0:T(8,128)(2,1)} %k_ref.3, bf16[1,2048,512]{2,1,0:T(8,128)(2,1)} %v_ref.3), custom_call_target="tpu_custom_call" | custom-call | tf_op jit(solution)/shard_map/cut/pallas_call | solution.py:134
  3.1 6.3 %all-to-all-start = ((bf16[8,3,128,512]{3,2,1,0:T(8,128)(2,1)}), bf16[8,3,128,512]{3,2,1,0:T(8,128)(2,1)}, u32[]{:S(2)}, u32[]{:S(2)}) async-start(bf16[8,3,128,512]{3,2,1,0:T(8,128)(2,1)} %cut.1), calls=%async_computation | async-start | bytes 6291456 | tf_op jit(solution)/shard_map/all_to_all | solution.py:500
  9.9 3.8 %cut_apart.1 = (bf16[3,128,512]{2,1,0:T(8,128)(2,1)}, bf16[3,128,512]{2,1,0:T(8,128)(2,1)}, bf16[3,128,512]{2,1,0:T(8,128)(2,1)}, bf16[3,128,512]{2,1,0:T(8,128)...) custom-call(s32[2]{0:T(128)} %pad_add_fusion.3.me_ref, ...), custom_call_target="tpu_custom_call" | custom-call | tf_op jit(solution)/shard_map/cut_apart/pallas_call | solution.py:178
  15.3 27.7 %collective-permute-done.rest_2_ = bf16[3,128,512]{2,1,0:T(8,128)(2,1)S(1)} collective-permute-done((bf16[3,128,512]{2,1,0:T(8,128)(2,1)}, bf16[3,128,512]{2,1,0:T(8,128)(2,1)S(1)}, u32[]{:S(2)}, u32[]{:S(2)}) %collective-permute-start) | collective-permute-done | bytes 393248 | tf_op jit(solution)/shard_map/ppermute | solution.py:503
  46.1 2.3 %collective-permute-start.2 = (bf16[3,128,512]{2,1,0:T(8,128)(2,1)}, bf16[3,128,512]{2,1,0:T(8,128)(2,1)S(1)}, u32[]{:S(2)}, u32[]{:S(2)}) collective-permute-start(bf16[3,128,512]{2,1,0:T(8,128)(2,1)} %get-tuple-element.39), channel_id=1, source_target_pairs={{0,12},{4,8},{8,4},{12,0},{16,28},{20,24},{24,20},{28,16},{1,13},{... | collective-permute-start | bytes 1179656 | tf_op jit(solution)/shard_map/ppermute | solution.py:503
  48.4 2.1 %collective-permute-start.3 = (bf16[3,128,512]{2,1,0:T(8,128)(2,1)}, bf16[3,128,512]{2,1,0:T(8,128)(2,1)S(1)}, u32[]{:S(2)}, u32[]{:S(2)}) collective-permute-start(bf16[3,128,512]{2,1,0:T(8,128)(2,1)} %get-tuple-element.40), channel_id=1, source_target_pairs={{0,16},{4,20},{8,24},{12,28},{16,0},{20,4},{24,8},{28,12},{1,17},{... | collective-permute-start | bytes 1179656 | tf_op jit(solution)/shard_map/ppermute | solution.py:503
  50.5 2.2 %collective-permute-start.4 = (bf16[3,128,512]{2,1,0:T(8,128)(2,1)}, bf16[3,128,512]{2,1,0:T(8,128)(2,1)}, u32[]{:S(2)}, u32[]{:S(2)}) collective-permute-start(bf16[3,128,512]{2,1,0:T(8,128)(2,1)} %get-tuple-element.41), channel_id=1, source_target_pairs={{0,20},{4,16},{8,28},{12,24},{16,4},{20,0},{24,12},{28,8},{1,21},{... | collective-permute-start | bytes 1179656 | tf_op jit(solution)/shard_map/ppermute | solution.py:503
  55.9 15.3 %collective-permute-done.1.rest_3_ = bf16[3,128,512]{2,1,0:T(8,128)(2,1)S(1)} collective-permute-done((bf16[3,128,512]{2,1,0:T(8,128)(2,1)}, bf16[3,128,512]{2,1,0:T(8,128)(2,1)S(1)}, u32[]{:S(2)}, u32[]{:S(2)}) %collective-permute-start.1) | collective-permute-done | bytes 393248 | tf_op jit(solution)/shard_map/ppermute | solution.py:503
  71.2 1.9 collective-permute-start.5
  73.2 7.8 %collective-permute-done.2.rest_4_ = bf16[3,128,512]{2,1,0:T(8,128)(2,1)S(1)} collective-permute-done((bf16[3,128,512]{2,1,0:T(8,128)(2,1)}, bf16[3,128,512]{2,1,0:T(8,128)(2,1)S(1)}, u32[]{:S(2)}, u32[]{:S(2)}) %collective-permute-start.2) | collective-permute-done | bytes 393248 | tf_op jit(solution)/shard_map/ppermute | solution.py:503
  82.5 37.4 %collective-permute-done.3.rest_5_ = bf16[3,128,512]{2,1,0:T(8,128)(2,1)S(1)} collective-permute-done((bf16[3,128,512]{2,1,0:T(8,128)(2,1)}, bf16[3,128,512]{2,1,0:T(8,128)(2,1)S(1)}, u32[]{:S(2)}, u32[]{:S(2)}) %collective-permute-start.3) | collective-permute-done | bytes 393248 | tf_op jit(solution)/shard_map/ppermute | solution.py:503
  120.4 14.6 %attend.3 = bf16[8,512,128]{2,1,0:T(8,128)(2,1)} custom-call(s32[2]{0:T(128)} %pad_add_fusion.3.me_ref, s32[384]{0:T(512)} %squeeze.22.rand_ref, s32[2]{0:T(128)} %bitcast.19, f32[64,8,2]{2,1,0:T(8,128)} %get-tuple-element.67.rest_0_, bf16[8,3,128,512]{3,2,1,0:T(8,128)(2,1)} %all-to-all-done.rest_1_), custom_call_target="tpu_custom_call" | custom-call | flops 15000000512 | bytes 4000000 | tf_op jit(solution)/shard_map/attend/pallas_call | solution.py:347
  135.1 7.3 %all-to-all-start.1 = ((bf16[8,512,128]{2,1,0:T(8,128)(2,1)}), bf16[8,512,128]{2,1,0:T(8,128)(2,1)S(1)}, u32[]{:S(2)}, u32[]{:S(2)}) async-start(bf16[8,512,128]{2,1,0:T(8,128)(2,1)} %attend.3), calls=%async_computation.1 | async-start | bytes 2097152 | tf_op jit(solution)/shard_map/all_to_all | solution.py:500
  143.3 7.7 %collective-permute-done.6.rest_8_ = bf16[3,128,512]{2,1,0:T(8,128)(2,1)} collective-permute-done((bf16[3,128,512]{2,1,0:T(8,128)(2,1)S(1)}, bf16[3,128,512]{2,1,0:T(8,128)(2,1)}, u32[]{:S(2)}, u32[]{:S(2)}) %collective-permute-start.6) | collective-permute-done | bytes 393248 | tf_op jit(solution)/shard_map/ppermute | solution.py:503
  150.9 14.6 %attend.2 = (bf16[512,128]{1,0:T(8,128)(2,1)}, bf16[512,128]{1,0:T(8,128)(2,1)}, bf16[512,128]{1,0:T(8,128)(2,1)}, bf16[512,128]{1,0:T(8,128)(2,1)}, bf16[512,12...) custom-call(s32[2]{0:T(128)} %pad_add_fusion.3.me_ref, ...), custom_call_target="tpu_custom_call" | custom-call | flops 15000000512 | bytes 4000000 | tf_op jit(solution)/shard_map/attend/pallas_call | solution.py:347
  166.0 3.1 %collective-permute-start.16 = (bf16[512,128]{1,0:T(8,128)(2,1)}, bf16[512,128]{1,0:T(8,128)(2,1)S(1)}, u32[]{:S(2)}, u32[]{:S(2)}) collective-permute-start(bf16[512,128]{1,0:T(8,128)(2,1)} %get-tuple-element.60), channel_id=1, source_target_pairs={{0,12},{4,8},{8,4},{12,0},{16,28},{20,24},{24,20},{28,16},{1,13},{... | collective-permute-start | bytes 393224 | tf_op jit(solution)/shard_map/ppermute | solution.py:503
  169.1 1.9 collective-permute-start.10
  172.2 1.8 collective-permute-start.12
  174.1 2.1 %collective-permute-start.13 = (bf16[512,128]{1,0:T(8,128)(2,1)}, bf16[512,128]{1,0:T(8,128)(2,1)S(1)}, u32[]{:S(2)}, u32[]{:S(2)}) collective-permute-start(bf16[512,128]{1,0:T(8,128)(2,1)} %get-tuple-element.56), channel_id=1, source_target_pairs={{0,28},{4,24},{8,20},{12,16},{16,12},{20,8},{24,4},{28,0},{1,29},{... | collective-permute-start | bytes 393224 | tf_op jit(solution)/shard_map/ppermute | solution.py:503
  178.5 7.8 %project_early.1 = (f32[1,512,2048]{2,1,0:T(8,128)S(1)}, bf16[512,2048]{1,0:T(8,128)(2,1)S(1)}) custom-call(s32[2]{0:T(128)S(1)} %copy-done, bf16[8,512,128]{2,1,0:T(8,128)(2,1)S(1)} %all-to-all-done.1.rest_0_, bf16[512,128]{1,0:T(8,128)(2,1)S(1)} %copy-done.1, bf16[512,128]{1,0:T(8,128)(2,1)S(1)} %collective-permute-done.14.rest_2_, ...), custom_call_target="tpu_custom_call" | custom-call | flops 3221225472 | bytes 10000000 | tf_op jit(solution)/shard_map/project_early/pallas_call | solution.py:434
  186.4 2.8 %collective-permute-done.11.rest_1_ = bf16[512,128]{1,0:T(8,128)(2,1)S(1)} collective-permute-done((bf16[512,128]{1,0:T(8,128)(2,1)}, bf16[512,128]{1,0:T(8,128)(2,1)S(1)}, u32[]{:S(2)}, u32[]{:S(2)}) %collective-permute-start.11) | collective-permute-done | bytes 131104 | tf_op jit(solution)/shard_map/ppermute | solution.py:503
  189.2 3.3 %collective-permute-done.12.rest_2_ = bf16[512,128]{1,0:T(8,128)(2,1)S(1)} collective-permute-done((bf16[512,128]{1,0:T(8,128)(2,1)}, bf16[512,128]{1,0:T(8,128)(2,1)S(1)}, u32[]{:S(2)}, u32[]{:S(2)}) %collective-permute-start.12) | collective-permute-done | bytes 131104 | tf_op jit(solution)/shard_map/ppermute | solution.py:503
  192.5 2.2 %collective-permute-done.13.rest_3_ = bf16[512,128]{1,0:T(8,128)(2,1)S(1)} collective-permute-done((bf16[512,128]{1,0:T(8,128)(2,1)}, bf16[512,128]{1,0:T(8,128)(2,1)S(1)}, u32[]{:S(2)}, u32[]{:S(2)}) %collective-permute-start.13) | collective-permute-done | bytes 131104 | tf_op jit(solution)/shard_map/ppermute | solution.py:503
  194.7 3.3 %project_late.1 = bf16[1,512,2048]{2,1,0:T(8,128)(2,1)} custom-call(s32[2]{0:T(128)S(1)} %copy-done, bf16[512,128]{1,0:T(8,128)(2,1)S(1)} %collective-permute-done.10.rest_0_, bf16[512,128]{1,0:T(8,128)(2,1)S(1)} %collective-permute-done.11.rest_1_, bf16[512,128]{1,0:T(8,128)(2,1)S(1)} %collective-permute-done.12.rest_2_, ...), custom_call_target="tpu_custom_call" | custom-call | flops 1073741824 | bytes 10000000 | tf_op jit(solution)/shard_map/project_late/pallas_call | solution.py:464
  (64 shorter events, 15.4 us)
Async XLA Ops:
  3.1 117.3 %all-to-all-start = ((bf16[8,3,128,512]{3,2,1,0:T(8,128)(2,1)}), bf16[8,3,128,512]{3,2,1,0:T(8,128)(2,1)}, u32[]{:S(2)}, u32[]{:S(2)}) async-start(bf16[8,3,128,512]{3,2,1,0:T(8,128)(2,1)} %cut.1), calls=%async_computation | async-start | bytes 6291456 | tf_op jit(solution)/shard_map/all_to_all | solution.py:500
  13.8 57.4 %copy-start.6 = (bf16[3,128,512]{2,1,0:T(8,128)(2,1)S(1)}, bf16[3,128,512]{2,1,0:T(8,128)(2,1)}, u32[]{:S(2)}) copy-start(bf16[3,128,512]{2,1,0:T(8,128)(2,1)} %get-tuple-element.42) | copy-start | bytes 1179652
  13.8 67.1 %copy-start.4 = (bf16[3,128,512]{2,1,0:T(8,128)(2,1)S(1)}, bf16[3,128,512]{2,1,0:T(8,128)(2,1)}, u32[]{:S(2)}) copy-start(bf16[3,128,512]{2,1,0:T(8,128)(2,1)} %get-tuple-element.43) | copy-start | bytes 1179652
  13.8 29.3 %collective-permute-start = (bf16[3,128,512]{2,1,0:T(8,128)(2,1)}, bf16[3,128,512]{2,1,0:T(8,128)(2,1)S(1)}, u32[]{:S(2)}, u32[]{:S(2)}) collective-permute-start(bf16[3,128,512]{2,1,0:T(8,128)(2,1)} %get-tuple-element.37), channel_id=1, source_target_pairs={{0,4},{4,0},{8,12},{12,8},{16,20},{20,16},{24,28},{28,24},{1,5},{5... | collective-permute-start | bytes 1179656 | tf_op jit(solution)/shard_map/ppermute | solution.py:503
  43.0 92.0 %copy-start.3 = (bf16[3,128,512]{2,1,0:T(8,128)(2,1)}, bf16[3,128,512]{2,1,0:T(8,128)(2,1)S(1)}, u32[]{:S(2)}) copy-start(bf16[3,128,512]{2,1,0:T(8,128)(2,1)S(1)} %collective-permute-done.rest_2_) | copy-start | bytes 1179652
  43.0 76.8 %collective-permute-start.8 = (bf16[512,2048]{1,0:T(8,128)(2,1)}, bf16[512,2048]{1,0:T(8,128)(2,1)}, u32[]{:S(2)}, u32[]{:S(2)}) collective-permute-start(bf16[512,2048]{1,0:T(8,128)(2,1)} %rest_5_), channel_id=1, source_target_pairs={{0,2},{1,3},{2,0},{3,1},{4,6},{5,7},{6,4},{7,5},{8,10},{9,11},{10,... | collective-permute-start | bytes 6291464 | tf_op jit(solution)/shard_map/ppermute | solution.py:486
  44.5 26.7 %collective-permute-start.1 = (bf16[3,128,512]{2,1,0:T(8,128)(2,1)}, bf16[3,128,512]{2,1,0:T(8,128)(2,1)S(1)}, u32[]{:S(2)}, u32[]{:S(2)}) collective-permute-start(bf16[3,128,512]{2,1,0:T(8,128)(2,1)} %get-tuple-element.38), channel_id=1, source_target_pairs={{0,8},{4,12},{8,0},{12,4},{16,24},{20,28},{24,16},{28,20},{1,9},{5... | collective-permute-start | bytes 1179656 | tf_op jit(solution)/shard_map/ppermute | solution.py:503
  46.1 34.9 %collective-permute-start.2 = (bf16[3,128,512]{2,1,0:T(8,128)(2,1)}, bf16[3,128,512]{2,1,0:T(8,128)(2,1)S(1)}, u32[]{:S(2)}, u32[]{:S(2)}) collective-permute-start(bf16[3,128,512]{2,1,0:T(8,128)(2,1)} %get-tuple-element.39), channel_id=1, source_target_pairs={{0,12},{4,8},{8,4},{12,0},{16,28},{20,24},{24,20},{28,16},{1,13},{... | collective-permute-start | bytes 1179656 | tf_op jit(solution)/shard_map/ppermute | solution.py:503
  48.4 71.5 %collective-permute-start.3 = (bf16[3,128,512]{2,1,0:T(8,128)(2,1)}, bf16[3,128,512]{2,1,0:T(8,128)(2,1)S(1)}, u32[]{:S(2)}, u32[]{:S(2)}) collective-permute-start(bf16[3,128,512]{2,1,0:T(8,128)(2,1)} %get-tuple-element.40), channel_id=1, source_target_pairs={{0,16},{4,20},{8,24},{12,28},{16,0},{20,4},{24,8},{28,12},{1,17},{... | collective-permute-start | bytes 1179656 | tf_op jit(solution)/shard_map/ppermute | solution.py:503
  50.5 92.8 %collective-permute-start.4 = (bf16[3,128,512]{2,1,0:T(8,128)(2,1)}, bf16[3,128,512]{2,1,0:T(8,128)(2,1)}, u32[]{:S(2)}, u32[]{:S(2)}) collective-permute-start(bf16[3,128,512]{2,1,0:T(8,128)(2,1)} %get-tuple-element.41), channel_id=1, source_target_pairs={{0,20},{4,16},{8,28},{12,24},{16,4},{20,0},{24,12},{28,8},{1,21},{... | collective-permute-start | bytes 1179656 | tf_op jit(solution)/shard_map/ppermute | solution.py:503
  71.2 63.8 %copy-start.5 = (bf16[3,128,512]{2,1,0:T(8,128)(2,1)}, bf16[3,128,512]{2,1,0:T(8,128)(2,1)S(1)}, u32[]{:S(2)}) copy-start(bf16[3,128,512]{2,1,0:T(8,128)(2,1)S(1)} %collective-permute-done.1.rest_3_) | copy-start | bytes 1179652
  71.2 72.0 %collective-permute-start.5 = (bf16[3,128,512]{2,1,0:T(8,128)(2,1)S(1)}, bf16[3,128,512]{2,1,0:T(8,128)(2,1)}, u32[]{:S(2)}, u32[]{:S(2)}) collective-permute-start(bf16[3,128,512]{2,1,0:T(8,128)(2,1)S(1)} %copy-done.6), channel_id=1, source_target_pairs={{0,24},{4,28},{8,16},{12,20},{16,8},{20,12},{24,0},{28,4},{1,25},{... | collective-permute-start | bytes 1179656 | tf_op jit(solution)/shard_map/ppermute | solution.py:503
  80.9 54.1 %copy-start.7 = (bf16[3,128,512]{2,1,0:T(8,128)(2,1)}, bf16[3,128,512]{2,1,0:T(8,128)(2,1)S(1)}, u32[]{:S(2)}) copy-start(bf16[3,128,512]{2,1,0:T(8,128)(2,1)S(1)} %collective-permute-done.2.rest_4_) | copy-start | bytes 1179652
  80.9 70.0 %collective-permute-start.6 = (bf16[3,128,512]{2,1,0:T(8,128)(2,1)S(1)}, bf16[3,128,512]{2,1,0:T(8,128)(2,1)}, u32[]{:S(2)}, u32[]{:S(2)}) collective-permute-start(bf16[3,128,512]{2,1,0:T(8,128)(2,1)S(1)} %copy-done.4), channel_id=1, source_target_pairs={{0,28},{4,24},{8,20},{12,16},{16,12},{20,8},{24,4},{28,0},{1,29},{... | collective-permute-start | bytes 1179656 | tf_op jit(solution)/shard_map/ppermute | solution.py:503
  119.9 45.7 %collective-permute-start.7 = (bf16[512,2048]{1,0:T(8,128)(2,1)}, bf16[512,2048]{1,0:T(8,128)(2,1)}, u32[]{:S(2)}, u32[]{:S(2)}) collective-permute-start(bf16[512,2048]{1,0:T(8,128)(2,1)} %rest_5_), channel_id=1, source_target_pairs={{0,1},{1,0},{2,3},{3,2},{4,5},{5,4},{6,7},{7,6},{8,9},{9,8},{10,11... | collective-permute-start | bytes 6291464 | tf_op jit(solution)/shard_map/ppermute | solution.py:486
  119.9 45.7 %collective-permute-start.9 = (bf16[512,2048]{1,0:T(8,128)(2,1)}, bf16[512,2048]{1,0:T(8,128)(2,1)}, u32[]{:S(2)}, u32[]{:S(2)}) collective-permute-start(bf16[512,2048]{1,0:T(8,128)(2,1)} %collective-permute-done.8.rest_7_), channel_id=1, source_target_pairs={{0,1},{1,0},{2,3},{3,2},{4,5},{5,4},{6,7},{7,6},{8,9},{9,8},{10,11... | collective-permute-start | bytes 6291464 | tf_op jit(solution)/shard_map/ppermute | solution.py:486
  135.1 42.5 %all-to-all-start.1 = ((bf16[8,512,128]{2,1,0:T(8,128)(2,1)}), bf16[8,512,128]{2,1,0:T(8,128)(2,1)S(1)}, u32[]{:S(2)}, u32[]{:S(2)}) async-start(bf16[8,512,128]{2,1,0:T(8,128)(2,1)} %attend.3), calls=%async_computation.1 | async-start | bytes 2097152 | tf_op jit(solution)/shard_map/all_to_all | solution.py:500
  165.6 6.6 %collective-permute-start.14 = (bf16[512,128]{1,0:T(8,128)(2,1)}, bf16[512,128]{1,0:T(8,128)(2,1)S(1)}, u32[]{:S(2)}, u32[]{:S(2)}) collective-permute-start(bf16[512,128]{1,0:T(8,128)(2,1)} %get-tuple-element.58), channel_id=1, source_target_pairs={{0,4},{4,0},{8,12},{12,8},{16,20},{20,16},{24,28},{28,24},{1,5},{5... | collective-permute-start | bytes 393224 | tf_op jit(solution)/shard_map/ppermute | solution.py:503
  166.0 8.0 %collective-permute-start.15 = (bf16[512,128]{1,0:T(8,128)(2,1)}, bf16[512,128]{1,0:T(8,128)(2,1)S(1)}, u32[]{:S(2)}, u32[]{:S(2)}) collective-permute-start(bf16[512,128]{1,0:T(8,128)(2,1)} %get-tuple-element.59), channel_id=1, source_target_pairs={{0,8},{4,12},{8,0},{12,4},{16,24},{20,28},{24,16},{28,20},{1,9},{5... | collective-permute-start | bytes 393224 | tf_op jit(solution)/shard_map/ppermute | solution.py:503
  166.0 11.6 %collective-permute-start.16 = (bf16[512,128]{1,0:T(8,128)(2,1)}, bf16[512,128]{1,0:T(8,128)(2,1)S(1)}, u32[]{:S(2)}, u32[]{:S(2)}) collective-permute-start(bf16[512,128]{1,0:T(8,128)(2,1)} %get-tuple-element.60), channel_id=1, source_target_pairs={{0,12},{4,8},{8,4},{12,0},{16,28},{20,24},{24,20},{28,16},{1,13},{... | collective-permute-start | bytes 393224 | tf_op jit(solution)/shard_map/ppermute | solution.py:503
  169.1 17.2 %collective-permute-start.10 = (bf16[512,128]{1,0:T(8,128)(2,1)}, bf16[512,128]{1,0:T(8,128)(2,1)S(1)}, u32[]{:S(2)}, u32[]{:S(2)}) collective-permute-start(bf16[512,128]{1,0:T(8,128)(2,1)} %get-tuple-element.53), channel_id=1, source_target_pairs={{0,16},{4,20},{8,24},{12,28},{16,0},{20,4},{24,8},{28,12},{1,17},{... | collective-permute-start | bytes 393224 | tf_op jit(solution)/shard_map/ppermute | solution.py:503
  171.0 18.1 %collective-permute-start.11 = (bf16[512,128]{1,0:T(8,128)(2,1)}, bf16[512,128]{1,0:T(8,128)(2,1)S(1)}, u32[]{:S(2)}, u32[]{:S(2)}) collective-permute-start(bf16[512,128]{1,0:T(8,128)(2,1)} %get-tuple-element.54), channel_id=1, source_target_pairs={{0,20},{4,16},{8,28},{12,24},{16,4},{20,0},{24,12},{28,8},{1,21},{... | collective-permute-start | bytes 393224 | tf_op jit(solution)/shard_map/ppermute | solution.py:503
  172.2 20.3 %collective-permute-start.12 = (bf16[512,128]{1,0:T(8,128)(2,1)}, bf16[512,128]{1,0:T(8,128)(2,1)S(1)}, u32[]{:S(2)}, u32[]{:S(2)}) collective-permute-start(bf16[512,128]{1,0:T(8,128)(2,1)} %get-tuple-element.55), channel_id=1, source_target_pairs={{0,24},{4,28},{8,16},{12,20},{16,8},{20,12},{24,0},{28,4},{1,25},{... | collective-permute-start | bytes 393224 | tf_op jit(solution)/shard_map/ppermute | solution.py:503
  174.1 20.6 %collective-permute-start.13 = (bf16[512,128]{1,0:T(8,128)(2,1)}, bf16[512,128]{1,0:T(8,128)(2,1)S(1)}, u32[]{:S(2)}, u32[]{:S(2)}) collective-permute-start(bf16[512,128]{1,0:T(8,128)(2,1)} %get-tuple-element.56), channel_id=1, source_target_pairs={{0,28},{4,24},{8,20},{12,16},{16,12},{20,8},{24,4},{28,0},{1,29},{... | collective-permute-start | bytes 393224 | tf_op jit(solution)/shard_map/ppermute | solution.py:503
  (5 other events, 128.3 us)

commit v6 on v5

--- a/solution.py
+++ b/solution.py
@@ -106,41 +106,29 @@
     return result.astype(jnp.bfloat16)[None]
 
 
-def cut_kernel(n, feats, row, q_ref, k_ref, v_ref, out, held, in_sems, out_sems):
-    def read(to, i):
-        src = (q_ref, k_ref, v_ref)[i]
-        return pltpu.make_async_copy(
-            src.at[0, pl.ds(to * feats + row, PAIR), :], held.at[to, i], in_sems.at[to, i]
-        )
-
-    def write(to):
-        return pltpu.make_async_copy(held.at[to], out.at[to], out_sems.at[to])
-
+def cut_kernel(n, feats, row, q_ref, k_ref, v_ref, out, sems):
+    copies = []
     for to in range(n):
-        for i in range(3):
-            read(to, i).start()
-    for to in range(n):
-        for i in range(3):
-            read(to, i).wait()
-        write(to).start()
-    for to in range(n):
-        write(to).wait()
+        for i, src in enumerate((q_ref, k_ref, v_ref)):
+            src = src.at[0, pl.ds(to * feats + row, PAIR), :]
+            copies.append(pltpu.make_async_copy(src, out.at[to, i], sems.at[to, i]))
+    for copy in copies:
+        copy.start()
+    for copy in copies:
+        copy.wait()
 
 
 def cut(n, row, queries, keys, values):
     feats = queries.shape[1] // n
     length = queries.shape[2]
-    hbm = pl.BlockSpec(memory_space=pltpu.HBM)
+    hbm = pl.BlockSpec(memory_space=pl.ANY)
     return pl.pallas_call(
         functools.partial(cut_kernel, n, feats, row),
-        out_shape=jax.ShapeDtypeStruct((n, 3, PAIR, length), queries.dtype),
+        out_shape=pltpu.VMEM((n, 3, PAIR, length), queries.dtype),
         in_specs=[hbm, hbm, hbm],
-        out_specs=hbm,
-        scratch_shapes=[
-            pltpu.VMEM((n, 3, PAIR, length), queries.dtype),
-            pltpu.SemaphoreType.DMA((n, 3)),
-            pltpu.SemaphoreType.DMA((n,)),
-        ],
+        out_specs=pl.BlockSpec(memory_space=pltpu.VMEM),
+        scratch_shapes=[pltpu.SemaphoreType.DMA((n, 3))],
+        compiler_params=pltpu.CompilerParams(vmem_limit_bytes=56 * 1024 * 1024),
         name="cut",
     )(queries, keys, values)
 

time: 198 us -> 197 us (level)
  starting transfers between devices: 39 us -> 36.8 us
    ppermute x14, starting transfers between devices: 23.4 us -> 21.1 us  [swap(): lax.ppermute(arrays[k], 'seq', [(i, i ^ k) for i in range(n)])]
  transfers between devices with their start and end apart: 19 -> 19, of which waited for: 11 -> 10; matrix products, arithmetic and copies ran while one was open for 2% -> 2% of each run, Pallas kernels for 21% -> 21%
where the time goes in v6:
time: 197 us
  waiting for transfers between devices  105 us (53%)
  Pallas kernels  48 us (24%)
  starting transfers between devices  36.8 us (19%)
  local copies, waits for them, and re-layouts  6.2 us (3%)
    ppermute x14, waiting for transfers between devices, swap(): lax.ppermute(arrays[k], 'seq', [(i, i ^ k) for i in range(n)])  105 us
    pallas_call x2, Pallas kernels, attend(): pl.pallas_call(functools.partial(attend_kernel, n, nblocks, apart_in, apa...  29.3 us
    ppermute x14, starting transfers between devices, swap(): lax.ppermute(arrays[k], 'seq', [(i, i ^ k) for i in range(n)])  21.1 us
    all_to_all x2, starting transfers between devices, exchange(): return lax.all_to_all(x, 'seq', split_axis=0, concat_axis=0, tiled=True)  13.7 us
    pallas_call x1, Pallas kernels, project_early(): pl.pallas_call(functools.partial(project_kernel, n, ndp, slots, ahead, Fa...  7.83 us
  transfers between devices with their start and end apart: 19, of which 10 were waited for; matrix products, arithmetic and copies ran while one was open for 2% of the time, Pallas kernels for 21%

profile of v6, /device:TPU:8, one launch (start us, length us, event | category | flops | bytes accessed | tf_op | source)
XLA Modules:
  0.0 196.9 jit_solution(6421308117780453306)
XLA Ops:
  0.0 3.8 %cut.1 = bf16[8,3,128,512]{3,2,1,0:T(8,128)(2,1)} custom-call(bf16[1,2048,512]{2,1,0:T(8,128)(2,1)} %q_ref.3, bf16[1,2048,512]{2,1,0:T(8,128)(2,1)} %k_ref.3, bf16[1,2048,512]{2,1,0:T(8,128)(2,1)} %v_ref.3), custom_call_target="tpu_custom_call" | custom-call | tf_op jit(solution)/shard_map/cut/pallas_call | solution.py:125
  3.8 6.3 %all-to-all-start = ((bf16[8,3,128,512]{3,2,1,0:T(8,128)(2,1)}), bf16[8,3,128,512]{3,2,1,0:T(8,128)(2,1)S(1)}, u32[]{:S(2)}, u32[]{:S(2)}) async-start(bf16[8,3,128,512]{3,2,1,0:T(8,128)(2,1)} %cut.1), calls=%async_computation | async-start | bytes 6291456 | tf_op jit(solution)/shard_map/all_to_all | solution.py:488
  10.7 3.8 %cut_apart.1 = (bf16[3,128,512]{2,1,0:T(8,128)(2,1)}, bf16[3,128,512]{2,1,0:T(8,128)(2,1)}, bf16[3,128,512]{2,1,0:T(8,128)(2,1)}, bf16[3,128,512]{2,1,0:T(8,128)...) custom-call(s32[2]{0:T(128)} %pad_add_fusion.3.me_ref, ...), custom_call_target="tpu_custom_call" | custom-call | tf_op jit(solution)/shard_map/cut_apart/pallas_call | solution.py:166
  16.1 27.7 %collective-permute-done.rest_2_ = bf16[3,128,512]{2,1,0:T(8,128)(2,1)S(1)} collective-permute-done((bf16[3,128,512]{2,1,0:T(8,128)(2,1)}, bf16[3,128,512]{2,1,0:T(8,128)(2,1)S(1)}, u32[]{:S(2)}, u32[]{:S(2)}) %collective-permute-start) | collective-permute-done | bytes 393248 | tf_op jit(solution)/shard_map/ppermute | solution.py:491
  46.8 2.3 %collective-permute-start.2 = (bf16[3,128,512]{2,1,0:T(8,128)(2,1)}, bf16[3,128,512]{2,1,0:T(8,128)(2,1)}, u32[]{:S(2)}, u32[]{:S(2)}) collective-permute-start(bf16[3,128,512]{2,1,0:T(8,128)(2,1)} %get-tuple-element.39), channel_id=1, source_target_pairs={{0,12},{4,8},{8,4},{12,0},{16,28},{20,24},{24,20},{28,16},{1,13},{... | collective-permute-start | bytes 1179656 | tf_op jit(solution)/shard_map/ppermute | solution.py:491
  49.1 2.1 %collective-permute-start.3 = (bf16[3,128,512]{2,1,0:T(8,128)(2,1)}, bf16[3,128,512]{2,1,0:T(8,128)(2,1)}, u32[]{:S(2)}, u32[]{:S(2)}) collective-permute-start(bf16[3,128,512]{2,1,0:T(8,128)(2,1)} %get-tuple-element.40), channel_id=1, source_target_pairs={{0,16},{4,20},{8,24},{12,28},{16,0},{20,4},{24,8},{28,12},{1,17},{... | collective-permute-start | bytes 1179656 | tf_op jit(solution)/shard_map/ppermute | solution.py:491
  51.2 2.2 %collective-permute-start.4 = (bf16[3,128,512]{2,1,0:T(8,128)(2,1)}, bf16[3,128,512]{2,1,0:T(8,128)(2,1)}, u32[]{:S(2)}, u32[]{:S(2)}) collective-permute-start(bf16[3,128,512]{2,1,0:T(8,128)(2,1)} %get-tuple-element.41), channel_id=1, source_target_pairs={{0,20},{4,16},{8,28},{12,24},{16,4},{20,0},{24,12},{28,8},{1,21},{... | collective-permute-start | bytes 1179656 | tf_op jit(solution)/shard_map/ppermute | solution.py:491
  56.6 15.4 %collective-permute-done.1.rest_3_ = bf16[3,128,512]{2,1,0:T(8,128)(2,1)} collective-permute-done((bf16[3,128,512]{2,1,0:T(8,128)(2,1)}, bf16[3,128,512]{2,1,0:T(8,128)(2,1)}, u32[]{:S(2)}, u32[]{:S(2)}) %collective-permute-start.1) | collective-permute-done | bytes 393248 | tf_op jit(solution)/shard_map/ppermute | solution.py:491
  72.0 1.9 collective-permute-start.5
  74.0 7.8 %collective-permute-done.2.rest_4_ = bf16[3,128,512]{2,1,0:T(8,128)(2,1)} collective-permute-done((bf16[3,128,512]{2,1,0:T(8,128)(2,1)}, bf16[3,128,512]{2,1,0:T(8,128)(2,1)}, u32[]{:S(2)}, u32[]{:S(2)}) %collective-permute-start.2) | collective-permute-done | bytes 393248 | tf_op jit(solution)/shard_map/ppermute | solution.py:491
  83.3 37.3 %collective-permute-done.3.rest_5_ = bf16[3,128,512]{2,1,0:T(8,128)(2,1)} collective-permute-done((bf16[3,128,512]{2,1,0:T(8,128)(2,1)}, bf16[3,128,512]{2,1,0:T(8,128)(2,1)}, u32[]{:S(2)}, u32[]{:S(2)}) %collective-permute-start.3) | collective-permute-done | bytes 393248 | tf_op jit(solution)/shard_map/ppermute | solution.py:491
  122.7 14.6 %attend.3 = bf16[8,512,128]{2,1,0:T(8,128)(2,1)} custom-call(s32[2]{0:T(128)} %pad_add_fusion.3.me_ref, s32[384]{0:T(512)} %squeeze.22.rand_ref, s32[2]{0:T(128)} %bitcast.19, f32[64,8,2]{2,1,0:T(8,128)} %get-tuple-element.67.rest_0_, bf16[8,3,128,512]{3,2,1,0:T(8,128)(2,1)} %copy-done.2), custom_call_target="tpu_custom_call" | custom-call | flops 15000000512 | bytes 4000000 | tf_op jit(solution)/shard_map/attend/pallas_call | solution.py:335
  137.4 7.4 %all-to-all-start.1 = ((bf16[8,512,128]{2,1,0:T(8,128)(2,1)}), bf16[8,512,128]{2,1,0:T(8,128)(2,1)S(1)}, u32[]{:S(2)}, u32[]{:S(2)}) async-start(bf16[8,512,128]{2,1,0:T(8,128)(2,1)} %attend.3), calls=%async_computation.1 | async-start | bytes 2097152 | tf_op jit(solution)/shard_map/all_to_all | solution.py:488
  145.7 2.7 %collective-permute-done.6.rest_8_ = bf16[3,128,512]{2,1,0:T(8,128)(2,1)} collective-permute-done((bf16[3,128,512]{2,1,0:T(8,128)(2,1)}, bf16[3,128,512]{2,1,0:T(8,128)(2,1)}, u32[]{:S(2)}, u32[]{:S(2)}) %collective-permute-start.6) | collective-permute-done | bytes 393248 | tf_op jit(solution)/shard_map/ppermute | solution.py:491
  148.3 14.7 %attend.2 = (bf16[512,128]{1,0:T(8,128)(2,1)}, bf16[512,128]{1,0:T(8,128)(2,1)}, bf16[512,128]{1,0:T(8,128)(2,1)}, bf16[512,128]{1,0:T(8,128)(2,1)}, bf16[512,12...) custom-call(s32[2]{0:T(128)} %pad_add_fusion.3.me_ref, ...), custom_call_target="tpu_custom_call" | custom-call | flops 15000000512 | bytes 4000000 | tf_op jit(solution)/shard_map/attend/pallas_call | solution.py:335
  163.2 3.4 %collective-permute-start.16 = (bf16[512,128]{1,0:T(8,128)(2,1)}, bf16[512,128]{1,0:T(8,128)(2,1)S(1)}, u32[]{:S(2)}, u32[]{:S(2)}) collective-permute-start(bf16[512,128]{1,0:T(8,128)(2,1)} %get-tuple-element.60), channel_id=1, source_target_pairs={{0,12},{4,8},{8,4},{12,0},{16,28},{20,24},{24,20},{28,16},{1,13},{... | collective-permute-start | bytes 393224 | tf_op jit(solution)/shard_map/ppermute | solution.py:491
  166.6 2.6 %collective-permute-start.10 = (bf16[512,128]{1,0:T(8,128)(2,1)}, bf16[512,128]{1,0:T(8,128)(2,1)S(1)}, u32[]{:S(2)}, u32[]{:S(2)}) collective-permute-start(bf16[512,128]{1,0:T(8,128)(2,1)} %get-tuple-element.53), channel_id=1, source_target_pairs={{0,16},{4,20},{8,24},{12,28},{16,0},{20,4},{24,8},{28,12},{1,17},{... | collective-permute-start | bytes 393224 | tf_op jit(solution)/shard_map/ppermute | solution.py:491
  170.1 2.6 %collective-permute-done.14.rest_2_ = bf16[512,128]{1,0:T(8,128)(2,1)S(1)} collective-permute-done((bf16[512,128]{1,0:T(8,128)(2,1)}, bf16[512,128]{1,0:T(8,128)(2,1)S(1)}, u32[]{:S(2)}, u32[]{:S(2)}) %collective-permute-start.14) | collective-permute-done | bytes 131104 | tf_op jit(solution)/shard_map/ppermute | solution.py:491
  173.6 2.2 %collective-permute-done.15.rest_3_ = bf16[512,128]{1,0:T(8,128)(2,1)S(1)} collective-permute-done((bf16[512,128]{1,0:T(8,128)(2,1)}, bf16[512,128]{1,0:T(8,128)(2,1)S(1)}, u32[]{:S(2)}, u32[]{:S(2)}) %collective-permute-start.15) | collective-permute-done | bytes 131104 | tf_op jit(solution)/shard_map/ppermute | solution.py:491
  175.8 2.7 %collective-permute-done.16.rest_4_ = bf16[512,128]{1,0:T(8,128)(2,1)S(1)} collective-permute-done((bf16[512,128]{1,0:T(8,128)(2,1)}, bf16[512,128]{1,0:T(8,128)(2,1)S(1)}, u32[]{:S(2)}, u32[]{:S(2)}) %collective-permute-start.16) | collective-permute-done | bytes 131104 | tf_op jit(solution)/shard_map/ppermute | solution.py:491
  179.4 7.8 %project_early.1 = (f32[1,512,2048]{2,1,0:T(8,128)S(1)}, bf16[512,2048]{1,0:T(8,128)(2,1)S(1)}) custom-call(s32[2]{0:T(128)S(1)} %copy-done, bf16[8,512,128]{2,1,0:T(8,128)(2,1)S(1)} %all-to-all-done.1.rest_0_, bf16[512,128]{1,0:T(8,128)(2,1)S(1)} %copy-done.1, bf16[512,128]{1,0:T(8,128)(2,1)S(1)} %collective-permute-done.14.rest_2_, ...), custom_call_target="tpu_custom_call" | custom-call | flops 3221225472 | bytes 10000000 | tf_op jit(solution)/shard_map/project_early/pallas_call | solution.py:422
  187.3 3.7 %collective-permute-done.12.rest_2_ = bf16[512,128]{1,0:T(8,128)(2,1)S(1)} collective-permute-done((bf16[512,128]{1,0:T(8,128)(2,1)}, bf16[512,128]{1,0:T(8,128)(2,1)S(1)}, u32[]{:S(2)}, u32[]{:S(2)}) %collective-permute-start.12) | collective-permute-done | bytes 131104 | tf_op jit(solution)/shard_map/ppermute | solution.py:491
  190.9 2.5 %collective-permute-done.13.rest_3_ = bf16[512,128]{1,0:T(8,128)(2,1)S(1)} collective-permute-done((bf16[512,128]{1,0:T(8,128)(2,1)}, bf16[512,128]{1,0:T(8,128)(2,1)S(1)}, u32[]{:S(2)}, u32[]{:S(2)}) %collective-permute-start.13) | collective-permute-done | bytes 131104 | tf_op jit(solution)/shard_map/ppermute | solution.py:491
  193.5 3.3 %project_late.1 = bf16[1,512,2048]{2,1,0:T(8,128)(2,1)} custom-call(s32[2]{0:T(128)S(1)} %copy-done, bf16[512,128]{1,0:T(8,128)(2,1)S(1)} %collective-permute-done.10.rest_0_, bf16[512,128]{1,0:T(8,128)(2,1)S(1)} %collective-permute-done.11.rest_1_, bf16[512,128]{1,0:T(8,128)(2,1)S(1)} %collective-permute-done.12.rest_2_, ...), custom_call_target="tpu_custom_call" | custom-call | flops 1073741824 | bytes 10000000 | tf_op jit(solution)/shard_map/project_late/pallas_call | solution.py:452
  (58 shorter events, 15.9 us)
Async XLA Ops:
  3.8 117.3 %all-to-all-start = ((bf16[8,3,128,512]{3,2,1,0:T(8,128)(2,1)}), bf16[8,3,128,512]{3,2,1,0:T(8,128)(2,1)S(1)}, u32[]{:S(2)}, u32[]{:S(2)}) async-start(bf16[8,3,128,512]{3,2,1,0:T(8,128)(2,1)} %cut.1), calls=%async_computation | async-start | bytes 6291456 | tf_op jit(solution)/shard_map/all_to_all | solution.py:488
  10.7 42.7 %copy-start.3 = (s32[1,4,64,3]{2,1,3,0:T(4,128)S(1)}, s32[1,4,64,3]{2,1,3,0:T(4,128)}, u32[]{:S(2)}) copy-start(s32[1,4,64,3]{2,1,3,0:T(4,128)} %param.9) | copy-start | bytes 9220
  10.7 42.7 %copy-start.6 = (s32[1,2]{1,0:T(1,128)S(1)}, s32[1,2]{1,0:T(1,128)}, u32[]{:S(2)}) copy-start(s32[1,2]{1,0:T(1,128)} %param.10) | copy-start | bytes 28
  14.5 29.2 %collective-permute-start = (bf16[3,128,512]{2,1,0:T(8,128)(2,1)}, bf16[3,128,512]{2,1,0:T(8,128)(2,1)S(1)}, u32[]{:S(2)}, u32[]{:S(2)}) collective-permute-start(bf16[3,128,512]{2,1,0:T(8,128)(2,1)} %get-tuple-element.37), channel_id=1, source_target_pairs={{0,4},{4,0},{8,12},{12,8},{16,20},{20,16},{24,28},{28,24},{1,5},{5... | collective-permute-start | bytes 1179656 | tf_op jit(solution)/shard_map/ppermute | solution.py:491
  43.7 9.6 %copy-start.4 = (bf16[3,128,512]{2,1,0:T(8,128)(2,1)}, bf16[3,128,512]{2,1,0:T(8,128)(2,1)S(1)}, u32[]{:S(2)}) copy-start(bf16[3,128,512]{2,1,0:T(8,128)(2,1)S(1)} %collective-permute-done.rest_2_) | copy-start | bytes 1179652
  43.7 76.8 %collective-permute-start.8 = (bf16[512,2048]{1,0:T(8,128)(2,1)}, bf16[512,2048]{1,0:T(8,128)(2,1)}, u32[]{:S(2)}, u32[]{:S(2)}) collective-permute-start(bf16[512,2048]{1,0:T(8,128)(2,1)} %rest_5_), channel_id=1, source_target_pairs={{0,2},{1,3},{2,0},{3,1},{4,6},{5,7},{6,4},{7,5},{8,10},{9,11},{10,... | collective-permute-start | bytes 6291464 | tf_op jit(solution)/shard_map/ppermute | solution.py:474
  45.2 26.8 %collective-permute-start.1 = (bf16[3,128,512]{2,1,0:T(8,128)(2,1)}, bf16[3,128,512]{2,1,0:T(8,128)(2,1)}, u32[]{:S(2)}, u32[]{:S(2)}) collective-permute-start(bf16[3,128,512]{2,1,0:T(8,128)(2,1)} %get-tuple-element.38), channel_id=1, source_target_pairs={{0,8},{4,12},{8,0},{12,4},{16,24},{20,28},{24,16},{28,20},{1,9},{5... | collective-permute-start | bytes 1179656 | tf_op jit(solution)/shard_map/ppermute | solution.py:491
  46.8 35.0 %collective-permute-start.2 = (bf16[3,128,512]{2,1,0:T(8,128)(2,1)}, bf16[3,128,512]{2,1,0:T(8,128)(2,1)}, u32[]{:S(2)}, u32[]{:S(2)}) collective-permute-start(bf16[3,128,512]{2,1,0:T(8,128)(2,1)} %get-tuple-element.39), channel_id=1, source_target_pairs={{0,12},{4,8},{8,4},{12,0},{16,28},{20,24},{24,20},{28,16},{1,13},{... | collective-permute-start | bytes 1179656 | tf_op jit(solution)/shard_map/ppermute | solution.py:491
  49.1 71.5 %collective-permute-start.3 = (bf16[3,128,512]{2,1,0:T(8,128)(2,1)}, bf16[3,128,512]{2,1,0:T(8,128)(2,1)}, u32[]{:S(2)}, u32[]{:S(2)}) collective-permute-start(bf16[3,128,512]{2,1,0:T(8,128)(2,1)} %get-tuple-element.40), channel_id=1, source_target_pairs={{0,16},{4,20},{8,24},{12,28},{16,0},{20,4},{24,8},{28,12},{1,17},{... | collective-permute-start | bytes 1179656 | tf_op jit(solution)/shard_map/ppermute | solution.py:491
  51.2 94.5 %collective-permute-start.4 = (bf16[3,128,512]{2,1,0:T(8,128)(2,1)}, bf16[3,128,512]{2,1,0:T(8,128)(2,1)}, u32[]{:S(2)}, u32[]{:S(2)}) collective-permute-start(bf16[3,128,512]{2,1,0:T(8,128)(2,1)} %get-tuple-element.41), channel_id=1, source_target_pairs={{0,20},{4,16},{8,28},{12,24},{16,4},{20,0},{24,12},{28,8},{1,21},{... | collective-permute-start | bytes 1179656 | tf_op jit(solution)/shard_map/ppermute | solution.py:491
  72.0 73.6 %collective-permute-start.5 = (bf16[3,128,512]{2,1,0:T(8,128)(2,1)}, bf16[3,128,512]{2,1,0:T(8,128)(2,1)S(1)}, u32[]{:S(2)}, u32[]{:S(2)}) collective-permute-start(bf16[3,128,512]{2,1,0:T(8,128)(2,1)} %get-tuple-element.42), channel_id=1, source_target_pairs={{0,24},{4,28},{8,16},{12,20},{16,8},{20,12},{24,0},{28,4},{1,25},{... | collective-permute-start | bytes 1179656 | tf_op jit(solution)/shard_map/ppermute | solution.py:491
  81.7 66.6 %collective-permute-start.6 = (bf16[3,128,512]{2,1,0:T(8,128)(2,1)}, bf16[3,128,512]{2,1,0:T(8,128)(2,1)}, u32[]{:S(2)}, u32[]{:S(2)}) collective-permute-start(bf16[3,128,512]{2,1,0:T(8,128)(2,1)} %get-tuple-element.43), channel_id=1, source_target_pairs={{0,28},{4,24},{8,20},{12,16},{16,12},{20,8},{24,4},{28,0},{1,29},{... | collective-permute-start | bytes 1179656 | tf_op jit(solution)/shard_map/ppermute | solution.py:491
  120.6 42.5 %collective-permute-start.7 = (bf16[512,2048]{1,0:T(8,128)(2,1)}, bf16[512,2048]{1,0:T(8,128)(2,1)}, u32[]{:S(2)}, u32[]{:S(2)}) collective-permute-start(bf16[512,2048]{1,0:T(8,128)(2,1)} %rest_5_), channel_id=1, source_target_pairs={{0,1},{1,0},{2,3},{3,2},{4,5},{5,4},{6,7},{7,6},{8,9},{9,8},{10,11... | collective-permute-start | bytes 6291464 | tf_op jit(solution)/shard_map/ppermute | solution.py:474
  120.6 42.5 %collective-permute-start.9 = (bf16[512,2048]{1,0:T(8,128)(2,1)}, bf16[512,2048]{1,0:T(8,128)(2,1)}, u32[]{:S(2)}, u32[]{:S(2)}) collective-permute-start(bf16[512,2048]{1,0:T(8,128)(2,1)} %collective-permute-done.8.rest_7_), channel_id=1, source_target_pairs={{0,1},{1,0},{2,3},{3,2},{4,5},{5,4},{6,7},{7,6},{8,9},{9,8},{10,11... | collective-permute-start | bytes 6291464 | tf_op jit(solution)/shard_map/ppermute | solution.py:474
  137.4 41.1 %all-to-all-start.1 = ((bf16[8,512,128]{2,1,0:T(8,128)(2,1)}), bf16[8,512,128]{2,1,0:T(8,128)(2,1)S(1)}, u32[]{:S(2)}, u32[]{:S(2)}) async-start(bf16[8,512,128]{2,1,0:T(8,128)(2,1)} %attend.3), calls=%async_computation.1 | async-start | bytes 2097152 | tf_op jit(solution)/shard_map/all_to_all | solution.py:488
  145.7 2.7 %copy-start.5 = (bf16[3,128,512]{2,1,0:T(8,128)(2,1)}, bf16[3,128,512]{2,1,0:T(8,128)(2,1)S(1)}, u32[]{:S(2)}) copy-start(bf16[3,128,512]{2,1,0:T(8,128)(2,1)S(1)} %collective-permute-done.5.rest_7_) | copy-start | bytes 1179652
  148.3 30.2 %copy-start = (s32[2]{0:T(128)S(1)}, s32[2]{0:T(128)}, u32[]{:S(2)}) copy-start(s32[2]{0:T(128)} %pad_add_fusion.3.me_ref) | copy-start | bytes 28
  163.1 9.6 %collective-permute-start.14 = (bf16[512,128]{1,0:T(8,128)(2,1)}, bf16[512,128]{1,0:T(8,128)(2,1)S(1)}, u32[]{:S(2)}, u32[]{:S(2)}) collective-permute-start(bf16[512,128]{1,0:T(8,128)(2,1)} %get-tuple-element.58), channel_id=1, source_target_pairs={{0,4},{4,0},{8,12},{12,8},{16,20},{20,16},{24,28},{28,24},{1,5},{5... | collective-permute-start | bytes 393224 | tf_op jit(solution)/shard_map/ppermute | solution.py:491
  163.2 12.6 %collective-permute-start.15 = (bf16[512,128]{1,0:T(8,128)(2,1)}, bf16[512,128]{1,0:T(8,128)(2,1)S(1)}, u32[]{:S(2)}, u32[]{:S(2)}) collective-permute-start(bf16[512,128]{1,0:T(8,128)(2,1)} %get-tuple-element.59), channel_id=1, source_target_pairs={{0,8},{4,12},{8,0},{12,4},{16,24},{20,28},{24,16},{28,20},{1,9},{5... | collective-permute-start | bytes 393224 | tf_op jit(solution)/shard_map/ppermute | solution.py:491
  163.2 15.3 %collective-permute-start.16 = (bf16[512,128]{1,0:T(8,128)(2,1)}, bf16[512,128]{1,0:T(8,128)(2,1)S(1)}, u32[]{:S(2)}, u32[]{:S(2)}) collective-permute-start(bf16[512,128]{1,0:T(8,128)(2,1)} %get-tuple-element.60), channel_id=1, source_target_pairs={{0,12},{4,8},{8,4},{12,0},{16,28},{20,24},{24,20},{28,16},{1,13},{... | collective-permute-start | bytes 393224 | tf_op jit(solution)/shard_map/ppermute | solution.py:491
  166.6 20.6 %collective-permute-start.10 = (bf16[512,128]{1,0:T(8,128)(2,1)}, bf16[512,128]{1,0:T(8,128)(2,1)S(1)}, u32[]{:S(2)}, u32[]{:S(2)}) collective-permute-start(bf16[512,128]{1,0:T(8,128)(2,1)} %get-tuple-element.53), channel_id=1, source_target_pairs={{0,16},{4,20},{8,24},{12,28},{16,0},{20,4},{24,8},{28,12},{1,17},{... | collective-permute-start | bytes 393224 | tf_op jit(solution)/shard_map/ppermute | solution.py:491
  169.2 18.1 %collective-permute-start.11 = (bf16[512,128]{1,0:T(8,128)(2,1)}, bf16[512,128]{1,0:T(8,128)(2,1)S(1)}, u32[]{:S(2)}, u32[]{:S(2)}) collective-permute-start(bf16[512,128]{1,0:T(8,128)(2,1)} %get-tuple-element.54), channel_id=1, source_target_pairs={{0,20},{4,16},{8,28},{12,24},{16,4},{20,0},{24,12},{28,8},{1,21},{... | collective-permute-start | bytes 393224 | tf_op jit(solution)/shard_map/ppermute | solution.py:491
  172.7 18.2 %collective-permute-start.12 = (bf16[512,128]{1,0:T(8,128)(2,1)}, bf16[512,128]{1,0:T(8,128)(2,1)S(1)}, u32[]{:S(2)}, u32[]{:S(2)}) collective-permute-start(bf16[512,128]{1,0:T(8,128)(2,1)} %get-tuple-element.55), channel_id=1, source_target_pairs={{0,24},{4,28},{8,16},{12,20},{16,8},{20,12},{24,0},{28,4},{1,25},{... | collective-permute-start | bytes 393224 | tf_op jit(solution)/shard_map/ppermute | solution.py:491
  175.8 17.7 %collective-permute-start.13 = (bf16[512,128]{1,0:T(8,128)(2,1)}, bf16[512,128]{1,0:T(8,128)(2,1)S(1)}, u32[]{:S(2)}, u32[]{:S(2)}) collective-permute-start(bf16[512,128]{1,0:T(8,128)(2,1)} %get-tuple-element.56), channel_id=1, source_target_pairs={{0,28},{4,24},{8,20},{12,16},{16,12},{20,8},{24,4},{28,0},{1,29},{... | collective-permute-start | bytes 393224 | tf_op jit(solution)/shard_map/ppermute | solution.py:491
  (2 other events, 2.5 us)

commit v7 on v6

--- a/solution.py
+++ b/solution.py
@@ -358,7 +358,7 @@
     arrays = sorted({i for i, _, _ in slots})
     pieces, rest = rest[: len(arrays)], rest[len(arrays) :]
     if before:
-        before_ref, w, o_ref, a, a_sems = rest
+        before_ref, w, o_ref, a, a_sems, done, out_sems = rest
     else:
         weights, rest = rest[:ndp], rest[ndp:]
         o_ref, ahead_ref, a, w, a_sems, w_sems, ahead_sems = rest
@@ -372,6 +372,10 @@
         src = src.at[me ^ k] if len(src.shape) == 3 else src
         dst = a.at[:, pl.ds(slot * PAIR, PAIR)]
         return pltpu.make_async_copy(src, dst, a_sems.at[slot])
+
+    def out_copy(t):
+        columns = pl.ds(t * tile, tile)
+        return pltpu.make_async_copy(done.at[:, columns], o_ref.at[0, :, columns], out_sems.at[t])
 
     for slot in range(len(slots)):
         piece_copy(slot).start()
@@ -407,8 +411,15 @@
         total = jnp.dot(a[...], w[:, columns], preferred_element_type=jnp.float32)
         if before:
             total = total + before_ref[0, :, columns]
-        o_ref[0, :, columns] = total.astype(o_ref.dtype)
-    if not before:
+        if before:
+            done[:, columns] = total.astype(o_ref.dtype)
+            out_copy(t).start()
+        else:
+            o_ref[0, :, columns] = total
+    if before:
+        for t in range(4):
+            out_copy(t).wait()
+    else:
         for slot in range(len(ahead)):
             weight_copy(ahead, slot, 0).wait()
 
@@ -453,10 +464,12 @@
         functools.partial(project_kernel, n, 0, slots, [], True),
         out_shape=jax.ShapeDtypeStruct((1, shard, width), jnp.bfloat16),
         in_specs=[pl.BlockSpec(memory_space=pltpu.SMEM)] + [hbm] * len(pieces) + [vmem, vmem],
-        out_specs=vmem,
+        out_specs=hbm,
         scratch_shapes=[
             pltpu.VMEM((shard, depth), jnp.bfloat16),
             pltpu.SemaphoreType.DMA((len(slots),)),
+            pltpu.VMEM((shard, width), jnp.bfloat16),
+            pltpu.SemaphoreType.DMA((4,)),
         ],
         compiler_params=pltpu.CompilerParams(vmem_limit_bytes=24 * 1024 * 1024),
         cost_estimate=pl.CostEstimate(

time: 197 us -> 197 us (level)
  no operation moved by 1% of the time
where the time goes in v7:
time: 197 us; the launch traced here: 196 us
  waiting for transfers between devices  105 us (53%)
  Pallas kernels  47.5 us (24%)
  starting transfers between devices  36.8 us (19%)
  local copies, waits for them, and re-layouts  6.2 us (3%)
    ppermute x14, waiting for transfers between devices, swap(): lax.ppermute(arrays[k], 'seq', [(i, i ^ k) for i in range(n)])  105 us
    pallas_call x2, Pallas kernels, attend(): pl.pallas_call(functools.partial(attend_kernel, n, nblocks, apart_in, apa...  29.3 us
    ppermute x14, starting transfers between devices, swap(): lax.ppermute(arrays[k], 'seq', [(i, i ^ k) for i in range(n)])  21.1 us
    all_to_all x2, starting transfers between devices, exchange(): return lax.all_to_all(x, 'seq', split_axis=0, concat_axis=0, tiled=True)  13.7 us
    pallas_call x1, Pallas kernels, project_early(): pl.pallas_call(functools.partial(project_kernel, n, ndp, slots, ahead, Fa...  7.83 us
  transfers between devices with their start and end apart: 19, of which 10 were waited for; matrix products, arithmetic and copies ran while one was open for 2% of the time, Pallas kernels for 21%

profile of v7, /device:TPU:8, one launch (start us, length us, event | category | flops | bytes accessed | tf_op | source)
XLA Modules:
  0.0 196.4 jit_solution(14767325376526631462)
XLA Ops:
  0.0 3.8 %cut.1 = bf16[8,3,128,512]{3,2,1,0:T(8,128)(2,1)} custom-call(bf16[1,2048,512]{2,1,0:T(8,128)(2,1)} %q_ref.3, bf16[1,2048,512]{2,1,0:T(8,128)(2,1)} %k_ref.3, bf16[1,2048,512]{2,1,0:T(8,128)(2,1)} %v_ref.3), custom_call_target="tpu_custom_call" | custom-call | tf_op jit(solution)/shard_map/cut/pallas_call | solution.py:125
  3.8 6.3 %all-to-all-start = ((bf16[8,3,128,512]{3,2,1,0:T(8,128)(2,1)}), bf16[8,3,128,512]{3,2,1,0:T(8,128)(2,1)S(1)}, u32[]{:S(2)}, u32[]{:S(2)}) async-start(bf16[8,3,128,512]{3,2,1,0:T(8,128)(2,1)} %cut.1), calls=%async_computation | async-start | bytes 6291456 | tf_op jit(solution)/shard_map/all_to_all | solution.py:501
  10.7 3.8 %cut_apart.1 = (bf16[3,128,512]{2,1,0:T(8,128)(2,1)}, bf16[3,128,512]{2,1,0:T(8,128)(2,1)}, bf16[3,128,512]{2,1,0:T(8,128)(2,1)}, bf16[3,128,512]{2,1,0:T(8,128)...) custom-call(s32[2]{0:T(128)} %pad_add_fusion.3.me_ref, ...), custom_call_target="tpu_custom_call" | custom-call | tf_op jit(solution)/shard_map/cut_apart/pallas_call | solution.py:166
  16.1 27.7 %collective-permute-done.rest_2_ = bf16[3,128,512]{2,1,0:T(8,128)(2,1)S(1)} collective-permute-done((bf16[3,128,512]{2,1,0:T(8,128)(2,1)}, bf16[3,128,512]{2,1,0:T(8,128)(2,1)S(1)}, u32[]{:S(2)}, u32[]{:S(2)}) %collective-permute-start) | collective-permute-done | bytes 393248 | tf_op jit(solution)/shard_map/ppermute | solution.py:504
  46.8 2.3 %collective-permute-start.2 = (bf16[3,128,512]{2,1,0:T(8,128)(2,1)}, bf16[3,128,512]{2,1,0:T(8,128)(2,1)}, u32[]{:S(2)}, u32[]{:S(2)}) collective-permute-start(bf16[3,128,512]{2,1,0:T(8,128)(2,1)} %get-tuple-element.39), channel_id=1, source_target_pairs={{0,12},{4,8},{8,4},{12,0},{16,28},{20,24},{24,20},{28,16},{1,13},{... | collective-permute-start | bytes 1179656 | tf_op jit(solution)/shard_map/ppermute | solution.py:504
  49.1 2.1 %collective-permute-start.3 = (bf16[3,128,512]{2,1,0:T(8,128)(2,1)}, bf16[3,128,512]{2,1,0:T(8,128)(2,1)}, u32[]{:S(2)}, u32[]{:S(2)}) collective-permute-start(bf16[3,128,512]{2,1,0:T(8,128)(2,1)} %get-tuple-element.40), channel_id=1, source_target_pairs={{0,16},{4,20},{8,24},{12,28},{16,0},{20,4},{24,8},{28,12},{1,17},{... | collective-permute-start | bytes 1179656 | tf_op jit(solution)/shard_map/ppermute | solution.py:504
  51.2 2.2 %collective-permute-start.4 = (bf16[3,128,512]{2,1,0:T(8,128)(2,1)}, bf16[3,128,512]{2,1,0:T(8,128)(2,1)}, u32[]{:S(2)}, u32[]{:S(2)}) collective-permute-start(bf16[3,128,512]{2,1,0:T(8,128)(2,1)} %get-tuple-element.41), channel_id=1, source_target_pairs={{0,20},{4,16},{8,28},{12,24},{16,4},{20,0},{24,12},{28,8},{1,21},{... | collective-permute-start | bytes 1179656 | tf_op jit(solution)/shard_map/ppermute | solution.py:504
  56.6 15.4 %collective-permute-done.1.rest_3_ = bf16[3,128,512]{2,1,0:T(8,128)(2,1)} collective-permute-done((bf16[3,128,512]{2,1,0:T(8,128)(2,1)}, bf16[3,128,512]{2,1,0:T(8,128)(2,1)}, u32[]{:S(2)}, u32[]{:S(2)}) %collective-permute-start.1) | collective-permute-done | bytes 393248 | tf_op jit(solution)/shard_map/ppermute | solution.py:504
  72.0 1.9 collective-permute-start.5
  74.0 7.8 %collective-permute-done.2.rest_4_ = bf16[3,128,512]{2,1,0:T(8,128)(2,1)} collective-permute-done((bf16[3,128,512]{2,1,0:T(8,128)(2,1)}, bf16[3,128,512]{2,1,0:T(8,128)(2,1)}, u32[]{:S(2)}, u32[]{:S(2)}) %collective-permute-start.2) | collective-permute-done | bytes 393248 | tf_op jit(solution)/shard_map/ppermute | solution.py:504
  83.3 37.3 %collective-permute-done.3.rest_5_ = bf16[3,128,512]{2,1,0:T(8,128)(2,1)} collective-permute-done((bf16[3,128,512]{2,1,0:T(8,128)(2,1)}, bf16[3,128,512]{2,1,0:T(8,128)(2,1)}, u32[]{:S(2)}, u32[]{:S(2)}) %collective-permute-start.3) | collective-permute-done | bytes 393248 | tf_op jit(solution)/shard_map/ppermute | solution.py:504
  122.7 14.6 %attend.3 = bf16[8,512,128]{2,1,0:T(8,128)(2,1)} custom-call(s32[2]{0:T(128)} %pad_add_fusion.3.me_ref, s32[384]{0:T(512)} %squeeze.22.rand_ref, s32[2]{0:T(128)} %bitcast.19, f32[64,8,2]{2,1,0:T(8,128)} %get-tuple-element.67.rest_0_, bf16[8,3,128,512]{3,2,1,0:T(8,128)(2,1)} %copy-done.2), custom_call_target="tpu_custom_call" | custom-call | flops 15000000512 | bytes 4000000 | tf_op jit(solution)/shard_map/attend/pallas_call | solution.py:335
  137.4 7.4 %all-to-all-start.1 = ((bf16[8,512,128]{2,1,0:T(8,128)(2,1)}), bf16[8,512,128]{2,1,0:T(8,128)(2,1)S(1)}, u32[]{:S(2)}, u32[]{:S(2)}) async-start(bf16[8,512,128]{2,1,0:T(8,128)(2,1)} %attend.3), calls=%async_computation.1 | async-start | bytes 2097152 | tf_op jit(solution)/shard_map/all_to_all | solution.py:501
  145.7 2.7 %collective-permute-done.6.rest_8_ = bf16[3,128,512]{2,1,0:T(8,128)(2,1)} collective-permute-done((bf16[3,128,512]{2,1,0:T(8,128)(2,1)}, bf16[3,128,512]{2,1,0:T(8,128)(2,1)}, u32[]{:S(2)}, u32[]{:S(2)}) %collective-permute-start.6) | collective-permute-done | bytes 393248 | tf_op jit(solution)/shard_map/ppermute | solution.py:504
  148.3 14.7 %attend.2 = (bf16[512,128]{1,0:T(8,128)(2,1)}, bf16[512,128]{1,0:T(8,128)(2,1)}, bf16[512,128]{1,0:T(8,128)(2,1)}, bf16[512,128]{1,0:T(8,128)(2,1)}, bf16[512,12...) custom-call(s32[2]{0:T(128)} %pad_add_fusion.3.me_ref, ...), custom_call_target="tpu_custom_call" | custom-call | flops 15000000512 | bytes 4000000 | tf_op jit(solution)/shard_map/attend/pallas_call | solution.py:335
  163.2 3.4 %collective-permute-start.16 = (bf16[512,128]{1,0:T(8,128)(2,1)}, bf16[512,128]{1,0:T(8,128)(2,1)S(1)}, u32[]{:S(2)}, u32[]{:S(2)}) collective-permute-start(bf16[512,128]{1,0:T(8,128)(2,1)} %get-tuple-element.60), channel_id=1, source_target_pairs={{0,12},{4,8},{8,4},{12,0},{16,28},{20,24},{24,20},{28,16},{1,13},{... | collective-permute-start | bytes 393224 | tf_op jit(solution)/shard_map/ppermute | solution.py:504
  166.6 2.6 %collective-permute-start.10 = (bf16[512,128]{1,0:T(8,128)(2,1)}, bf16[512,128]{1,0:T(8,128)(2,1)S(1)}, u32[]{:S(2)}, u32[]{:S(2)}) collective-permute-start(bf16[512,128]{1,0:T(8,128)(2,1)} %get-tuple-element.53), channel_id=1, source_target_pairs={{0,16},{4,20},{8,24},{12,28},{16,0},{20,4},{24,8},{28,12},{1,17},{... | collective-permute-start | bytes 393224 | tf_op jit(solution)/shard_map/ppermute | solution.py:504
  170.1 2.6 %collective-permute-done.14.rest_2_ = bf16[512,128]{1,0:T(8,128)(2,1)S(1)} collective-permute-done((bf16[512,128]{1,0:T(8,128)(2,1)}, bf16[512,128]{1,0:T(8,128)(2,1)S(1)}, u32[]{:S(2)}, u32[]{:S(2)}) %collective-permute-start.14) | collective-permute-done | bytes 131104 | tf_op jit(solution)/shard_map/ppermute | solution.py:504
  173.6 2.2 %collective-permute-done.15.rest_3_ = bf16[512,128]{1,0:T(8,128)(2,1)S(1)} collective-permute-done((bf16[512,128]{1,0:T(8,128)(2,1)}, bf16[512,128]{1,0:T(8,128)(2,1)S(1)}, u32[]{:S(2)}, u32[]{:S(2)}) %collective-permute-start.15) | collective-permute-done | bytes 131104 | tf_op jit(solution)/shard_map/ppermute | solution.py:504
  175.8 2.7 %collective-permute-done.16.rest_4_ = bf16[512,128]{1,0:T(8,128)(2,1)S(1)} collective-permute-done((bf16[512,128]{1,0:T(8,128)(2,1)}, bf16[512,128]{1,0:T(8,128)(2,1)S(1)}, u32[]{:S(2)}, u32[]{:S(2)}) %collective-permute-start.16) | collective-permute-done | bytes 131104 | tf_op jit(solution)/shard_map/ppermute | solution.py:504
  179.4 7.8 %project_early.1 = (f32[1,512,2048]{2,1,0:T(8,128)S(1)}, bf16[512,2048]{1,0:T(8,128)(2,1)S(1)}) custom-call(s32[2]{0:T(128)S(1)} %copy-done, bf16[8,512,128]{2,1,0:T(8,128)(2,1)S(1)} %all-to-all-done.1.rest_0_, bf16[512,128]{1,0:T(8,128)(2,1)S(1)} %copy-done.1, bf16[512,128]{1,0:T(8,128)(2,1)S(1)} %collective-permute-done.14.rest_2_, ...), custom_call_target="tpu_custom_call" | custom-call | flops 3221225472 | bytes 10000000 | tf_op jit(solution)/shard_map/project_early/pallas_call | solution.py:433
  187.3 3.7 %collective-permute-done.12.rest_2_ = bf16[512,128]{1,0:T(8,128)(2,1)S(1)} collective-permute-done((bf16[512,128]{1,0:T(8,128)(2,1)}, bf16[512,128]{1,0:T(8,128)(2,1)S(1)}, u32[]{:S(2)}, u32[]{:S(2)}) %collective-permute-start.12) | collective-permute-done | bytes 131104 | tf_op jit(solution)/shard_map/ppermute | solution.py:504
  190.9 2.5 %collective-permute-done.13.rest_3_ = bf16[512,128]{1,0:T(8,128)(2,1)S(1)} collective-permute-done((bf16[512,128]{1,0:T(8,128)(2,1)}, bf16[512,128]{1,0:T(8,128)(2,1)S(1)}, u32[]{:S(2)}, u32[]{:S(2)}) %collective-permute-start.13) | collective-permute-done | bytes 131104 | tf_op jit(solution)/shard_map/ppermute | solution.py:504
  193.5 2.8 %project_late.1 = bf16[1,512,2048]{2,1,0:T(8,128)(2,1)} custom-call(s32[2]{0:T(128)S(1)} %copy-done, bf16[512,128]{1,0:T(8,128)(2,1)S(1)} %collective-permute-done.10.rest_0_, bf16[512,128]{1,0:T(8,128)(2,1)S(1)} %collective-permute-done.11.rest_1_, bf16[512,128]{1,0:T(8,128)(2,1)S(1)} %collective-permute-done.12.rest_2_, ...), custom_call_target="tpu_custom_call" | custom-call | flops 1073741824 | bytes 10000000 | tf_op jit(solution)/shard_map/project_late/pallas_call | solution.py:463
  (58 shorter events, 15.9 us)
Async XLA Ops:
  3.8 117.3 %all-to-all-start = ((bf16[8,3,128,512]{3,2,1,0:T(8,128)(2,1)}), bf16[8,3,128,512]{3,2,1,0:T(8,128)(2,1)S(1)}, u32[]{:S(2)}, u32[]{:S(2)}) async-start(bf16[8,3,128,512]{3,2,1,0:T(8,128)(2,1)} %cut.1), calls=%async_computation | async-start | bytes 6291456 | tf_op jit(solution)/shard_map/all_to_all | solution.py:501
  10.7 42.7 %copy-start.3 = (s32[1,4,64,3]{2,1,3,0:T(4,128)S(1)}, s32[1,4,64,3]{2,1,3,0:T(4,128)}, u32[]{:S(2)}) copy-start(s32[1,4,64,3]{2,1,3,0:T(4,128)} %param.9) | copy-start | bytes 9220
  10.7 42.7 %copy-start.6 = (s32[1,2]{1,0:T(1,128)S(1)}, s32[1,2]{1,0:T(1,128)}, u32[]{:S(2)}) copy-start(s32[1,2]{1,0:T(1,128)} %param.10) | copy-start | bytes 28
  14.5 29.2 %collective-permute-start = (bf16[3,128,512]{2,1,0:T(8,128)(2,1)}, bf16[3,128,512]{2,1,0:T(8,128)(2,1)S(1)}, u32[]{:S(2)}, u32[]{:S(2)}) collective-permute-start(bf16[3,128,512]{2,1,0:T(8,128)(2,1)} %get-tuple-element.37), channel_id=1, source_target_pairs={{0,4},{4,0},{8,12},{12,8},{16,20},{20,16},{24,28},{28,24},{1,5},{5... | collective-permute-start | bytes 1179656 | tf_op jit(solution)/shard_map/ppermute | solution.py:504
  43.7 9.6 %copy-start.4 = (bf16[3,128,512]{2,1,0:T(8,128)(2,1)}, bf16[3,128,512]{2,1,0:T(8,128)(2,1)S(1)}, u32[]{:S(2)}) copy-start(bf16[3,128,512]{2,1,0:T(8,128)(2,1)S(1)} %collective-permute-done.rest_2_) | copy-start | bytes 1179652
  43.7 76.8 %collective-permute-start.8 = (bf16[512,2048]{1,0:T(8,128)(2,1)}, bf16[512,2048]{1,0:T(8,128)(2,1)}, u32[]{:S(2)}, u32[]{:S(2)}) collective-permute-start(bf16[512,2048]{1,0:T(8,128)(2,1)} %rest_5_), channel_id=1, source_target_pairs={{0,2},{1,3},{2,0},{3,1},{4,6},{5,7},{6,4},{7,5},{8,10},{9,11},{10,... | collective-permute-start | bytes 6291464 | tf_op jit(solution)/shard_map/ppermute | solution.py:487
  45.2 26.8 %collective-permute-start.1 = (bf16[3,128,512]{2,1,0:T(8,128)(2,1)}, bf16[3,128,512]{2,1,0:T(8,128)(2,1)}, u32[]{:S(2)}, u32[]{:S(2)}) collective-permute-start(bf16[3,128,512]{2,1,0:T(8,128)(2,1)} %get-tuple-element.38), channel_id=1, source_target_pairs={{0,8},{4,12},{8,0},{12,4},{16,24},{20,28},{24,16},{28,20},{1,9},{5... | collective-permute-start | bytes 1179656 | tf_op jit(solution)/shard_map/ppermute | solution.py:504
  46.8 35.0 %collective-permute-start.2 = (bf16[3,128,512]{2,1,0:T(8,128)(2,1)}, bf16[3,128,512]{2,1,0:T(8,128)(2,1)}, u32[]{:S(2)}, u32[]{:S(2)}) collective-permute-start(bf16[3,128,512]{2,1,0:T(8,128)(2,1)} %get-tuple-element.39), channel_id=1, source_target_pairs={{0,12},{4,8},{8,4},{12,0},{16,28},{20,24},{24,20},{28,16},{1,13},{... | collective-permute-start | bytes 1179656 | tf_op jit(solution)/shard_map/ppermute | solution.py:504
  49.1 71.5 %collective-permute-start.3 = (bf16[3,128,512]{2,1,0:T(8,128)(2,1)}, bf16[3,128,512]{2,1,0:T(8,128)(2,1)}, u32[]{:S(2)}, u32[]{:S(2)}) collective-permute-start(bf16[3,128,512]{2,1,0:T(8,128)(2,1)} %get-tuple-element.40), channel_id=1, source_target_pairs={{0,16},{4,20},{8,24},{12,28},{16,0},{20,4},{24,8},{28,12},{1,17},{... | collective-permute-start | bytes 1179656 | tf_op jit(solution)/shard_map/ppermute | solution.py:504
  51.2 94.5 %collective-permute-start.4 = (bf16[3,128,512]{2,1,0:T(8,128)(2,1)}, bf16[3,128,512]{2,1,0:T(8,128)(2,1)}, u32[]{:S(2)}, u32[]{:S(2)}) collective-permute-start(bf16[3,128,512]{2,1,0:T(8,128)(2,1)} %get-tuple-element.41), channel_id=1, source_target_pairs={{0,20},{4,16},{8,28},{12,24},{16,4},{20,0},{24,12},{28,8},{1,21},{... | collective-permute-start | bytes 1179656 | tf_op jit(solution)/shard_map/ppermute | solution.py:504
  72.0 73.6 %collective-permute-start.5 = (bf16[3,128,512]{2,1,0:T(8,128)(2,1)}, bf16[3,128,512]{2,1,0:T(8,128)(2,1)S(1)}, u32[]{:S(2)}, u32[]{:S(2)}) collective-permute-start(bf16[3,128,512]{2,1,0:T(8,128)(2,1)} %get-tuple-element.42), channel_id=1, source_target_pairs={{0,24},{4,28},{8,16},{12,20},{16,8},{20,12},{24,0},{28,4},{1,25},{... | collective-permute-start | bytes 1179656 | tf_op jit(solution)/shard_map/ppermute | solution.py:504
  81.7 66.6 %collective-permute-start.6 = (bf16[3,128,512]{2,1,0:T(8,128)(2,1)}, bf16[3,128,512]{2,1,0:T(8,128)(2,1)}, u32[]{:S(2)}, u32[]{:S(2)}) collective-permute-start(bf16[3,128,512]{2,1,0:T(8,128)(2,1)} %get-tuple-element.43), channel_id=1, source_target_pairs={{0,28},{4,24},{8,20},{12,16},{16,12},{20,8},{24,4},{28,0},{1,29},{... | collective-permute-start | bytes 1179656 | tf_op jit(solution)/shard_map/ppermute | solution.py:504
  120.6 42.5 %collective-permute-start.7 = (bf16[512,2048]{1,0:T(8,128)(2,1)}, bf16[512,2048]{1,0:T(8,128)(2,1)}, u32[]{:S(2)}, u32[]{:S(2)}) collective-permute-start(bf16[512,2048]{1,0:T(8,128)(2,1)} %rest_5_), channel_id=1, source_target_pairs={{0,1},{1,0},{2,3},{3,2},{4,5},{5,4},{6,7},{7,6},{8,9},{9,8},{10,11... | collective-permute-start | bytes 6291464 | tf_op jit(solution)/shard_map/ppermute | solution.py:487
  120.6 42.5 %collective-permute-start.9 = (bf16[512,2048]{1,0:T(8,128)(2,1)}, bf16[512,2048]{1,0:T(8,128)(2,1)}, u32[]{:S(2)}, u32[]{:S(2)}) collective-permute-start(bf16[512,2048]{1,0:T(8,128)(2,1)} %collective-permute-done.8.rest_7_), channel_id=1, source_target_pairs={{0,1},{1,0},{2,3},{3,2},{4,5},{5,4},{6,7},{7,6},{8,9},{9,8},{10,11... | collective-permute-start | bytes 6291464 | tf_op jit(solution)/shard_map/ppermute | solution.py:487
  137.4 41.1 %all-to-all-start.1 = ((bf16[8,512,128]{2,1,0:T(8,128)(2,1)}), bf16[8,512,128]{2,1,0:T(8,128)(2,1)S(1)}, u32[]{:S(2)}, u32[]{:S(2)}) async-start(bf16[8,512,128]{2,1,0:T(8,128)(2,1)} %attend.3), calls=%async_computation.1 | async-start | bytes 2097152 | tf_op jit(solution)/shard_map/all_to_all | solution.py:501
  145.7 2.7 %copy-start.5 = (bf16[3,128,512]{2,1,0:T(8,128)(2,1)}, bf16[3,128,512]{2,1,0:T(8,128)(2,1)S(1)}, u32[]{:S(2)}) copy-start(bf16[3,128,512]{2,1,0:T(8,128)(2,1)S(1)} %collective-permute-done.5.rest_7_) | copy-start | bytes 1179652
  148.3 30.2 %copy-start = (s32[2]{0:T(128)S(1)}, s32[2]{0:T(128)}, u32[]{:S(2)}) copy-start(s32[2]{0:T(128)} %pad_add_fusion.3.me_ref) | copy-start | bytes 28
  163.1 9.6 %collective-permute-start.14 = (bf16[512,128]{1,0:T(8,128)(2,1)}, bf16[512,128]{1,0:T(8,128)(2,1)S(1)}, u32[]{:S(2)}, u32[]{:S(2)}) collective-permute-start(bf16[512,128]{1,0:T(8,128)(2,1)} %get-tuple-element.58), channel_id=1, source_target_pairs={{0,4},{4,0},{8,12},{12,8},{16,20},{20,16},{24,28},{28,24},{1,5},{5... | collective-permute-start | bytes 393224 | tf_op jit(solution)/shard_map/ppermute | solution.py:504
  163.2 12.6 %collective-permute-start.15 = (bf16[512,128]{1,0:T(8,128)(2,1)}, bf16[512,128]{1,0:T(8,128)(2,1)S(1)}, u32[]{:S(2)}, u32[]{:S(2)}) collective-permute-start(bf16[512,128]{1,0:T(8,128)(2,1)} %get-tuple-element.59), channel_id=1, source_target_pairs={{0,8},{4,12},{8,0},{12,4},{16,24},{20,28},{24,16},{28,20},{1,9},{5... | collective-permute-start | bytes 393224 | tf_op jit(solution)/shard_map/ppermute | solution.py:504
  163.2 15.3 %collective-permute-start.16 = (bf16[512,128]{1,0:T(8,128)(2,1)}, bf16[512,128]{1,0:T(8,128)(2,1)S(1)}, u32[]{:S(2)}, u32[]{:S(2)}) collective-permute-start(bf16[512,128]{1,0:T(8,128)(2,1)} %get-tuple-element.60), channel_id=1, source_target_pairs={{0,12},{4,8},{8,4},{12,0},{16,28},{20,24},{24,20},{28,16},{1,13},{... | collective-permute-start | bytes 393224 | tf_op jit(solution)/shard_map/ppermute | solution.py:504
  166.6 20.6 %collective-permute-start.10 = (bf16[512,128]{1,0:T(8,128)(2,1)}, bf16[512,128]{1,0:T(8,128)(2,1)S(1)}, u32[]{:S(2)}, u32[]{:S(2)}) collective-permute-start(bf16[512,128]{1,0:T(8,128)(2,1)} %get-tuple-element.53), channel_id=1, source_target_pairs={{0,16},{4,20},{8,24},{12,28},{16,0},{20,4},{24,8},{28,12},{1,17},{... | collective-permute-start | bytes 393224 | tf_op jit(solution)/shard_map/ppermute | solution.py:504
  169.2 18.1 %collective-permute-start.11 = (bf16[512,128]{1,0:T(8,128)(2,1)}, bf16[512,128]{1,0:T(8,128)(2,1)S(1)}, u32[]{:S(2)}, u32[]{:S(2)}) collective-permute-start(bf16[512,128]{1,0:T(8,128)(2,1)} %get-tuple-element.54), channel_id=1, source_target_pairs={{0,20},{4,16},{8,28},{12,24},{16,4},{20,0},{24,12},{28,8},{1,21},{... | collective-permute-start | bytes 393224 | tf_op jit(solution)/shard_map/ppermute | solution.py:504
  172.7 18.2 %collective-permute-start.12 = (bf16[512,128]{1,0:T(8,128)(2,1)}, bf16[512,128]{1,0:T(8,128)(2,1)S(1)}, u32[]{:S(2)}, u32[]{:S(2)}) collective-permute-start(bf16[512,128]{1,0:T(8,128)(2,1)} %get-tuple-element.55), channel_id=1, source_target_pairs={{0,24},{4,28},{8,16},{12,20},{16,8},{20,12},{24,0},{28,4},{1,25},{... | collective-permute-start | bytes 393224 | tf_op jit(solution)/shard_map/ppermute | solution.py:504
  175.8 17.7 %collective-permute-start.13 = (bf16[512,128]{1,0:T(8,128)(2,1)}, bf16[512,128]{1,0:T(8,128)(2,1)S(1)}, u32[]{:S(2)}, u32[]{:S(2)}) collective-permute-start(bf16[512,128]{1,0:T(8,128)(2,1)} %get-tuple-element.56), channel_id=1, source_target_pairs={{0,28},{4,24},{8,20},{12,16},{16,12},{20,8},{24,4},{28,0},{1,29},{... | collective-permute-start | bytes 393224 | tf_op jit(solution)/shard_map/ppermute | solution.py:504
  (2 other events, 2.5 us)

commit v8 on v7

--- a/solution.py
+++ b/solution.py
@@ -186,6 +186,7 @@
     ins, rest = (rest[:n], rest[n:]) if apart_in else (rest[:1], rest[1:])
     outs, rest = (rest[:n], rest[n:]) if apart_out else (rest[:1], rest[1:])
     raw, kt, vv, ob, sg, in_sems, out_sems = rest
+    ob = ob if apart_out else outs[0]
     me = me_ref[0]
     shard = raw.shape[3]
     per = shard // BLK
@@ -312,12 +313,10 @@
             pltpu.make_async_copy(ob.at[me ^ k], outs[k], out_sems.at[k])
             for k in range(n)
         ]
-    else:
-        leaving = [pltpu.make_async_copy(ob, outs[0], out_sems.at[0])]
-    for copy in leaving:
-        copy.start()
-    for copy in leaving:
-        copy.wait()
+        for copy in leaving:
+            copy.start()
+        for copy in leaving:
+            copy.wait()
 
 
 def attend(n, me, rand, glob, pen, arrays, apart_out):
@@ -331,12 +330,12 @@
     if apart_out:
         out_shape = [jax.ShapeDtypeStruct((shard, PAIR), jnp.bfloat16)] * n
     else:
-        out_shape = [jax.ShapeDtypeStruct((n, shard, PAIR), jnp.bfloat16)]
+        out_shape = [pltpu.VMEM((n, shard, PAIR), jnp.bfloat16)]
     return pl.pallas_call(
         functools.partial(attend_kernel, n, nblocks, apart_in, apart_out),
         out_shape=out_shape,
         in_specs=[smem, smem, smem, vmem] + [hbm] * len(arrays),
-        out_specs=[hbm] * len(out_shape),
+        out_specs=[hbm] * n if apart_out else [vmem],
         scratch_shapes=[
             pltpu.VMEM((n, 3, PAIR, shard), jnp.bfloat16),
             pltpu.VMEM((length, PAIR), jnp.bfloat16),
@@ -346,7 +345,7 @@
             pltpu.SemaphoreType.DMA((n,)),
             pltpu.SemaphoreType.DMA((n,)),
         ],
-        compiler_params=pltpu.CompilerParams(vmem_limit_bytes=60 * 1024 * 1024),
+        compiler_params=pltpu.CompilerParams(vmem_limit_bytes=56 * 1024 * 1024),
         cost_estimate=pl.CostEstimate(
             flops=15_000_000_000, bytes_accessed=4_000_000, transcendentals=0
         ),
@@ -523,7 +522,7 @@
         slots += [(p, p, k) for k in range(n)]
     outs = attend(n, me, rand[last], glob, pen[last], messages, True)
     outs, weights = lax.optimization_barrier((list(outs), weights))
-    results = swap(outs, far + near)
+    results = swap(outs, far[::-1] + near)
     pieces += [results[k] for k in [0] + near]
     slots += [(last + i, last, k) for i, k in enumerate([0] + near)]
     late = [(i, last, k) for i, k in enumerate(far)]

time: 197 us -> 197 us (level)
  no operation moved by 1% of the time
where the time goes in v8:
time: 197 us; the launch traced here: 196 us
  waiting for transfers between devices  105 us (53%)
  Pallas kernels  47.5 us (24%)
  starting transfers between devices  36.8 us (19%)
  local copies, waits for them, and re-layouts  6.2 us (3%)
    ppermute x14, waiting for transfers between devices, swap(): lax.ppermute(arrays[k], 'seq', [(i, i ^ k) for i in range(n)])  105 us
    pallas_call x2, Pallas kernels, attend(): pl.pallas_call(functools.partial(attend_kernel, n, nblocks, apart_in, apa...  29.3 us
    ppermute x14, starting transfers between devices, swap(): lax.ppermute(arrays[k], 'seq', [(i, i ^ k) for i in range(n)])  21.1 us
    all_to_all x2, starting transfers between devices, exchange(): return lax.all_to_all(x, 'seq', split_axis=0, concat_axis=0, tiled=True)  13.7 us
    pallas_call x1, Pallas kernels, project_early(): pl.pallas_call(functools.partial(project_kernel, n, ndp, slots, ahead, Fa...  7.83 us
  transfers between devices with their start and end apart: 19, of which 10 were waited for; matrix products, arithmetic and copies ran while one was open for 2% of the time, Pallas kernels for 21%

profile of v8, /device:TPU:8, one launch (start us, length us, event | category | flops | bytes accessed | tf_op | source)
XLA Modules:
  0.0 196.5 jit_solution(3601063436770262743)
XLA Ops:
  0.0 3.8 %cut.1 = bf16[8,3,128,512]{3,2,1,0:T(8,128)(2,1)} custom-call(bf16[1,2048,512]{2,1,0:T(8,128)(2,1)} %q_ref.3, bf16[1,2048,512]{2,1,0:T(8,128)(2,1)} %k_ref.3, bf16[1,2048,512]{2,1,0:T(8,128)(2,1)} %v_ref.3), custom_call_target="tpu_custom_call" | custom-call | tf_op jit(solution)/shard_map/cut/pallas_call | solution.py:125
  3.8 6.3 %all-to-all-start = ((bf16[8,3,128,512]{3,2,1,0:T(8,128)(2,1)}), bf16[8,3,128,512]{3,2,1,0:T(8,128)(2,1)S(1)}, u32[]{:S(2)}, u32[]{:S(2)}) async-start(bf16[8,3,128,512]{3,2,1,0:T(8,128)(2,1)} %cut.1), calls=%async_computation | async-start | bytes 6291456 | tf_op jit(solution)/shard_map/all_to_all | solution.py:500
  10.7 3.8 %cut_apart.1 = (bf16[3,128,512]{2,1,0:T(8,128)(2,1)}, bf16[3,128,512]{2,1,0:T(8,128)(2,1)}, bf16[3,128,512]{2,1,0:T(8,128)(2,1)}, bf16[3,128,512]{2,1,0:T(8,128)...) custom-call(s32[2]{0:T(128)} %pad_add_fusion.3.me_ref, ...), custom_call_target="tpu_custom_call" | custom-call | tf_op jit(solution)/shard_map/cut_apart/pallas_call | solution.py:166
  16.1 27.7 %collective-permute-done.rest_2_ = bf16[3,128,512]{2,1,0:T(8,128)(2,1)S(1)} collective-permute-done((bf16[3,128,512]{2,1,0:T(8,128)(2,1)}, bf16[3,128,512]{2,1,0:T(8,128)(2,1)S(1)}, u32[]{:S(2)}, u32[]{:S(2)}) %collective-permute-start) | collective-permute-done | bytes 393248 | tf_op jit(solution)/shard_map/ppermute | solution.py:503
  46.8 2.3 %collective-permute-start.2 = (bf16[3,128,512]{2,1,0:T(8,128)(2,1)}, bf16[3,128,512]{2,1,0:T(8,128)(2,1)}, u32[]{:S(2)}, u32[]{:S(2)}) collective-permute-start(bf16[3,128,512]{2,1,0:T(8,128)(2,1)} %get-tuple-element.39), channel_id=1, source_target_pairs={{0,12},{4,8},{8,4},{12,0},{16,28},{20,24},{24,20},{28,16},{1,13},{... | collective-permute-start | bytes 1179656 | tf_op jit(solution)/shard_map/ppermute | solution.py:503
  49.1 2.1 %collective-permute-start.3 = (bf16[3,128,512]{2,1,0:T(8,128)(2,1)}, bf16[3,128,512]{2,1,0:T(8,128)(2,1)}, u32[]{:S(2)}, u32[]{:S(2)}) collective-permute-start(bf16[3,128,512]{2,1,0:T(8,128)(2,1)} %get-tuple-element.40), channel_id=1, source_target_pairs={{0,16},{4,20},{8,24},{12,28},{16,0},{20,4},{24,8},{28,12},{1,17},{... | collective-permute-start | bytes 1179656 | tf_op jit(solution)/shard_map/ppermute | solution.py:503
  51.2 2.2 %collective-permute-start.4 = (bf16[3,128,512]{2,1,0:T(8,128)(2,1)}, bf16[3,128,512]{2,1,0:T(8,128)(2,1)}, u32[]{:S(2)}, u32[]{:S(2)}) collective-permute-start(bf16[3,128,512]{2,1,0:T(8,128)(2,1)} %get-tuple-element.41), channel_id=1, source_target_pairs={{0,20},{4,16},{8,28},{12,24},{16,4},{20,0},{24,12},{28,8},{1,21},{... | collective-permute-start | bytes 1179656 | tf_op jit(solution)/shard_map/ppermute | solution.py:503
  56.6 15.4 %collective-permute-done.1.rest_3_ = bf16[3,128,512]{2,1,0:T(8,128)(2,1)} collective-permute-done((bf16[3,128,512]{2,1,0:T(8,128)(2,1)}, bf16[3,128,512]{2,1,0:T(8,128)(2,1)}, u32[]{:S(2)}, u32[]{:S(2)}) %collective-permute-start.1) | collective-permute-done | bytes 393248 | tf_op jit(solution)/shard_map/ppermute | solution.py:503
  72.0 1.9 collective-permute-start.5
  74.0 7.8 %collective-permute-done.2.rest_4_ = bf16[3,128,512]{2,1,0:T(8,128)(2,1)} collective-permute-done((bf16[3,128,512]{2,1,0:T(8,128)(2,1)}, bf16[3,128,512]{2,1,0:T(8,128)(2,1)}, u32[]{:S(2)}, u32[]{:S(2)}) %collective-permute-start.2) | collective-permute-done | bytes 393248 | tf_op jit(solution)/shard_map/ppermute | solution.py:503
  83.3 37.3 %collective-permute-done.3.rest_5_ = bf16[3,128,512]{2,1,0:T(8,128)(2,1)} collective-permute-done((bf16[3,128,512]{2,1,0:T(8,128)(2,1)}, bf16[3,128,512]{2,1,0:T(8,128)(2,1)}, u32[]{:S(2)}, u32[]{:S(2)}) %collective-permute-start.3) | collective-permute-done | bytes 393248 | tf_op jit(solution)/shard_map/ppermute | solution.py:503
  122.7 14.6 %attend.3 = bf16[8,512,128]{2,1,0:T(8,128)(2,1)} custom-call(s32[2]{0:T(128)} %pad_add_fusion.3.me_ref, s32[384]{0:T(512)} %squeeze.22.rand_ref, s32[2]{0:T(128)} %bitcast.19, f32[64,8,2]{2,1,0:T(8,128)} %get-tuple-element.67.rest_0_, bf16[8,3,128,512]{3,2,1,0:T(8,128)(2,1)} %copy-done.2), custom_call_target="tpu_custom_call" | custom-call | flops 15000000512 | bytes 4000000 | tf_op jit(solution)/shard_map/attend/pallas_call | solution.py:334
  137.4 7.4 %all-to-all-start.1 = ((bf16[8,512,128]{2,1,0:T(8,128)(2,1)}), bf16[8,512,128]{2,1,0:T(8,128)(2,1)S(1)}, u32[]{:S(2)}, u32[]{:S(2)}) async-start(bf16[8,512,128]{2,1,0:T(8,128)(2,1)} %attend.3), calls=%async_computation.1 | async-start | bytes 2097152 | tf_op jit(solution)/shard_map/all_to_all | solution.py:500
  145.7 2.7 %collective-permute-done.6.rest_8_ = bf16[3,128,512]{2,1,0:T(8,128)(2,1)} collective-permute-done((bf16[3,128,512]{2,1,0:T(8,128)(2,1)}, bf16[3,128,512]{2,1,0:T(8,128)(2,1)}, u32[]{:S(2)}, u32[]{:S(2)}) %collective-permute-start.6) | collective-permute-done | bytes 393248 | tf_op jit(solution)/shard_map/ppermute | solution.py:503
  148.3 14.7 %attend.2 = (bf16[512,128]{1,0:T(8,128)(2,1)}, bf16[512,128]{1,0:T(8,128)(2,1)}, bf16[512,128]{1,0:T(8,128)(2,1)}, bf16[512,128]{1,0:T(8,128)(2,1)}, bf16[512,12...) custom-call(s32[2]{0:T(128)} %pad_add_fusion.3.me_ref, ...), custom_call_target="tpu_custom_call" | custom-call | flops 15000000512 | bytes 4000000 | tf_op jit(solution)/shard_map/attend/pallas_call | solution.py:334
  163.2 3.4 %collective-permute-start.16 = (bf16[512,128]{1,0:T(8,128)(2,1)}, bf16[512,128]{1,0:T(8,128)(2,1)S(1)}, u32[]{:S(2)}, u32[]{:S(2)}) collective-permute-start(bf16[512,128]{1,0:T(8,128)(2,1)} %get-tuple-element.60), channel_id=1, source_target_pairs={{0,12},{4,8},{8,4},{12,0},{16,28},{20,24},{24,20},{28,16},{1,13},{... | collective-permute-start | bytes 393224 | tf_op jit(solution)/shard_map/ppermute | solution.py:503
  166.6 2.6 %collective-permute-start.10 = (bf16[512,128]{1,0:T(8,128)(2,1)}, bf16[512,128]{1,0:T(8,128)(2,1)S(1)}, u32[]{:S(2)}, u32[]{:S(2)}) collective-permute-start(bf16[512,128]{1,0:T(8,128)(2,1)} %get-tuple-element.53), channel_id=1, source_target_pairs={{0,16},{4,20},{8,24},{12,28},{16,0},{20,4},{24,8},{28,12},{1,17},{... | collective-permute-start | bytes 393224 | tf_op jit(solution)/shard_map/ppermute | solution.py:503
  170.1 2.6 %collective-permute-done.14.rest_2_ = bf16[512,128]{1,0:T(8,128)(2,1)S(1)} collective-permute-done((bf16[512,128]{1,0:T(8,128)(2,1)}, bf16[512,128]{1,0:T(8,128)(2,1)S(1)}, u32[]{:S(2)}, u32[]{:S(2)}) %collective-permute-start.14) | collective-permute-done | bytes 131104 | tf_op jit(solution)/shard_map/ppermute | solution.py:503
  173.6 2.2 %collective-permute-done.15.rest_3_ = bf16[512,128]{1,0:T(8,128)(2,1)S(1)} collective-permute-done((bf16[512,128]{1,0:T(8,128)(2,1)}, bf16[512,128]{1,0:T(8,128)(2,1)S(1)}, u32[]{:S(2)}, u32[]{:S(2)}) %collective-permute-start.15) | collective-permute-done | bytes 131104 | tf_op jit(solution)/shard_map/ppermute | solution.py:503
  175.8 2.7 %collective-permute-done.16.rest_4_ = bf16[512,128]{1,0:T(8,128)(2,1)S(1)} collective-permute-done((bf16[512,128]{1,0:T(8,128)(2,1)}, bf16[512,128]{1,0:T(8,128)(2,1)S(1)}, u32[]{:S(2)}, u32[]{:S(2)}) %collective-permute-start.16) | collective-permute-done | bytes 131104 | tf_op jit(solution)/shard_map/ppermute | solution.py:503
  179.4 7.8 %project_early.1 = (f32[1,512,2048]{2,1,0:T(8,128)S(1)}, bf16[512,2048]{1,0:T(8,128)(2,1)S(1)}) custom-call(s32[2]{0:T(128)S(1)} %copy-done, bf16[8,512,128]{2,1,0:T(8,128)(2,1)S(1)} %all-to-all-done.1.rest_0_, bf16[512,128]{1,0:T(8,128)(2,1)S(1)} %copy-done.1, bf16[512,128]{1,0:T(8,128)(2,1)S(1)} %collective-permute-done.14.rest_2_, ...), custom_call_target="tpu_custom_call" | custom-call | flops 3221225472 | bytes 10000000 | tf_op jit(solution)/shard_map/project_early/pallas_call | solution.py:432
  187.3 3.7 %collective-permute-done.12.rest_2_ = bf16[512,128]{1,0:T(8,128)(2,1)S(1)} collective-permute-done((bf16[512,128]{1,0:T(8,128)(2,1)}, bf16[512,128]{1,0:T(8,128)(2,1)S(1)}, u32[]{:S(2)}, u32[]{:S(2)}) %collective-permute-start.12) | collective-permute-done | bytes 131104 | tf_op jit(solution)/shard_map/ppermute | solution.py:503
  190.9 2.5 %collective-permute-done.13.rest_3_ = bf16[512,128]{1,0:T(8,128)(2,1)S(1)} collective-permute-done((bf16[512,128]{1,0:T(8,128)(2,1)}, bf16[512,128]{1,0:T(8,128)(2,1)S(1)}, u32[]{:S(2)}, u32[]{:S(2)}) %collective-permute-start.13) | collective-permute-done | bytes 131104 | tf_op jit(solution)/shard_map/ppermute | solution.py:503
  193.5 2.8 %project_late.1 = bf16[1,512,2048]{2,1,0:T(8,128)(2,1)} custom-call(s32[2]{0:T(128)S(1)} %copy-done, bf16[512,128]{1,0:T(8,128)(2,1)S(1)} %collective-permute-done.10.rest_0_, bf16[512,128]{1,0:T(8,128)(2,1)S(1)} %collective-permute-done.11.rest_1_, bf16[512,128]{1,0:T(8,128)(2,1)S(1)} %collective-permute-done.12.rest_2_, ...), custom_call_target="tpu_custom_call" | custom-call | flops 1073741824 | bytes 10000000 | tf_op jit(solution)/shard_map/project_late/pallas_call | solution.py:462
  (58 shorter events, 15.9 us)
Async XLA Ops:
  3.8 117.3 %all-to-all-start = ((bf16[8,3,128,512]{3,2,1,0:T(8,128)(2,1)}), bf16[8,3,128,512]{3,2,1,0:T(8,128)(2,1)S(1)}, u32[]{:S(2)}, u32[]{:S(2)}) async-start(bf16[8,3,128,512]{3,2,1,0:T(8,128)(2,1)} %cut.1), calls=%async_computation | async-start | bytes 6291456 | tf_op jit(solution)/shard_map/all_to_all | solution.py:500
  10.7 42.7 %copy-start.3 = (s32[1,4,64,3]{2,1,3,0:T(4,128)S(1)}, s32[1,4,64,3]{2,1,3,0:T(4,128)}, u32[]{:S(2)}) copy-start(s32[1,4,64,3]{2,1,3,0:T(4,128)} %param.9) | copy-start | bytes 9220
  10.7 42.7 %copy-start.6 = (s32[1,2]{1,0:T(1,128)S(1)}, s32[1,2]{1,0:T(1,128)}, u32[]{:S(2)}) copy-start(s32[1,2]{1,0:T(1,128)} %param.10) | copy-start | bytes 28
  14.5 29.2 %collective-permute-start = (bf16[3,128,512]{2,1,0:T(8,128)(2,1)}, bf16[3,128,512]{2,1,0:T(8,128)(2,1)S(1)}, u32[]{:S(2)}, u32[]{:S(2)}) collective-permute-start(bf16[3,128,512]{2,1,0:T(8,128)(2,1)} %get-tuple-element.37), channel_id=1, source_target_pairs={{0,4},{4,0},{8,12},{12,8},{16,20},{20,16},{24,28},{28,24},{1,5},{5... | collective-permute-start | bytes 1179656 | tf_op jit(solution)/shard_map/ppermute | solution.py:503
  43.7 9.6 %copy-start.4 = (bf16[3,128,512]{2,1,0:T(8,128)(2,1)}, bf16[3,128,512]{2,1,0:T(8,128)(2,1)S(1)}, u32[]{:S(2)}) copy-start(bf16[3,128,512]{2,1,0:T(8,128)(2,1)S(1)} %collective-permute-done.rest_2_) | copy-start | bytes 1179652
  43.7 76.8 %collective-permute-start.8 = (bf16[512,2048]{1,0:T(8,128)(2,1)}, bf16[512,2048]{1,0:T(8,128)(2,1)}, u32[]{:S(2)}, u32[]{:S(2)}) collective-permute-start(bf16[512,2048]{1,0:T(8,128)(2,1)} %rest_5_), channel_id=1, source_target_pairs={{0,2},{1,3},{2,0},{3,1},{4,6},{5,7},{6,4},{7,5},{8,10},{9,11},{10,... | collective-permute-start | bytes 6291464 | tf_op jit(solution)/shard_map/ppermute | solution.py:486
  45.2 26.8 %collective-permute-start.1 = (bf16[3,128,512]{2,1,0:T(8,128)(2,1)}, bf16[3,128,512]{2,1,0:T(8,128)(2,1)}, u32[]{:S(2)}, u32[]{:S(2)}) collective-permute-start(bf16[3,128,512]{2,1,0:T(8,128)(2,1)} %get-tuple-element.38), channel_id=1, source_target_pairs={{0,8},{4,12},{8,0},{12,4},{16,24},{20,28},{24,16},{28,20},{1,9},{5... | collective-permute-start | bytes 1179656 | tf_op jit(solution)/shard_map/ppermute | solution.py:503
  46.8 35.0 %collective-permute-start.2 = (bf16[3,128,512]{2,1,0:T(8,128)(2,1)}, bf16[3,128,512]{2,1,0:T(8,128)(2,1)}, u32[]{:S(2)}, u32[]{:S(2)}) collective-permute-start(bf16[3,128,512]{2,1,0:T(8,128)(2,1)} %get-tuple-element.39), channel_id=1, source_target_pairs={{0,12},{4,8},{8,4},{12,0},{16,28},{20,24},{24,20},{28,16},{1,13},{... | collective-permute-start | bytes 1179656 | tf_op jit(solution)/shard_map/ppermute | solution.py:503
  49.1 71.5 %collective-permute-start.3 = (bf16[3,128,512]{2,1,0:T(8,128)(2,1)}, bf16[3,128,512]{2,1,0:T(8,128)(2,1)}, u32[]{:S(2)}, u32[]{:S(2)}) collective-permute-start(bf16[3,128,512]{2,1,0:T(8,128)(2,1)} %get-tuple-element.40), channel_id=1, source_target_pairs={{0,16},{4,20},{8,24},{12,28},{16,0},{20,4},{24,8},{28,12},{1,17},{... | collective-permute-start | bytes 1179656 | tf_op jit(solution)/shard_map/ppermute | solution.py:503
  51.2 94.5 %collective-permute-start.4 = (bf16[3,128,512]{2,1,0:T(8,128)(2,1)}, bf16[3,128,512]{2,1,0:T(8,128)(2,1)}, u32[]{:S(2)}, u32[]{:S(2)}) collective-permute-start(bf16[3,128,512]{2,1,0:T(8,128)(2,1)} %get-tuple-element.41), channel_id=1, source_target_pairs={{0,20},{4,16},{8,28},{12,24},{16,4},{20,0},{24,12},{28,8},{1,21},{... | collective-permute-start | bytes 1179656 | tf_op jit(solution)/shard_map/ppermute | solution.py:503
  72.0 73.6 %collective-permute-start.5 = (bf16[3,128,512]{2,1,0:T(8,128)(2,1)}, bf16[3,128,512]{2,1,0:T(8,128)(2,1)S(1)}, u32[]{:S(2)}, u32[]{:S(2)}) collective-permute-start(bf16[3,128,512]{2,1,0:T(8,128)(2,1)} %get-tuple-element.42), channel_id=1, source_target_pairs={{0,24},{4,28},{8,16},{12,20},{16,8},{20,12},{24,0},{28,4},{1,25},{... | collective-permute-start | bytes 1179656 | tf_op jit(solution)/shard_map/ppermute | solution.py:503
  81.7 66.6 %collective-permute-start.6 = (bf16[3,128,512]{2,1,0:T(8,128)(2,1)}, bf16[3,128,512]{2,1,0:T(8,128)(2,1)}, u32[]{:S(2)}, u32[]{:S(2)}) collective-permute-start(bf16[3,128,512]{2,1,0:T(8,128)(2,1)} %get-tuple-element.43), channel_id=1, source_target_pairs={{0,28},{4,24},{8,20},{12,16},{16,12},{20,8},{24,4},{28,0},{1,29},{... | collective-permute-start | bytes 1179656 | tf_op jit(solution)/shard_map/ppermute | solution.py:503
  120.6 42.5 %collective-permute-start.7 = (bf16[512,2048]{1,0:T(8,128)(2,1)}, bf16[512,2048]{1,0:T(8,128)(2,1)}, u32[]{:S(2)}, u32[]{:S(2)}) collective-permute-start(bf16[512,2048]{1,0:T(8,128)(2,1)} %rest_5_), channel_id=1, source_target_pairs={{0,1},{1,0},{2,3},{3,2},{4,5},{5,4},{6,7},{7,6},{8,9},{9,8},{10,11... | collective-permute-start | bytes 6291464 | tf_op jit(solution)/shard_map/ppermute | solution.py:486
  120.6 42.5 %collective-permute-start.9 = (bf16[512,2048]{1,0:T(8,128)(2,1)}, bf16[512,2048]{1,0:T(8,128)(2,1)}, u32[]{:S(2)}, u32[]{:S(2)}) collective-permute-start(bf16[512,2048]{1,0:T(8,128)(2,1)} %collective-permute-done.8.rest_7_), channel_id=1, source_target_pairs={{0,1},{1,0},{2,3},{3,2},{4,5},{5,4},{6,7},{7,6},{8,9},{9,8},{10,11... | collective-permute-start | bytes 6291464 | tf_op jit(solution)/shard_map/ppermute | solution.py:486
  137.4 41.1 %all-to-all-start.1 = ((bf16[8,512,128]{2,1,0:T(8,128)(2,1)}), bf16[8,512,128]{2,1,0:T(8,128)(2,1)S(1)}, u32[]{:S(2)}, u32[]{:S(2)}) async-start(bf16[8,512,128]{2,1,0:T(8,128)(2,1)} %attend.3), calls=%async_computation.1 | async-start | bytes 2097152 | tf_op jit(solution)/shard_map/all_to_all | solution.py:500
  145.7 2.7 %copy-start.5 = (bf16[3,128,512]{2,1,0:T(8,128)(2,1)}, bf16[3,128,512]{2,1,0:T(8,128)(2,1)S(1)}, u32[]{:S(2)}) copy-start(bf16[3,128,512]{2,1,0:T(8,128)(2,1)S(1)} %collective-permute-done.5.rest_7_) | copy-start | bytes 1179652
  148.3 30.2 %copy-start = (s32[2]{0:T(128)S(1)}, s32[2]{0:T(128)}, u32[]{:S(2)}) copy-start(s32[2]{0:T(128)} %pad_add_fusion.3.me_ref) | copy-start | bytes 28
  163.1 9.6 %collective-permute-start.14 = (bf16[512,128]{1,0:T(8,128)(2,1)}, bf16[512,128]{1,0:T(8,128)(2,1)S(1)}, u32[]{:S(2)}, u32[]{:S(2)}) collective-permute-start(bf16[512,128]{1,0:T(8,128)(2,1)} %get-tuple-element.58), channel_id=1, source_target_pairs={{0,4},{4,0},{8,12},{12,8},{16,20},{20,16},{24,28},{28,24},{1,5},{5... | collective-permute-start | bytes 393224 | tf_op jit(solution)/shard_map/ppermute | solution.py:503
  163.2 12.6 %collective-permute-start.15 = (bf16[512,128]{1,0:T(8,128)(2,1)}, bf16[512,128]{1,0:T(8,128)(2,1)S(1)}, u32[]{:S(2)}, u32[]{:S(2)}) collective-permute-start(bf16[512,128]{1,0:T(8,128)(2,1)} %get-tuple-element.59), channel_id=1, source_target_pairs={{0,8},{4,12},{8,0},{12,4},{16,24},{20,28},{24,16},{28,20},{1,9},{5... | collective-permute-start | bytes 393224 | tf_op jit(solution)/shard_map/ppermute | solution.py:503
  163.2 15.3 %collective-permute-start.16 = (bf16[512,128]{1,0:T(8,128)(2,1)}, bf16[512,128]{1,0:T(8,128)(2,1)S(1)}, u32[]{:S(2)}, u32[]{:S(2)}) collective-permute-start(bf16[512,128]{1,0:T(8,128)(2,1)} %get-tuple-element.60), channel_id=1, source_target_pairs={{0,12},{4,8},{8,4},{12,0},{16,28},{20,24},{24,20},{28,16},{1,13},{... | collective-permute-start | bytes 393224 | tf_op jit(solution)/shard_map/ppermute | solution.py:503
  166.6 20.6 %collective-permute-start.10 = (bf16[512,128]{1,0:T(8,128)(2,1)}, bf16[512,128]{1,0:T(8,128)(2,1)S(1)}, u32[]{:S(2)}, u32[]{:S(2)}) collective-permute-start(bf16[512,128]{1,0:T(8,128)(2,1)} %get-tuple-element.53), channel_id=1, source_target_pairs={{0,16},{4,20},{8,24},{12,28},{16,0},{20,4},{24,8},{28,12},{1,17},{... | collective-permute-start | bytes 393224 | tf_op jit(solution)/shard_map/ppermute | solution.py:503
  169.2 18.1 %collective-permute-start.11 = (bf16[512,128]{1,0:T(8,128)(2,1)}, bf16[512,128]{1,0:T(8,128)(2,1)S(1)}, u32[]{:S(2)}, u32[]{:S(2)}) collective-permute-start(bf16[512,128]{1,0:T(8,128)(2,1)} %get-tuple-element.54), channel_id=1, source_target_pairs={{0,20},{4,16},{8,28},{12,24},{16,4},{20,0},{24,12},{28,8},{1,21},{... | collective-permute-start | bytes 393224 | tf_op jit(solution)/shard_map/ppermute | solution.py:503
  172.7 18.2 %collective-permute-start.12 = (bf16[512,128]{1,0:T(8,128)(2,1)}, bf16[512,128]{1,0:T(8,128)(2,1)S(1)}, u32[]{:S(2)}, u32[]{:S(2)}) collective-permute-start(bf16[512,128]{1,0:T(8,128)(2,1)} %get-tuple-element.55), channel_id=1, source_target_pairs={{0,24},{4,28},{8,16},{12,20},{16,8},{20,12},{24,0},{28,4},{1,25},{... | collective-permute-start | bytes 393224 | tf_op jit(solution)/shard_map/ppermute | solution.py:503
  175.8 17.7 %collective-permute-start.13 = (bf16[512,128]{1,0:T(8,128)(2,1)}, bf16[512,128]{1,0:T(8,128)(2,1)S(1)}, u32[]{:S(2)}, u32[]{:S(2)}) collective-permute-start(bf16[512,128]{1,0:T(8,128)(2,1)} %get-tuple-element.56), channel_id=1, source_target_pairs={{0,28},{4,24},{8,20},{12,16},{16,12},{20,8},{24,4},{28,0},{1,29},{... | collective-permute-start | bytes 393224 | tf_op jit(solution)/shard_map/ppermute | solution.py:503
  (2 other events, 2.5 us)

commit v9 on v7

--- a/solution.py
+++ b/solution.py
@@ -358,7 +358,7 @@
     arrays = sorted({i for i, _, _ in slots})
     pieces, rest = rest[: len(arrays)], rest[len(arrays) :]
     if before:
-        before_ref, w, o_ref, a, a_sems, done, out_sems = rest
+        before_ref, w, o_ref, done, out_sems = rest
     else:
         weights, rest = rest[:ndp], rest[ndp:]
         o_ref, ahead_ref, a, w, a_sems, w_sems, ahead_sems = rest
@@ -377,9 +377,9 @@
         columns = pl.ds(t * tile, tile)
         return pltpu.make_async_copy(done.at[:, columns], o_ref.at[0, :, columns], out_sems.at[t])
 
-    for slot in range(len(slots)):
-        piece_copy(slot).start()
     if not before:
+        for slot in range(len(slots)):
+            piece_copy(slot).start()
         held = n // ndp
         feats = weights[0].shape[0] // held
 
@@ -404,11 +404,14 @@
 
         for slot in range(len(slots)):
             weight_copy(slots, slot, 0).wait()
-    for slot in range(len(slots)):
-        piece_copy(slot).wait()
+        for slot in range(len(slots)):
+            piece_copy(slot).wait()
+        rows = a[...]
+    else:
+        rows = jnp.concatenate([piece[...] for piece in pieces], axis=1)
     for t in range(4):
         columns = slice(t * tile, (t + 1) * tile)
-        total = jnp.dot(a[...], w[:, columns], preferred_element_type=jnp.float32)
+        total = jnp.dot(rows, w[:, columns], preferred_element_type=jnp.float32)
         if before:
             total = total + before_ref[0, :, columns]
         if before:
@@ -459,15 +462,15 @@
     depth = len(slots) * PAIR
     hbm = pl.BlockSpec(memory_space=pl.ANY)
     vmem = pl.BlockSpec(memory_space=pltpu.VMEM)
-    before, rows = (pltpu.with_memory_space_constraint(x, pltpu.VMEM) for x in (before, rows))
+    before, rows, *pieces = (
+        pltpu.with_memory_space_constraint(x, pltpu.VMEM) for x in (before, rows, *pieces)
+    )
     return pl.pallas_call(
         functools.partial(project_kernel, n, 0, slots, [], True),
         out_shape=jax.ShapeDtypeStruct((1, shard, width), jnp.bfloat16),
-        in_specs=[pl.BlockSpec(memory_space=pltpu.SMEM)] + [hbm] * len(pieces) + [vmem, vmem],
+        in_specs=[pl.BlockSpec(memory_space=pltpu.SMEM)] + [vmem] * len(pieces) + [vmem, vmem],
         out_specs=hbm,
         scratch_shapes=[
-            pltpu.VMEM((shard, depth), jnp.bfloat16),
-            pltpu.SemaphoreType.DMA((len(slots),)),
             pltpu.VMEM((shard, width), jnp.bfloat16),
             pltpu.SemaphoreType.DMA((4,)),
         ],

time: 197 us -> 197 us (level)
  no operation moved by 1% of the time
where the time goes in v9:
time: 197 us; the launch traced here: 196 us
  waiting for transfers between devices  105 us (53%)
  Pallas kernels  47.4 us (24%)
  starting transfers between devices  36.8 us (19%)
  local copies, waits for them, and re-layouts  6.2 us (3%)
    ppermute x14, waiting for transfers between devices, swap(): lax.ppermute(arrays[k], 'seq', [(i, i ^ k) for i in range(n)])  105 us
    pallas_call x2, Pallas kernels, attend(): pl.pallas_call(functools.partial(attend_kernel, n, nblocks, apart_in, apa...  29.3 us
    ppermute x14, starting transfers between devices, swap(): lax.ppermute(arrays[k], 'seq', [(i, i ^ k) for i in range(n)])  21.1 us
    all_to_all x2, starting transfers between devices, exchange(): return lax.all_to_all(x, 'seq', split_axis=0, concat_axis=0, tiled=True)  13.7 us
    pallas_call x1, Pallas kernels, project_early(): pl.pallas_call(functools.partial(project_kernel, n, ndp, slots, ahead, Fa...  7.83 us
  transfers between devices with their start and end apart: 19, of which 10 were waited for; matrix products, arithmetic and copies ran while one was open for 2% of the time, Pallas kernels for 21%

profile of v9, /device:TPU:8, one launch (start us, length us, event | category | flops | bytes accessed | tf_op | source)
XLA Modules:
  0.0 196.3 jit_solution(2755867786145370452)
XLA Ops:
  0.0 3.8 %cut.1 = bf16[8,3,128,512]{3,2,1,0:T(8,128)(2,1)} custom-call(bf16[1,2048,512]{2,1,0:T(8,128)(2,1)} %q_ref.3, bf16[1,2048,512]{2,1,0:T(8,128)(2,1)} %k_ref.3, bf16[1,2048,512]{2,1,0:T(8,128)(2,1)} %v_ref.3), custom_call_target="tpu_custom_call" | custom-call | tf_op jit(solution)/shard_map/cut/pallas_call | solution.py:125
  3.8 6.3 %all-to-all-start = ((bf16[8,3,128,512]{3,2,1,0:T(8,128)(2,1)}), bf16[8,3,128,512]{3,2,1,0:T(8,128)(2,1)S(1)}, u32[]{:S(2)}, u32[]{:S(2)}) async-start(bf16[8,3,128,512]{3,2,1,0:T(8,128)(2,1)} %cut.1), calls=%async_computation | async-start | bytes 6291456 | tf_op jit(solution)/shard_map/all_to_all | solution.py:504
  10.7 3.8 %cut_apart.1 = (bf16[3,128,512]{2,1,0:T(8,128)(2,1)}, bf16[3,128,512]{2,1,0:T(8,128)(2,1)}, bf16[3,128,512]{2,1,0:T(8,128)(2,1)}, bf16[3,128,512]{2,1,0:T(8,128)...) custom-call(s32[2]{0:T(128)} %pad_add_fusion.3.me_ref, ...), custom_call_target="tpu_custom_call" | custom-call | tf_op jit(solution)/shard_map/cut_apart/pallas_call | solution.py:166
  16.1 27.7 %collective-permute-done.rest_2_ = bf16[3,128,512]{2,1,0:T(8,128)(2,1)S(1)} collective-permute-done((bf16[3,128,512]{2,1,0:T(8,128)(2,1)}, bf16[3,128,512]{2,1,0:T(8,128)(2,1)S(1)}, u32[]{:S(2)}, u32[]{:S(2)}) %collective-permute-start) | collective-permute-done | bytes 393248 | tf_op jit(solution)/shard_map/ppermute | solution.py:507
  46.8 2.3 %collective-permute-start.2 = (bf16[3,128,512]{2,1,0:T(8,128)(2,1)}, bf16[3,128,512]{2,1,0:T(8,128)(2,1)}, u32[]{:S(2)}, u32[]{:S(2)}) collective-permute-start(bf16[3,128,512]{2,1,0:T(8,128)(2,1)} %get-tuple-element.39), channel_id=1, source_target_pairs={{0,12},{4,8},{8,4},{12,0},{16,28},{20,24},{24,20},{28,16},{1,13},{... | collective-permute-start | bytes 1179656 | tf_op jit(solution)/shard_map/ppermute | solution.py:507
  49.1 2.1 %collective-permute-start.3 = (bf16[3,128,512]{2,1,0:T(8,128)(2,1)}, bf16[3,128,512]{2,1,0:T(8,128)(2,1)}, u32[]{:S(2)}, u32[]{:S(2)}) collective-permute-start(bf16[3,128,512]{2,1,0:T(8,128)(2,1)} %get-tuple-element.40), channel_id=1, source_target_pairs={{0,16},{4,20},{8,24},{12,28},{16,0},{20,4},{24,8},{28,12},{1,17},{... | collective-permute-start | bytes 1179656 | tf_op jit(solution)/shard_map/ppermute | solution.py:507
  51.2 2.2 %collective-permute-start.4 = (bf16[3,128,512]{2,1,0:T(8,128)(2,1)}, bf16[3,128,512]{2,1,0:T(8,128)(2,1)}, u32[]{:S(2)}, u32[]{:S(2)}) collective-permute-start(bf16[3,128,512]{2,1,0:T(8,128)(2,1)} %get-tuple-element.41), channel_id=1, source_target_pairs={{0,20},{4,16},{8,28},{12,24},{16,4},{20,0},{24,12},{28,8},{1,21},{... | collective-permute-start | bytes 1179656 | tf_op jit(solution)/shard_map/ppermute | solution.py:507
  56.6 15.4 %collective-permute-done.1.rest_3_ = bf16[3,128,512]{2,1,0:T(8,128)(2,1)} collective-permute-done((bf16[3,128,512]{2,1,0:T(8,128)(2,1)}, bf16[3,128,512]{2,1,0:T(8,128)(2,1)}, u32[]{:S(2)}, u32[]{:S(2)}) %collective-permute-start.1) | collective-permute-done | bytes 393248 | tf_op jit(solution)/shard_map/ppermute | solution.py:507
  72.0 1.9 collective-permute-start.5
  74.0 7.8 %collective-permute-done.2.rest_4_ = bf16[3,128,512]{2,1,0:T(8,128)(2,1)} collective-permute-done((bf16[3,128,512]{2,1,0:T(8,128)(2,1)}, bf16[3,128,512]{2,1,0:T(8,128)(2,1)}, u32[]{:S(2)}, u32[]{:S(2)}) %collective-permute-start.2) | collective-permute-done | bytes 393248 | tf_op jit(solution)/shard_map/ppermute | solution.py:507
  83.3 37.3 %collective-permute-done.3.rest_5_ = bf16[3,128,512]{2,1,0:T(8,128)(2,1)} collective-permute-done((bf16[3,128,512]{2,1,0:T(8,128)(2,1)}, bf16[3,128,512]{2,1,0:T(8,128)(2,1)}, u32[]{:S(2)}, u32[]{:S(2)}) %collective-permute-start.3) | collective-permute-done | bytes 393248 | tf_op jit(solution)/shard_map/ppermute | solution.py:507
  122.7 14.6 %attend.3 = bf16[8,512,128]{2,1,0:T(8,128)(2,1)} custom-call(s32[2]{0:T(128)} %pad_add_fusion.3.me_ref, s32[384]{0:T(512)} %squeeze.22.rand_ref, s32[2]{0:T(128)} %bitcast.19, f32[64,8,2]{2,1,0:T(8,128)} %get-tuple-element.67.rest_0_, bf16[8,3,128,512]{3,2,1,0:T(8,128)(2,1)} %copy-done.2), custom_call_target="tpu_custom_call" | custom-call | flops 15000000512 | bytes 4000000 | tf_op jit(solution)/shard_map/attend/pallas_call | solution.py:335
  137.4 7.4 %all-to-all-start.1 = ((bf16[8,512,128]{2,1,0:T(8,128)(2,1)}), bf16[8,512,128]{2,1,0:T(8,128)(2,1)S(1)}, u32[]{:S(2)}, u32[]{:S(2)}) async-start(bf16[8,512,128]{2,1,0:T(8,128)(2,1)} %attend.3), calls=%async_computation.1 | async-start | bytes 2097152 | tf_op jit(solution)/shard_map/all_to_all | solution.py:504
  145.7 2.7 %collective-permute-done.6.rest_8_ = bf16[3,128,512]{2,1,0:T(8,128)(2,1)} collective-permute-done((bf16[3,128,512]{2,1,0:T(8,128)(2,1)}, bf16[3,128,512]{2,1,0:T(8,128)(2,1)}, u32[]{:S(2)}, u32[]{:S(2)}) %collective-permute-start.6) | collective-permute-done | bytes 393248 | tf_op jit(solution)/shard_map/ppermute | solution.py:507
  148.3 14.7 %attend.2 = (bf16[512,128]{1,0:T(8,128)(2,1)}, bf16[512,128]{1,0:T(8,128)(2,1)}, bf16[512,128]{1,0:T(8,128)(2,1)}, bf16[512,128]{1,0:T(8,128)(2,1)}, bf16[512,12...) custom-call(s32[2]{0:T(128)} %pad_add_fusion.3.me_ref, ...), custom_call_target="tpu_custom_call" | custom-call | flops 15000000512 | bytes 4000000 | tf_op jit(solution)/shard_map/attend/pallas_call | solution.py:335
  163.2 3.4 %collective-permute-start.16 = (bf16[512,128]{1,0:T(8,128)(2,1)}, bf16[512,128]{1,0:T(8,128)(2,1)S(1)}, u32[]{:S(2)}, u32[]{:S(2)}) collective-permute-start(bf16[512,128]{1,0:T(8,128)(2,1)} %get-tuple-element.60), channel_id=1, source_target_pairs={{0,12},{4,8},{8,4},{12,0},{16,28},{20,24},{24,20},{28,16},{1,13},{... | collective-permute-start | bytes 393224 | tf_op jit(solution)/shard_map/ppermute | solution.py:507
  166.6 2.6 %collective-permute-start.10 = (bf16[512,128]{1,0:T(8,128)(2,1)}, bf16[512,128]{1,0:T(8,128)(2,1)S(1)}, u32[]{:S(2)}, u32[]{:S(2)}) collective-permute-start(bf16[512,128]{1,0:T(8,128)(2,1)} %get-tuple-element.53), channel_id=1, source_target_pairs={{0,16},{4,20},{8,24},{12,28},{16,0},{20,4},{24,8},{28,12},{1,17},{... | collective-permute-start | bytes 393224 | tf_op jit(solution)/shard_map/ppermute | solution.py:507
  170.1 2.6 %collective-permute-done.14.rest_2_ = bf16[512,128]{1,0:T(8,128)(2,1)S(1)} collective-permute-done((bf16[512,128]{1,0:T(8,128)(2,1)}, bf16[512,128]{1,0:T(8,128)(2,1)S(1)}, u32[]{:S(2)}, u32[]{:S(2)}) %collective-permute-start.14) | collective-permute-done | bytes 131104 | tf_op jit(solution)/shard_map/ppermute | solution.py:507
  173.6 2.2 %collective-permute-done.15.rest_3_ = bf16[512,128]{1,0:T(8,128)(2,1)S(1)} collective-permute-done((bf16[512,128]{1,0:T(8,128)(2,1)}, bf16[512,128]{1,0:T(8,128)(2,1)S(1)}, u32[]{:S(2)}, u32[]{:S(2)}) %collective-permute-start.15) | collective-permute-done | bytes 131104 | tf_op jit(solution)/shard_map/ppermute | solution.py:507
  175.8 2.7 %collective-permute-done.16.rest_4_ = bf16[512,128]{1,0:T(8,128)(2,1)S(1)} collective-permute-done((bf16[512,128]{1,0:T(8,128)(2,1)}, bf16[512,128]{1,0:T(8,128)(2,1)S(1)}, u32[]{:S(2)}, u32[]{:S(2)}) %collective-permute-start.16) | collective-permute-done | bytes 131104 | tf_op jit(solution)/shard_map/ppermute | solution.py:507
  179.4 7.8 %project_early.1 = (f32[1,512,2048]{2,1,0:T(8,128)S(1)}, bf16[512,2048]{1,0:T(8,128)(2,1)S(1)}) custom-call(s32[2]{0:T(128)S(1)} %copy-done, bf16[8,512,128]{2,1,0:T(8,128)(2,1)S(1)} %all-to-all-done.1.rest_0_, bf16[512,128]{1,0:T(8,128)(2,1)S(1)} %copy-done.1, bf16[512,128]{1,0:T(8,128)(2,1)S(1)} %collective-permute-done.14.rest_2_, ...), custom_call_target="tpu_custom_call" | custom-call | flops 3221225472 | bytes 10000000 | tf_op jit(solution)/shard_map/project_early/pallas_call | solution.py:436
  187.3 3.7 %collective-permute-done.12.rest_2_ = bf16[512,128]{1,0:T(8,128)(2,1)S(1)} collective-permute-done((bf16[512,128]{1,0:T(8,128)(2,1)}, bf16[512,128]{1,0:T(8,128)(2,1)S(1)}, u32[]{:S(2)}, u32[]{:S(2)}) %collective-permute-start.12) | collective-permute-done | bytes 131104 | tf_op jit(solution)/shard_map/ppermute | solution.py:507
  190.9 2.5 %collective-permute-done.13.rest_3_ = bf16[512,128]{1,0:T(8,128)(2,1)S(1)} collective-permute-done((bf16[512,128]{1,0:T(8,128)(2,1)}, bf16[512,128]{1,0:T(8,128)(2,1)S(1)}, u32[]{:S(2)}, u32[]{:S(2)}) %collective-permute-start.13) | collective-permute-done | bytes 131104 | tf_op jit(solution)/shard_map/ppermute | solution.py:507
  193.5 2.7 %project_late.1 = bf16[1,512,2048]{2,1,0:T(8,128)(2,1)} custom-call(s32[2]{0:T(128)S(1)} %copy-done, bf16[512,128]{1,0:T(8,128)(2,1)S(1)} %collective-permute-done.10.rest_0_, bf16[512,128]{1,0:T(8,128)(2,1)S(1)} %collective-permute-done.11.rest_1_, bf16[512,128]{1,0:T(8,128)(2,1)S(1)} %collective-permute-done.12.rest_2_, ...), custom_call_target="tpu_custom_call" | custom-call | flops 1073741824 | bytes 10000000 | tf_op jit(solution)/shard_map/project_late/pallas_call | solution.py:468
  (58 shorter events, 15.9 us)
Async XLA Ops:
  3.8 117.3 %all-to-all-start = ((bf16[8,3,128,512]{3,2,1,0:T(8,128)(2,1)}), bf16[8,3,128,512]{3,2,1,0:T(8,128)(2,1)S(1)}, u32[]{:S(2)}, u32[]{:S(2)}) async-start(bf16[8,3,128,512]{3,2,1,0:T(8,128)(2,1)} %cut.1), calls=%async_computation | async-start | bytes 6291456 | tf_op jit(solution)/shard_map/all_to_all | solution.py:504
  10.7 42.7 %copy-start.3 = (s32[1,4,64,3]{2,1,3,0:T(4,128)S(1)}, s32[1,4,64,3]{2,1,3,0:T(4,128)}, u32[]{:S(2)}) copy-start(s32[1,4,64,3]{2,1,3,0:T(4,128)} %param.9) | copy-start | bytes 9220
  10.7 42.7 %copy-start.6 = (s32[1,2]{1,0:T(1,128)S(1)}, s32[1,2]{1,0:T(1,128)}, u32[]{:S(2)}) copy-start(s32[1,2]{1,0:T(1,128)} %param.10) | copy-start | bytes 28
  14.5 29.2 %collective-permute-start = (bf16[3,128,512]{2,1,0:T(8,128)(2,1)}, bf16[3,128,512]{2,1,0:T(8,128)(2,1)S(1)}, u32[]{:S(2)}, u32[]{:S(2)}) collective-permute-start(bf16[3,128,512]{2,1,0:T(8,128)(2,1)} %get-tuple-element.37), channel_id=1, source_target_pairs={{0,4},{4,0},{8,12},{12,8},{16,20},{20,16},{24,28},{28,24},{1,5},{5... | collective-permute-start | bytes 1179656 | tf_op jit(solution)/shard_map/ppermute | solution.py:507
  43.7 9.6 %copy-start.4 = (bf16[3,128,512]{2,1,0:T(8,128)(2,1)}, bf16[3,128,512]{2,1,0:T(8,128)(2,1)S(1)}, u32[]{:S(2)}) copy-start(bf16[3,128,512]{2,1,0:T(8,128)(2,1)S(1)} %collective-permute-done.rest_2_) | copy-start | bytes 1179652
  43.7 76.8 %collective-permute-start.8 = (bf16[512,2048]{1,0:T(8,128)(2,1)}, bf16[512,2048]{1,0:T(8,128)(2,1)}, u32[]{:S(2)}, u32[]{:S(2)}) collective-permute-start(bf16[512,2048]{1,0:T(8,128)(2,1)} %rest_5_), channel_id=1, source_target_pairs={{0,2},{1,3},{2,0},{3,1},{4,6},{5,7},{6,4},{7,5},{8,10},{9,11},{10,... | collective-permute-start | bytes 6291464 | tf_op jit(solution)/shard_map/ppermute | solution.py:490
  45.2 26.8 %collective-permute-start.1 = (bf16[3,128,512]{2,1,0:T(8,128)(2,1)}, bf16[3,128,512]{2,1,0:T(8,128)(2,1)}, u32[]{:S(2)}, u32[]{:S(2)}) collective-permute-start(bf16[3,128,512]{2,1,0:T(8,128)(2,1)} %get-tuple-element.38), channel_id=1, source_target_pairs={{0,8},{4,12},{8,0},{12,4},{16,24},{20,28},{24,16},{28,20},{1,9},{5... | collective-permute-start | bytes 1179656 | tf_op jit(solution)/shard_map/ppermute | solution.py:507
  46.8 35.0 %collective-permute-start.2 = (bf16[3,128,512]{2,1,0:T(8,128)(2,1)}, bf16[3,128,512]{2,1,0:T(8,128)(2,1)}, u32[]{:S(2)}, u32[]{:S(2)}) collective-permute-start(bf16[3,128,512]{2,1,0:T(8,128)(2,1)} %get-tuple-element.39), channel_id=1, source_target_pairs={{0,12},{4,8},{8,4},{12,0},{16,28},{20,24},{24,20},{28,16},{1,13},{... | collective-permute-start | bytes 1179656 | tf_op jit(solution)/shard_map/ppermute | solution.py:507
  49.1 71.5 %collective-permute-start.3 = (bf16[3,128,512]{2,1,0:T(8,128)(2,1)}, bf16[3,128,512]{2,1,0:T(8,128)(2,1)}, u32[]{:S(2)}, u32[]{:S(2)}) collective-permute-start(bf16[3,128,512]{2,1,0:T(8,128)(2,1)} %get-tuple-element.40), channel_id=1, source_target_pairs={{0,16},{4,20},{8,24},{12,28},{16,0},{20,4},{24,8},{28,12},{1,17},{... | collective-permute-start | bytes 1179656 | tf_op jit(solution)/shard_map/ppermute | solution.py:507
  51.2 94.5 %collective-permute-start.4 = (bf16[3,128,512]{2,1,0:T(8,128)(2,1)}, bf16[3,128,512]{2,1,0:T(8,128)(2,1)}, u32[]{:S(2)}, u32[]{:S(2)}) collective-permute-start(bf16[3,128,512]{2,1,0:T(8,128)(2,1)} %get-tuple-element.41), channel_id=1, source_target_pairs={{0,20},{4,16},{8,28},{12,24},{16,4},{20,0},{24,12},{28,8},{1,21},{... | collective-permute-start | bytes 1179656 | tf_op jit(solution)/shard_map/ppermute | solution.py:507
  72.0 73.6 %collective-permute-start.5 = (bf16[3,128,512]{2,1,0:T(8,128)(2,1)}, bf16[3,128,512]{2,1,0:T(8,128)(2,1)S(1)}, u32[]{:S(2)}, u32[]{:S(2)}) collective-permute-start(bf16[3,128,512]{2,1,0:T(8,128)(2,1)} %get-tuple-element.42), channel_id=1, source_target_pairs={{0,24},{4,28},{8,16},{12,20},{16,8},{20,12},{24,0},{28,4},{1,25},{... | collective-permute-start | bytes 1179656 | tf_op jit(solution)/shard_map/ppermute | solution.py:507
  81.7 66.6 %collective-permute-start.6 = (bf16[3,128,512]{2,1,0:T(8,128)(2,1)}, bf16[3,128,512]{2,1,0:T(8,128)(2,1)}, u32[]{:S(2)}, u32[]{:S(2)}) collective-permute-start(bf16[3,128,512]{2,1,0:T(8,128)(2,1)} %get-tuple-element.43), channel_id=1, source_target_pairs={{0,28},{4,24},{8,20},{12,16},{16,12},{20,8},{24,4},{28,0},{1,29},{... | collective-permute-start | bytes 1179656 | tf_op jit(solution)/shard_map/ppermute | solution.py:507
  120.6 42.5 %collective-permute-start.7 = (bf16[512,2048]{1,0:T(8,128)(2,1)}, bf16[512,2048]{1,0:T(8,128)(2,1)}, u32[]{:S(2)}, u32[]{:S(2)}) collective-permute-start(bf16[512,2048]{1,0:T(8,128)(2,1)} %rest_5_), channel_id=1, source_target_pairs={{0,1},{1,0},{2,3},{3,2},{4,5},{5,4},{6,7},{7,6},{8,9},{9,8},{10,11... | collective-permute-start | bytes 6291464 | tf_op jit(solution)/shard_map/ppermute | solution.py:490
  120.6 42.5 %collective-permute-start.9 = (bf16[512,2048]{1,0:T(8,128)(2,1)}, bf16[512,2048]{1,0:T(8,128)(2,1)}, u32[]{:S(2)}, u32[]{:S(2)}) collective-permute-start(bf16[512,2048]{1,0:T(8,128)(2,1)} %collective-permute-done.8.rest_7_), channel_id=1, source_target_pairs={{0,1},{1,0},{2,3},{3,2},{4,5},{5,4},{6,7},{7,6},{8,9},{9,8},{10,11... | collective-permute-start | bytes 6291464 | tf_op jit(solution)/shard_map/ppermute | solution.py:490
  137.4 41.1 %all-to-all-start.1 = ((bf16[8,512,128]{2,1,0:T(8,128)(2,1)}), bf16[8,512,128]{2,1,0:T(8,128)(2,1)S(1)}, u32[]{:S(2)}, u32[]{:S(2)}) async-start(bf16[8,512,128]{2,1,0:T(8,128)(2,1)} %attend.3), calls=%async_computation.1 | async-start | bytes 2097152 | tf_op jit(solution)/shard_map/all_to_all | solution.py:504
  145.7 2.7 %copy-start.5 = (bf16[3,128,512]{2,1,0:T(8,128)(2,1)}, bf16[3,128,512]{2,1,0:T(8,128)(2,1)S(1)}, u32[]{:S(2)}) copy-start(bf16[3,128,512]{2,1,0:T(8,128)(2,1)S(1)} %collective-permute-done.5.rest_7_) | copy-start | bytes 1179652
  148.3 30.2 %copy-start = (s32[2]{0:T(128)S(1)}, s32[2]{0:T(128)}, u32[]{:S(2)}) copy-start(s32[2]{0:T(128)} %pad_add_fusion.3.me_ref) | copy-start | bytes 28
  163.1 9.6 %collective-permute-start.14 = (bf16[512,128]{1,0:T(8,128)(2,1)}, bf16[512,128]{1,0:T(8,128)(2,1)S(1)}, u32[]{:S(2)}, u32[]{:S(2)}) collective-permute-start(bf16[512,128]{1,0:T(8,128)(2,1)} %get-tuple-element.58), channel_id=1, source_target_pairs={{0,4},{4,0},{8,12},{12,8},{16,20},{20,16},{24,28},{28,24},{1,5},{5... | collective-permute-start | bytes 393224 | tf_op jit(solution)/shard_map/ppermute | solution.py:507
  163.2 12.6 %collective-permute-start.15 = (bf16[512,128]{1,0:T(8,128)(2,1)}, bf16[512,128]{1,0:T(8,128)(2,1)S(1)}, u32[]{:S(2)}, u32[]{:S(2)}) collective-permute-start(bf16[512,128]{1,0:T(8,128)(2,1)} %get-tuple-element.59), channel_id=1, source_target_pairs={{0,8},{4,12},{8,0},{12,4},{16,24},{20,28},{24,16},{28,20},{1,9},{5... | collective-permute-start | bytes 393224 | tf_op jit(solution)/shard_map/ppermute | solution.py:507
  163.2 15.3 %collective-permute-start.16 = (bf16[512,128]{1,0:T(8,128)(2,1)}, bf16[512,128]{1,0:T(8,128)(2,1)S(1)}, u32[]{:S(2)}, u32[]{:S(2)}) collective-permute-start(bf16[512,128]{1,0:T(8,128)(2,1)} %get-tuple-element.60), channel_id=1, source_target_pairs={{0,12},{4,8},{8,4},{12,0},{16,28},{20,24},{24,20},{28,16},{1,13},{... | collective-permute-start | bytes 393224 | tf_op jit(solution)/shard_map/ppermute | solution.py:507
  166.6 20.6 %collective-permute-start.10 = (bf16[512,128]{1,0:T(8,128)(2,1)}, bf16[512,128]{1,0:T(8,128)(2,1)S(1)}, u32[]{:S(2)}, u32[]{:S(2)}) collective-permute-start(bf16[512,128]{1,0:T(8,128)(2,1)} %get-tuple-element.53), channel_id=1, source_target_pairs={{0,16},{4,20},{8,24},{12,28},{16,0},{20,4},{24,8},{28,12},{1,17},{... | collective-permute-start | bytes 393224 | tf_op jit(solution)/shard_map/ppermute | solution.py:507
  169.2 18.1 %collective-permute-start.11 = (bf16[512,128]{1,0:T(8,128)(2,1)}, bf16[512,128]{1,0:T(8,128)(2,1)S(1)}, u32[]{:S(2)}, u32[]{:S(2)}) collective-permute-start(bf16[512,128]{1,0:T(8,128)(2,1)} %get-tuple-element.54), channel_id=1, source_target_pairs={{0,20},{4,16},{8,28},{12,24},{16,4},{20,0},{24,12},{28,8},{1,21},{... | collective-permute-start | bytes 393224 | tf_op jit(solution)/shard_map/ppermute | solution.py:507
  172.7 18.2 %collective-permute-start.12 = (bf16[512,128]{1,0:T(8,128)(2,1)}, bf16[512,128]{1,0:T(8,128)(2,1)S(1)}, u32[]{:S(2)}, u32[]{:S(2)}) collective-permute-start(bf16[512,128]{1,0:T(8,128)(2,1)} %get-tuple-element.55), channel_id=1, source_target_pairs={{0,24},{4,28},{8,16},{12,20},{16,8},{20,12},{24,0},{28,4},{1,25},{... | collective-permute-start | bytes 393224 | tf_op jit(solution)/shard_map/ppermute | solution.py:507
  175.8 17.7 %collective-permute-start.13 = (bf16[512,128]{1,0:T(8,128)(2,1)}, bf16[512,128]{1,0:T(8,128)(2,1)S(1)}, u32[]{:S(2)}, u32[]{:S(2)}) collective-permute-start(bf16[512,128]{1,0:T(8,128)(2,1)} %get-tuple-element.56), channel_id=1, source_target_pairs={{0,28},{4,24},{8,20},{12,16},{16,12},{20,8},{24,4},{28,0},{1,29},{... | collective-permute-start | bytes 393224 | tf_op jit(solution)/shard_map/ppermute | solution.py:507
  (2 other events, 2.5 us)
